TPU v7x, 512 devices: a whole 4x4x16 slice. The times are simulated.
512 devices in a mesh: ctx: 32 (over y, x, core), exp: 16 (over z).
Axes of the slice: x: 4, y: 4, z: 16, core: 2. Of those that a mesh axis runs over, the one named last changes fastest.
Arguments:
- hidden: bfloat16 [128, 32, 7168], P('exp', None, 'ctx'), may hold values from -60 to 60
- routes: int32 [128, 32, 8], P('exp'), may hold values from 0 to 255, as said below
- gates: float32 [128, 32, 8], P('exp'), may hold values from 0.4 to 2
- moe_gain: float32 [7168], P('ctx'), may hold values from 0.25 to 1.75
- gate_weight: bfloat16 [16, 7168, 2048], P('exp', 'ctx'), may hold values from -0.125 to 0.125
- up_weight: bfloat16 [16, 7168, 2048], P('exp', 'ctx'), may hold values from -0.125 to 0.125
- down_weight: bfloat16 [16, 2048, 7168], P('exp', None, 'ctx'), may hold values from -0.125 to 0.125
- latent_weight: bfloat16 [7168, 512], P('ctx'), may hold values from -2 to 2
- latent_gain: float32 [512], replicated, may hold values from 0.25 to 1.75
- queries: bfloat16 [4096, 64, 512], P('ctx', 'exp'), may hold values from -280 to 280
- subtree_end: int32 [4096], replicated, may hold values from 512 to 4095, as said below
Outputs:
- next_hidden: bfloat16 [128, 32, 7168], P('exp', None, 'ctx')
- attn_out: bfloat16 [4096, 64, 512], P('ctx', 'exp')
Inputs may be any that keep to these rules, and one draw needn't show every extreme that they name: `routes`: each row names 8 different experts, at most one of them below 16. In the rows of one index of exp (aligned blocks of 256 rows in the order of the first two dimensions) no expert below 16 is named by more than 12 rows, and in every block some expert below 16 is named by exactly 12 rows. subtree_end[j] is the last position of the subtree of token j in a tree laid out in depth-first order, so subtree_end[j] >= j. The first 512 tokens form a chain from which every later token descends; the rest splits into runs of 512 consecutive tokens, each a subtree of its own.
All inputs are finite; a program needn't handle non-finite values.
Results may differ from a plain program's by a relative error of at most 0.033.
Values may be sent and summed in bfloat16 or wider, within the bound.
No kernel may reach another device: no remote copies, remote signals or barrier semaphores. Data moves between devices by JAX's collectives and lax.ppermute only.
A program may use at most 64 MiB of HBM per device.

v0:
```python
import jax
import jax.numpy as jnp
from jax import lax
from jax.sharding import PartitionSpec as P

D = 7168
EXPERTS_ALL = 256
TOP = 8


score_scale = 192 ** (-0.5)
norm_eps = 1e-06
neg_fill = -1e30


def expert_block(received, gate_weight, up_weight, down_weight):
    source_count, local_count, slot_count, slice_width = received.shape
    token_rows = jnp.transpose(received, (1, 0, 2, 3)).reshape(
        local_count, source_count * slot_count, slice_width
    )
    gate_part = jnp.einsum(
        "erd,edf->erf", token_rows, gate_weight, preferred_element_type=jnp.float32
    )
    up_part = jnp.einsum("erd,edf->erf", token_rows, up_weight, preferred_element_type=jnp.float32)
    gate_total, up_total = lax.psum((gate_part, up_part), "ctx")
    activated = (jax.nn.silu(gate_total) * up_total).astype(jnp.bfloat16)
    expert_out = jnp.einsum(
        "erf,efd->erd", activated, down_weight, preferred_element_type=jnp.float32
    ).astype(jnp.bfloat16)
    expert_out = jnp.transpose(
        expert_out.reshape(local_count, source_count, slot_count, slice_width), (1, 0, 2, 3)
    )
    return lax.all_to_all(expert_out, "exp", split_axis=0, concat_axis=0, tiled=True)


def body(
    hidden,
    routes,
    gates,
    moe_gain,
    gate_weight,
    up_weight,
    down_weight,
    latent_weight,
    latent_gain,
    queries,
    subtree_end,
):
    row_group, shard_count, slice_width = hidden.shape
    token_count = row_group * shard_count
    local_experts = gate_weight.shape[0]
    exp_count = lax.axis_size("exp")
    window_experts = local_experts * exp_count
    capacity = max(2, 3 * token_count * TOP // (2 * EXPERTS_ALL))
    hidden_float = hidden.astype(jnp.float32)
    square_part = jnp.sum(hidden_float * hidden_float, axis=2)
    square_total = lax.psum(square_part, "ctx")
    inv_rms = lax.rsqrt(square_total / D + norm_eps)
    normed = (hidden_float * inv_rms[:, :, None] * moe_gain[None, None, :]).astype(jnp.bfloat16)
    token_rows = normed.reshape(token_count, slice_width)
    route_ids = routes.reshape(token_count, TOP)
    route_gates = gates.reshape(token_count, TOP)
    expert_range = jnp.arange(window_experts, dtype=jnp.int32)
    matches = route_ids[:, :, None] == expert_range[None, None, :]
    picked = jnp.sum(matches.astype(jnp.int32), axis=1)
    gate_table = jnp.sum(jnp.where(matches, route_gates[:, :, None], 0.0), axis=1)
    slot_rank = jnp.cumsum(picked, axis=0) - picked
    slot_range = jnp.arange(capacity, dtype=jnp.int32)
    placed = (picked.T[:, None, :] == 1) & (slot_rank.T[:, None, :] == slot_range[None, :, None])
    dispatched = jnp.einsum(
        "est,td->esd", placed.astype(jnp.bfloat16), token_rows, preferred_element_type=jnp.float32
    ).astype(jnp.bfloat16)
    dispatched = dispatched.reshape(exp_count, local_experts, capacity, slice_width)
    returned = expert_block(
        lax.all_to_all(dispatched, "exp", split_axis=0, concat_axis=0, tiled=True),
        gate_weight,
        up_weight,
        down_weight,
    )
    returned = returned.reshape(window_experts, capacity, slice_width).astype(jnp.float32)
    combine_weights = placed.astype(jnp.float32) * gate_table.T[:, None, :]
    moe_sum = jnp.einsum("est,esd->td", combine_weights, returned, precision=lax.Precision.HIGHEST)
    next_hidden = (hidden_float + moe_sum.reshape(row_group, shard_count, slice_width)).astype(
        jnp.bfloat16
    )
    latent_raw = lax.psum_scatter(
        jnp.einsum("rcd,dl->crl", next_hidden, latent_weight, preferred_element_type=jnp.float32),
        "ctx",
        scatter_dimension=0,
        tiled=True,
    )[0]
    latent_rms = lax.rsqrt(jnp.mean(latent_raw * latent_raw, axis=1, keepdims=True) + norm_eps)
    latent_local = (latent_raw * latent_rms * latent_gain[None, :]).astype(jnp.bfloat16)
    shard_latent = lax.all_gather(latent_local, "exp", axis=0, tiled=True)
    tile_len = shard_latent.shape[0]
    head_count = queries.shape[1]
    shard_index = lax.axis_index("ctx")
    query_index = shard_index * tile_len + jnp.arange(tile_len, dtype=jnp.int32)
    key_block = lax.all_gather(shard_latent, "ctx", axis=0, tiled=True)
    run_max = jnp.full((tile_len, head_count), neg_fill, jnp.float32)
    key_count = key_block.shape[0]
    key_index = jnp.arange(key_count, dtype=jnp.int32)
    visible = (
        (key_index[None, :] <= query_index[:, None])
        & (query_index[:, None] <= subtree_end[None, :])
        & True
    )
    scores = (
        jnp.einsum("qhl,kl->qhk", queries, key_block, preferred_element_type=jnp.float32)
        * score_scale
    )
    scores = jnp.where(visible[:, None, :], scores, neg_fill)
    new_max = jnp.maximum(run_max, jnp.max(scores, axis=2))
    exp_scores = jnp.where(visible[:, None, :], jnp.exp(scores - new_max[:, :, None]), 0.0)
    run_sum = jnp.sum(exp_scores, axis=2)
    mixed_part = jnp.einsum(
        "qhk,kl->qhl",
        exp_scores.astype(jnp.bfloat16),
        key_block,
        preferred_element_type=jnp.float32,
    )
    run_acc = mixed_part
    final_state = (new_max, run_sum, run_acc)
    run_max, run_sum, run_acc = final_state
    attn_out = (run_acc / run_sum[:, :, None]).astype(jnp.bfloat16)
    return (next_hidden, attn_out)


def solution(mesh):
    return jax.shard_map(
        body,
        mesh=mesh,
        in_specs=(
            P("exp", None, "ctx"),
            P("exp", None, None),
            P("exp", None, None),
            P("ctx"),
            P("exp", "ctx", None),
            P("exp", "ctx", None),
            P("exp", None, "ctx"),
            P("ctx", None),
            P(),
            P("ctx", "exp", None),
            P(),
        ),
        out_specs=(P("exp", None, "ctx"), P("ctx", "exp", None)),
        check_vma=False,
    )
```

profile of v0, /device:TPU:1, one launch (start us, length us, event | category | flops | bytes accessed | tf_op | source)
XLA Modules:
  0.0 473.4 jit_solution(4325240717740560194)
XLA Ops:
  7.2 0.0 copy-start
  7.2 0.0 copy-start.2
  7.2 0.0 all-reduce.3.cloned.1.call-start
  7.2 0.9 copy.48
  8.1 0.1 eq.55
  8.3 1.0 fusion.27
  9.3 68.9 %psum.21 = f32[8,32]{1,0:T(8,128)S(1)} all-reduce(f32[8,32]{1,0:T(8,128)S(1)} %fusion.27), channel_id=1, replica_groups=mesh['ctx'=32,'exp'=16] {'ctx'}, use_global_device_ids=true, to_apply=%region_5.6 | all-reduce | flops 256 | bytes 2048 | tf_op jit(solution)/shard_map/psum | solution.py:57
  78.2 0.6 reduce-window.6
  78.8 0.2 slice_reduce_fusion
  79.0 0.1 bitcast_subtract_fusion
  79.1 1.0 fusion.29
  80.1 0.2 fusion.16
  80.3 21.6 %all_to_all.10 = bf16[16,1,12,224]{3,2,1,0:T(8,128)(2,1)S(1)} all-to-all(bf16[16,1,12,224]{3,2,1,0:T(8,128)(2,1)S(1)} %copy.53), channel_id=1, replica_groups=mesh['ctx'=32,'exp'=16] {'exp'}, dimensions={0} | all-to-all | bytes 172032 | tf_op jit(solution)/shard_map/all_to_all | solution.py:75
  102.0 0.0 copy-done
  102.0 0.0 copy-start.5
  102.0 0.0 copy-start.9
  102.0 1.5 convolution_bitcast_fusion
  103.5 0.0 copy-done.2
  103.5 1.5 convolution_bitcast_fusion.1
  105.1 0.0 all-reduce.3.cloned.1.call-update
  105.1 0.0 copy-done.5
  105.1 0.1 broadcast_in_dim.52
  105.2 134.5 %all-reduce.3.cloned.1.call-done = (f32[1,192,2048]{2,1,0:T(8,128)}, f32[1,192,2048]{2,1,0:T(8,128)}) async-done(((f32[1,192,2048]{2,1,0:T(8,128)}, f32[1,192,2048]{2,1,0:T(8,128)}), (f32[1,192,2048]{2,1,0:T(8,128)}, f32[1,192,2048]{2,1,0:T(8,128)})) %all-reduce.3.cloned.1.call-update) | async-done | bytes 3145744 | tf_op jit(solution)/shard_map/psum | solution.py:25
  239.7 0.0 copy-done.9
  239.7 0.0 copy-start.1
  239.7 0.0 copy-start.4
  239.7 2.5 convolution_convert_fusion
  242.2 0.0 copy-start.7
  242.2 0.0 copy-start.6
  242.2 0.0 copy-start.10
  242.2 0.7 transpose_reshape.3
  242.9 12.0 %all-to-all-start.1 = ((bf16[16,1,12,224]{3,2,1,0:T(8,128)(2,1)}), bf16[16,1,12,224]{3,2,1,0:T(8,128)(2,1)S(1)}, u32[]{:S(2)}, u32[]{:S(2)}) async-start(bf16[16,1,12,224]{3,2,1,0:T(8,128)(2,1)} %bitcast.11), calls=%async_computation.1 | async-start | bytes 262144 | tf_op jit(solution)/shard_map/all_to_all | solution.py:33
  254.9 0.0 reduce-scatter.2.cloned.1.call-start
  255.1 0.2 mul.69
  255.3 11.6 %all-to-all-done.1 = bf16[16,1,12,224]{3,2,1,0:T(8,128)(2,1)S(1)} async-done(((bf16[16,1,12,224]{3,2,1,0:T(8,128)(2,1)}), bf16[16,1,12,224]{3,2,1,0:T(8,128)(2,1)S(1)}, u32[]{:S(2)}, u32[]{:S(2)}) %all-to-all-start.1) | async-done | bytes 86048 | tf_op jit(solution)/shard_map/all_to_all | solution.py:33
  266.9 0.0 copy-done.1
  266.9 0.8 fusion.15
  267.7 0.0 copy-done.4
  267.7 0.0 copy-start.3
  267.7 0.2 convolution_bitcast_fusion.2
  268.0 1.1 copy.57
  269.1 0.0 reduce-scatter.2.cloned.1.call-update
  269.1 0.0 all-gather.2.cloned.1.call-start
  269.1 93.1 %reduce-scatter.2.cloned.1.call-done = f32[1,8,512]{2,1,0:T(8,128)} async-done(((f32[32,8,512]{2,1,0:T(8,128)}), f32[1,8,512]{2,1,0:T(8,128)}) %reduce-scatter.2.cloned.1.call-update) | async-done | bytes 16400 | tf_op jit(solution)/shard_map/reduce_scatter | solution.py:86
  362.3 0.8 fusion.39
  363.1 0.0 copy-done.7
  363.1 0.8 fusion.41
  363.9 26.5 %all_gather.6 = bf16[128,512]{1,0:T(8,128)(2,1)} all-gather(bf16[8,512]{1,0:T(8,128)(2,1)S(1)} %fusion.41), channel_id=1, replica_groups=mesh['ctx'=32,'exp'=16] {'exp'}, dimensions={0}, use_global_device_ids=true | all-gather | bytes 139264 | tf_op jit(solution)/shard_map/all_gather | solution.py:94
  390.4 0.0 all-gather.2.cloned.1.call-update
  390.4 0.0 copy-done.6
  390.5 1.9 fusion.13
  392.3 64.2 %all-gather.2.cloned.1.call-done = bf16[4096,512]{1,0:T(8,128)(2,1)} async-done(((bf16[128,512]{1,0:T(8,128)(2,1)}), bf16[4096,512]{1,0:T(8,128)(2,1)}) %all-gather.2.cloned.1.call-update) | async-done | bytes 4194320 | tf_op jit(solution)/shard_map/all_gather | solution.py:99
  456.6 0.0 copy-done.10
  456.6 4.4 fusion
  460.9 0.0 copy-done.3
  461.0 0.0 copy-start.8
  461.0 2.1 fusion.1
  463.1 0.1 copy-done.8
  463.2 2.5 divide_convert_fusion
  465.7 1.2 copy.60
  (15 shorter events, 0.3 us)
Async XLA Ops:
  7.2 94.8 %copy-start = (bf16[1,224,2048]{2,1,0:T(8,128)(2,1)S(1)}, bf16[1,224,2048]{2,1,0:T(8,128)(2,1)}, u32[]{:S(2)}) copy-start(bf16[1,224,2048]{2,1,0:T(8,128)(2,1)} %param.16) | copy-start | bytes 2752516
  7.2 96.4 %copy-start.2 = (bf16[1,224,2048]{2,1,0:T(8,128)(2,1)S(1)}, bf16[1,224,2048]{2,1,0:T(8,128)(2,1)}, u32[]{:S(2)}) copy-start(bf16[1,224,2048]{2,1,0:T(8,128)(2,1)} %param.15) | copy-start | bytes 2752516
  7.2 232.5 %all-reduce.3.cloned.1.call-start = ((), (), s32[]{:S(2)}) async-start(), calls=%async_computation.5 | async-start | bytes 6291456 | tf_op jit(solution)/shard_map/psum | solution.py:25
  102.0 3.1 copy-start.5
  102.0 137.7 %copy-start.9 = (bf16[1,2048,224]{1,2,0:T(8,128)(2,1)S(1)}, bf16[1,2048,224]{1,2,0:T(8,128)(2,1)}, u32[]{:S(2)}) copy-start(bf16[1,2048,224]{1,2,0:T(8,128)(2,1)} %param.17) | copy-start | bytes 2752516
  239.7 27.3 %copy-start.1 = (bf16[8,32,224]{2,1,0:T(8,128)(2,1)S(1)}, bf16[8,32,224]{2,1,0:T(8,128)(2,1)}, u32[]{:S(2)}) copy-start(bf16[8,32,224]{2,1,0:T(8,128)(2,1)} %param.11) | copy-start | bytes 344068
  239.7 28.0 %copy-start.4 = (bf16[224,512]{1,0:T(8,128)(2,1)S(1)}, bf16[224,512]{1,0:T(8,128)(2,1)}, u32[]{:S(2)}) copy-start(bf16[224,512]{1,0:T(8,128)(2,1)} %param.18) | copy-start | bytes 688132
  242.2 120.9 %copy-start.7 = (f32[512]{0:T(512)S(1)}, f32[512]{0:T(512)}, u32[]{:S(2)}) copy-start(f32[512]{0:T(512)} %param.19) | copy-start | bytes 6148
  242.2 148.2 %copy-start.6 = (s32[4096]{0:T(1024)S(1)}, s32[4096]{0:T(1024)}, u32[]{:S(2)}) copy-start(s32[4096]{0:T(1024)} %param.21) | copy-start | bytes 49156
  242.2 214.3 %copy-start.10 = (bf16[128,4,512]{2,1,0:T(4,128)(2,1)S(1)}, bf16[128,4,512]{2,1,0:T(4,128)(2,1)}, u32[]{:S(2)}) copy-start(bf16[128,4,512]{2,1,0:T(4,128)(2,1)} %param.20) | copy-start | bytes 1572868
  242.9 24.0 %all-to-all-start.1 = ((bf16[16,1,12,224]{3,2,1,0:T(8,128)(2,1)}), bf16[16,1,12,224]{3,2,1,0:T(8,128)(2,1)S(1)}, u32[]{:S(2)}, u32[]{:S(2)}) async-start(bf16[16,1,12,224]{3,2,1,0:T(8,128)(2,1)} %bitcast.11), calls=%async_computation.1 | async-start | bytes 262144 | tf_op jit(solution)/shard_map/all_to_all | solution.py:33
  254.9 107.3 %reduce-scatter.2.cloned.1.call-start = ((), (), s32[]{:S(2)}) async-start(), calls=%async_computation.3 | async-start | bytes 540672 | tf_op jit(solution)/shard_map/reduce_scatter | solution.py:86
  267.7 193.2 %copy-start.3 = (bf16[8,32,224]{2,1,0:T(8,128)(2,1)}, bf16[8,32,224]{2,1,0:T(8,128)(2,1)S(1)}, u32[]{:S(2)}) copy-start(bf16[8,32,224]{2,1,0:T(8,128)(2,1)S(1)} %fusion.15) | copy-start | bytes 344068
  269.1 187.5 %all-gather.2.cloned.1.call-start = ((), (), s32[]{:S(2)}) async-start(), calls=%async_computation.4 | async-start | bytes 4325376 | tf_op jit(solution)/shard_map/all_gather | solution.py:99
  461.0 2.2 copy-start.8
Sparse Core Ops, SparseCore 0:
  105.2 134.4 all-reduce.2
  269.2 93.0 reduce-scatter.1
  390.6 65.9 all-gather.1
where the time goes:
time: 474 us; the launch traced here: 473 us
  waiting for transfers between devices  304 us (64%)
  blocking collectives  117 us (25%)
  between operations  14 us (3%)
  matrix products  13.6 us (3%)
  starting transfers between devices  12.1 us (3%)
  other arithmetic  8.43 us (2%)
    psum x1, waiting for transfers between devices, expert_block(): gate_total, up_total = lax.psum((gate_part, up_part), 'ctx')  134 us
    reduce_scatter x1, waiting for transfers between devices, body(): lax.psum_scatter(jnp.einsum('rcd,dl->crl', next_hidden, latent_weight, pr...  93.1 us
    psum x1, blocking collectives, body(): square_total = lax.psum(square_part, 'ctx')  68.9 us
    all_gather x1, waiting for transfers between devices, body(): key_block = lax.all_gather(shard_latent, 'ctx', axis=0, tiled=True)  64.2 us
    all_gather x1, blocking collectives, body(): shard_latent = lax.all_gather(latent_local, 'exp', axis=0, tiled=True)  26.5 us
    all_to_all x1, blocking collectives, body(): lax.all_to_all(dispatched, 'exp', split_axis=0, concat_axis=0, tiled=True)  21.6 us
    all_to_all x1, starting transfers between devices, expert_block(): lax.all_to_all(expert_out, 'exp', split_axis=0, concat_axis=0, tiled=True)  12 us
    all_to_all x1, waiting for transfers between devices, expert_block(): lax.all_to_all(expert_out, 'exp', split_axis=0, concat_axis=0, tiled=True)  11.6 us
  transfers between devices with their start and end apart: 4, of which 4 were waited for; matrix products, arithmetic and copies ran while one was open for 0% of the time, Pallas kernels for 0%

commit v1 on v0

v1 whole, which is shorter than its diff:
```python
import jax
import jax.numpy as jnp
from jax import lax
from jax.sharding import PartitionSpec as P

D = 7168
TOP = 8
CAP = 12
GROUPS = 8
BLOCK = 4


score_scale = 192 ** (-0.5)
norm_eps = 1e-06
neg_fill = -1e30


def exchange(chunks, axis):
    return lax.all_to_all(chunks, axis, split_axis=0, concat_axis=0, tiled=True)


def split_two(value):
    high = value.astype(jnp.bfloat16)
    low = (value - high.astype(jnp.float32)).astype(jnp.bfloat16)
    return high, low


def body(
    hidden,
    routes,
    gates,
    moe_gain,
    gate_weight,
    up_weight,
    down_weight,
    latent_weight,
    latent_gain,
    queries,
    subtree_end,
):
    bf16, f32 = jnp.bfloat16, jnp.float32
    row_group, shard_count, width = hidden.shape
    tokens = row_group * shard_count
    exp_count = lax.axis_size("exp")
    ctx_count = lax.axis_size("ctx")
    chips = ctx_count // 2
    slots = exp_count * CAP
    half = slots // 2
    hidden_width = gate_weight.shape[2]
    lanes = hidden_width // chips
    latent_width = latent_weight.shape[1]

    rows = hidden.reshape(tokens, width)
    route_ids = routes.reshape(tokens, TOP)
    route_gates = gates.reshape(tokens, TOP)
    expert_range = jnp.arange(exp_count, dtype=jnp.int32)
    matches = route_ids[:, :, None] == expert_range[None, None, :]
    picked = jnp.sum(matches.astype(f32), axis=1)
    gate_table = jnp.sum(jnp.where(matches, route_gates[:, :, None], 0.0), axis=1)
    earlier = (jnp.arange(tokens)[:, None] < jnp.arange(tokens)[None, :]).astype(bf16)
    rank = jnp.einsum("te,tu->eu", picked.astype(bf16), earlier, preferred_element_type=f32)
    code = jnp.where(picked.T > 0, rank, -1.0)
    placed = code[:, None, :] == jnp.arange(CAP, dtype=f32)[None, :, None]
    placed = placed.reshape(slots, tokens)
    dispatched = jnp.dot(placed.astype(bf16), rows, preferred_element_type=f32).astype(bf16)
    dispatched = jnp.pad(dispatched.reshape(exp_count, CAP, width), ((0, 0), (0, 0), (0, 256 - width)))
    received = exchange(dispatched.reshape(exp_count, 2 * CAP, 128), "exp")
    received = received.reshape(exp_count, CAP, 256)[:, :, :width].reshape(slots, width)

    received_float = received.astype(f32)
    square_part = jnp.sum(received_float * received_float, axis=1)
    scaled = (received_float * moe_gain[None, :]).astype(bf16)
    gate_part = jnp.dot(scaled, gate_weight[0], preferred_element_type=f32).astype(bf16)
    up_part = jnp.dot(scaled, up_weight[0], preferred_element_type=f32).astype(bf16)

    def by_owner(part):
        return part.reshape(2, half, chips, lanes).transpose(2, 0, 1, 3)

    high, low = split_two(square_part.reshape(2, half))
    square_rows = jnp.pad(jnp.stack([high, low], axis=1), ((0, 0), (0, 6), (0, lanes - half)))
    square_rows = jnp.broadcast_to(square_rows[None], (chips,) + square_rows.shape)
    partial = jnp.concatenate([by_owner(gate_part), by_owner(up_part), square_rows], axis=2)
    partial = exchange(partial.reshape(ctx_count, 2 * half + 8, lanes), "ctx")
    total = jnp.sum(partial.astype(f32), axis=0)
    square_total = total[2 * half, :half] + total[2 * half + 1, :half]
    inv_rms = lax.rsqrt(square_total / D + norm_eps)[:, None]
    activated = (jax.nn.silu(total[:half] * inv_rms) * (total[half : 2 * half] * inv_rms)).astype(bf16)
    spread = exchange(jnp.broadcast_to(activated[None], (ctx_count, half, lanes)), "ctx")
    spread = spread.reshape(chips, 2, half, lanes).transpose(1, 2, 0, 3).reshape(slots, hidden_width)
    expert_out = jnp.dot(spread, down_weight[0], preferred_element_type=f32).astype(bf16)

    expert_out = jnp.pad(expert_out.reshape(exp_count, CAP, width), ((0, 0), (0, 0), (0, 256 - width)))
    returned = exchange(expert_out.reshape(exp_count, 2 * CAP, 128), "exp")
    returned = returned.reshape(exp_count, CAP, 256)[:, :, :width].reshape(slots, width)
    gate_high, gate_low = split_two(gate_table.T)

    def weighted(table):
        spread_table = jnp.broadcast_to(table[:, None, :], (exp_count, CAP, tokens)).reshape(slots, tokens)
        return jnp.where(placed, spread_table, jnp.zeros_like(spread_table))

    moe = jnp.einsum("qt,qd->td", weighted(gate_high), returned, preferred_element_type=f32)
    moe += jnp.einsum("qt,qd->td", weighted(gate_low), returned, preferred_element_type=f32)
    next_rows = (rows.astype(f32) + moe).astype(bf16)

    latent_part = jnp.dot(next_rows, latent_weight, preferred_element_type=f32).astype(bf16)
    latent_part = latent_part.reshape(row_group, GROUPS, BLOCK, latent_width).transpose(2, 0, 1, 3)
    latent_part = exchange(latent_part.reshape(ctx_count, GROUPS, latent_width), "ctx")
    latent_raw = jnp.sum(latent_part.astype(f32), axis=0)
    latent_rms = lax.rsqrt(jnp.mean(latent_raw * latent_raw, axis=1, keepdims=True) + norm_eps)
    latent = (latent_raw * latent_rms * latent_gain[None, :]).astype(bf16)
    plane = exchange(jnp.broadcast_to(latent[None], (exp_count,) + latent.shape), "exp")
    plane = plane.transpose(1, 0, 2)
    own = jnp.repeat(plane, BLOCK, axis=0)
    prompt = jnp.broadcast_to(plane[:1], own.shape)
    keys = exchange(jnp.concatenate([prompt, own], axis=1), "ctx")
    keys = keys.reshape(ctx_count * 2 * exp_count, latent_width)

    shard_index = lax.axis_index("ctx")
    group = shard_index // BLOCK
    ends = subtree_end.reshape(GROUPS, BLOCK, exp_count, row_group)
    positions = jnp.arange(subtree_end.shape[0], dtype=jnp.int32).reshape(ends.shape)

    def key_order(table, hide):
        own_table = lax.dynamic_index_in_dim(table, group, 0, keepdims=False)
        own_table = jnp.where(group == 0, hide, own_table)
        both = jnp.stack([table[0], own_table])
        return both.transpose(1, 3, 0, 2).reshape(-1)

    key_end = key_order(ends, -1)
    key_index = key_order(positions, 0)
    local = queries.shape[0]
    heads = queries.shape[1]
    query_index = shard_index * local + jnp.arange(local, dtype=jnp.int32)
    visible = (key_index[None, :] <= query_index[:, None]) & (query_index[:, None] <= key_end[None, :])
    scores = jnp.einsum("qhl,kl->qhk", queries, keys, preferred_element_type=f32) * score_scale
    scores = jnp.where(visible[:, None, :], scores, neg_fill)
    top = jnp.max(scores, axis=2, keepdims=True)
    exp_scores = jnp.where(visible[:, None, :], jnp.exp(scores - top), 0.0)
    denom = jnp.sum(exp_scores, axis=2)
    mixed = jnp.einsum("qhk,kl->qhl", exp_scores.astype(bf16), keys, preferred_element_type=f32)
    attn_out = (mixed / denom[:, :, None]).astype(bf16)
    return (next_rows.reshape(hidden.shape), attn_out)


def solution(mesh):
    return jax.shard_map(
        body,
        mesh=mesh,
        in_specs=(
            P("exp", None, "ctx"),
            P("exp", None, None),
            P("exp", None, None),
            P("ctx"),
            P("exp", "ctx", None),
            P("exp", "ctx", None),
            P("exp", None, "ctx"),
            P("ctx", None),
            P(),
            P("ctx", "exp", None),
            P(),
        ),
        out_specs=(P("exp", None, "ctx"), P("ctx", "exp", None)),
        check_vma=False,
    )
```

time: 474 us -> 165 us (0.35)
  waiting for transfers between devices: 304 us -> 27 us
  between operations: 14 us -> 1.09 us
  blocking collectives: 117 us -> 109 us
  matrix products: 13.6 us -> 7.52 us
  other arithmetic: 8.43 us -> 2.39 us
    psum x1 -> x0, waiting for transfers between devices: 134 us -> none  [expert_block(): gate_total, up_total = lax.psum((gate_part, up_part), 'ctx')]
    reduce_scatter x1 -> x0, waiting for transfers between devices: 93.1 us -> none  [body(): lax.psum_scatter(jnp.einsum('rcd,dl->crl', next_hidden, latent_weight, pr...]
    all_to_all x1 -> x5, blocking collectives: 21.6 us -> 109 us  [exchange(): return lax.all_to_all(chunks, axis, split_axis=0, concat_axis=0, tiled=True)]
    psum x1 -> x0, blocking collectives: 68.9 us -> none  [body(): square_total = lax.psum(square_part, 'ctx')]
    all_gather x1 -> x0, waiting for transfers between devices: 64.2 us -> none  [body(): key_block = lax.all_gather(shard_latent, 'ctx', axis=0, tiled=True)]
    all_gather x1 -> x0, blocking collectives: 26.5 us -> none  [body(): shard_latent = lax.all_gather(latent_local, 'exp', axis=0, tiled=True)]
    all_to_all x1 -> x2, waiting for transfers between devices: 11.6 us -> 27 us  [exchange(): return lax.all_to_all(chunks, axis, split_axis=0, concat_axis=0, tiled=True)]
    dot_general x8 -> x9, matrix products: 13.6 us -> 5.11 us  [the longest x1 1.96 us: body(): jnp.einsum('qhk,kl->qhl', exp_scores.astype(bf16), keys, preferred_elemen...]
  transfers between devices with their start and end apart: 4 -> 2, of which waited for: 4 -> 2; matrix products, arithmetic and copies ran while one was open for 0% -> 1% of each run, Pallas kernels for 0% -> 0%
where the time goes in v1:
time: 165 us
  blocking collectives  109 us (66%)
  waiting for transfers between devices  27 us (16%)
  starting transfers between devices  10.2 us (6%)
  local copies, waits for them, and re-layouts  7.85 us (5%)
  matrix products  7.52 us (5%)
  other arithmetic  2.39 us (1%)
    all_to_all x5, blocking collectives, exchange(): return lax.all_to_all(chunks, axis, split_axis=0, concat_axis=0, tiled=True)  109 us
    all_to_all x2, waiting for transfers between devices, exchange(): return lax.all_to_all(chunks, axis, split_axis=0, concat_axis=0, tiled=True)  27 us
    all_to_all x2, starting transfers between devices, exchange(): return lax.all_to_all(chunks, axis, split_axis=0, concat_axis=0, tiled=True)  10.2 us
    unnamed x23, local copies, waits for them, and re-layouts  3.82 us
  transfers between devices with their start and end apart: 2, of which 2 were waited for; matrix products, arithmetic and copies ran while one was open for 1% of the time, Pallas kernels for 0%

profile of v1, /device:TPU:1, one launch (start us, length us, event | category | flops | bytes accessed | tf_op | source)
XLA Modules:
  0.0 164.7 jit_solution(17809259969846127078)
XLA Ops:
  0.6 0.0 copy-start
  0.6 0.0 copy-start.6
  0.7 0.9 copy.84
  1.5 0.1 broadcast_in_dim.99
  1.6 0.8 copy.83
  2.4 0.1 eq.44
  2.5 0.2 convolution_select_fusion
  2.7 1.1 convolution_convert_fusion.4
  3.9 27.4 %all_to_all.35 = bf16[16,24,128]{2,1,0:T(8,128)(2,1)S(1)} all-to-all(bf16[16,24,128]{2,1,0:T(8,128)(2,1)S(1)} %reshape.320), channel_id=1, replica_groups=mesh['ctx'=32,'exp'=16] {'exp'}, dimensions={0} | all-to-all | bytes 196608 | tf_op jit(solution)/shard_map/all_to_all | solution.py:19
  31.4 0.0 copy-done.6
  31.4 0.1 fusion.19
  31.5 0.0 copy-done
  31.5 0.0 copy-start.1
  31.6 0.4 fusion.3
  31.9 0.2 copy.97
  32.1 0.6 copy-done.1
  32.7 0.4 fusion.4
  33.1 0.2 copy.98
  33.3 0.1 reshape.324
  33.4 0.4 copy_bitcast_fusion
  33.8 0.1 pad_maximum_fusion
  33.9 33.0 %all_to_all.36 = bf16[32,200,128]{2,1,0:T(8,128)(2,1)S(1)} all-to-all(bf16[32,200,128]{2,1,0:T(8,128)(2,1)S(1)} %bitcast.88), channel_id=1, replica_groups=mesh['ctx'=32,'exp'=16] {'ctx'}, dimensions={0} | all-to-all | bytes 3276800 | tf_op jit(solution)/shard_map/all_to_all | solution.py:19
  66.9 0.2 convert_reduce_fusion
  67.2 0.1 fusion.38
  67.3 0.1 broadcast_in_dim.104
  67.4 0.0 copy-start.7
  67.4 17.9 %all_to_all.37 = bf16[32,96,128]{2,1,0:T(8,128)(2,1)S(1)} all-to-all(bf16[32,96,128]{2,1,0:T(8,128)(2,1)S(1)} %broadcast_in_dim.104), channel_id=1, replica_groups=mesh['ctx'=32,'exp'=16] {'ctx'}, dimensions={0} | all-to-all | bytes 1572864 | tf_op jit(solution)/shard_map/all_to_all | solution.py:19
  85.3 0.5 copy.87
  85.8 0.0 copy-start.2
  85.8 0.0 copy-done.7
  85.8 0.5 convolution_convert_fusion.3
  86.3 0.0 copy-start.3
  86.4 0.7 reshape.329
  87.1 3.5 %all-to-all-start.3 = ((bf16[16,24,128]{2,1,0:T(8,128)(2,1)}), bf16[16,24,128]{2,1,0:T(8,128)(2,1)S(1)}, u32[]{:S(2)}, u32[]{:S(2)}) async-start(bf16[16,24,128]{2,1,0:T(8,128)(2,1)} %reshape.329), calls=%async_computation.3 | async-start | bytes 196608 | tf_op jit(solution)/shard_map/all_to_all | solution.py:19
  90.6 0.0 copy-done.2
  90.6 0.1 copy.82
  90.7 11.6 %all-to-all-done.3 = bf16[16,24,128]{2,1,0:T(8,128)(2,1)S(1)} async-done(((bf16[16,24,128]{2,1,0:T(8,128)(2,1)}), bf16[16,24,128]{2,1,0:T(8,128)(2,1)S(1)}, u32[]{:S(2)}, u32[]{:S(2)}) %all-to-all-start.3) | async-done | bytes 98336 | tf_op jit(solution)/shard_map/all_to_all | solution.py:19
  102.4 0.2 convolution_bitcast_fusion
  102.6 0.0 copy-start.5
  102.6 0.2 fusion.7
  102.9 0.0 copy-done.3
  102.9 0.2 convolution_convert_fusion.2
  103.2 0.1 reshape.342
  103.3 14.7 %all_to_all.38 = bf16[32,8,512]{2,1,0:T(8,128)(2,1)S(1)} all-to-all(bf16[32,8,512]{2,1,0:T(8,128)(2,1)S(1)} %bitcast.95), channel_id=1, replica_groups=mesh['ctx'=32,'exp'=16] {'ctx'}, dimensions={0} | all-to-all | bytes 524288 | tf_op jit(solution)/shard_map/all_to_all | solution.py:19
  118.0 0.1 multiply_reduce_fusion
  118.2 0.1 multiply_convert_fusion
  118.3 15.7 %all_to_all.39 = bf16[16,8,512]{2,1,0:T(8,128)(2,1)S(1)} all-to-all(bf16[16,8,512]{2,1,0:T(8,128)(2,1)S(1)} %broadcast_in_dim.109), channel_id=1, replica_groups=mesh['ctx'=32,'exp'=16] {'exp'}, dimensions={0} | all-to-all | bytes 262144 | tf_op jit(solution)/shard_map/all_to_all | solution.py:19
  134.0 0.1 broadcast_in_dim.111
  134.1 0.1 broadcast_in_dim.112
  134.1 0.0 copy-start.4
  134.1 1.1 pad_maximum_fusion.1
  135.2 6.7 %all-to-all-start.6 = ((bf16[32,32,512]{2,1,0:T(8,128)(2,1)}), bf16[32,32,512]{2,1,0:T(8,128)(2,1)S(1)}, u32[]{:S(2)}, u32[]{:S(2)}) async-start(bf16[32,32,512]{2,1,0:T(8,128)(2,1)} %pad_maximum_fusion.1), calls=%async_computation.6 | async-start | bytes 2097152 | tf_op jit(solution)/shard_map/all_to_all | solution.py:19
  141.9 0.2 reshape.341
  142.2 0.1 copy.89
  142.2 0.1 le.36
  142.3 0.1 slice.46
  142.5 0.1 copy.90
  142.6 0.1 le.40
  142.7 0.3 compare_and_fusion
  143.0 0.8 copy.88
  143.8 15.4 %all-to-all-done.6 = bf16[32,32,512]{2,1,0:T(8,128)(2,1)S(1)} async-done(((bf16[32,32,512]{2,1,0:T(8,128)(2,1)}), bf16[32,32,512]{2,1,0:T(8,128)(2,1)S(1)}, u32[]{:S(2)}, u32[]{:S(2)}) %all-to-all-start.6) | async-done | bytes 1048608 | tf_op jit(solution)/shard_map/all_to_all | solution.py:19
  159.2 2.4 %fusion.56 = (f32[128,4]{0,1:T(4,128)S(1)}, bf16[128,4,1024]{0,2,1:T(8,128)(2,1)}) fusion(pred[128,1024]{0,1:T(8,128)(4,1)S(1)} %compare_and_fusion, bf16[1024,512,1]{1,0,2:T(8,128)(2,1)S(1)} %bitcast.93, bf16[128,4,512]{2,1,0:T(4,128)(2,1)S(1)} %copy-done.8), kind=kOutput, calls=%fused_computation.93 | convolution fusion | flops 540017664 | bytes 2754560 | tf_op jit(solution)/shard_map/sub | solution.py:138
  161.6 2.0 %fusion.2 = bf16[128,4,512]{2,0,1:T(8,128)(2,1)S(1)} fusion(bf16[1024,512,1]{1,0,2:T(8,128)(2,1)S(1)} %bitcast.94, bf16[128,4,1024]{0,2,1:T(8,128)(2,1)} %get-tuple-element.25, f32[128,4]{0,1:T(4,128)S(1)} %get-tuple-element.24), kind=kOutput, calls=%fused_computation.9 | convolution fusion | flops 537395200 | bytes 2623488 | tf_op jit(solution)/shard_map/qhk,kl->qhl/dot_general | solution.py:140
  163.5 1.2 copy.95
  (33 shorter events, 0.7 us)
Async XLA Ops:
  0.6 30.9 %copy-start = (bf16[1,224,2048]{2,1,0:T(8,128)(2,1)S(1)}, bf16[1,224,2048]{2,1,0:T(8,128)(2,1)}, u32[]{:S(2)}) copy-start(bf16[1,224,2048]{2,1,0:T(8,128)(2,1)} %param.15) | copy-start | bytes 2752516
  0.6 30.7 %copy-start.6 = (f32[224]{0:T(256)S(1)}, f32[224]{0:T(256)}, u32[]{:S(2)}) copy-start(f32[224]{0:T(256)} %param.14) | copy-start | bytes 2692
  31.5 1.2 copy-start.1
  67.4 18.4 %copy-start.7 = (bf16[1,2048,224]{1,2,0:T(8,128)(2,1)S(1)}, bf16[1,2048,224]{1,2,0:T(8,128)(2,1)}, u32[]{:S(2)}) copy-start(bf16[1,2048,224]{1,2,0:T(8,128)(2,1)} %param.17) | copy-start | bytes 2752516
  85.8 4.8 %copy-start.2 = (bf16[8,32,224]{2,1,0:T(8,128)(2,1)S(1)}, bf16[8,32,224]{2,1,0:T(8,128)(2,1)}, u32[]{:S(2)}) copy-start(bf16[8,32,224]{2,1,0:T(8,128)(2,1)} %param.11) | copy-start | bytes 344068
  86.3 16.6 %copy-start.3 = (bf16[224,512]{1,0:T(8,128)(2,1)S(1)}, bf16[224,512]{1,0:T(8,128)(2,1)}, u32[]{:S(2)}) copy-start(bf16[224,512]{1,0:T(8,128)(2,1)} %param.18) | copy-start | bytes 688132
  87.1 15.3 %all-to-all-start.3 = ((bf16[16,24,128]{2,1,0:T(8,128)(2,1)}), bf16[16,24,128]{2,1,0:T(8,128)(2,1)S(1)}, u32[]{:S(2)}, u32[]{:S(2)}) async-start(bf16[16,24,128]{2,1,0:T(8,128)(2,1)} %reshape.329), calls=%async_computation.3 | async-start | bytes 196608 | tf_op jit(solution)/shard_map/all_to_all | solution.py:19
  102.6 15.5 %copy-start.5 = (f32[512]{0:T(512)S(1)}, f32[512]{0:T(512)}, u32[]{:S(2)}) copy-start(f32[512]{0:T(512)} %param.19) | copy-start | bytes 6148
  134.1 7.8 %copy-start.4 = (s32[4096]{0:T(1024)S(1)}, s32[4096]{0:T(1024)}, u32[]{:S(2)}) copy-start(s32[4096]{0:T(1024)} %param.21) | copy-start | bytes 49156
  135.2 7.1 %slice-start = ((s32[4096]{0:T(1024)}), s32[512]{0:T(512)S(1)}, s32[]{:S(2)}) async-start(s32[4096]{0:T(1024)} %param.21), calls=%async_computation.7 | async-start | bytes 4096 | tf_op jit(solution)/shard_map/slice | solution.py:126
  135.2 24.0 %copy-start.8 = (bf16[128,4,512]{2,1,0:T(4,128)(2,1)S(1)}, bf16[128,4,512]{2,1,0:T(4,128)(2,1)}, u32[]{:S(2)}) copy-start(bf16[128,4,512]{2,1,0:T(4,128)(2,1)} %param.20) | copy-start | bytes 1572868
  135.2 24.0 %all-to-all-start.6 = ((bf16[32,32,512]{2,1,0:T(8,128)(2,1)}), bf16[32,32,512]{2,1,0:T(8,128)(2,1)S(1)}, u32[]{:S(2)}, u32[]{:S(2)}) async-start(bf16[32,32,512]{2,1,0:T(8,128)(2,1)} %pad_maximum_fusion.1), calls=%async_computation.6 | async-start | bytes 2097152 | tf_op jit(solution)/shard_map/all_to_all | solution.py:19

commit v2 on v1

v2 whole, which is shorter than its diff:
```python
import jax
import jax.numpy as jnp
from jax import lax
from jax.experimental import pallas as pl
from jax.experimental.pallas import tpu as pltpu
from jax.sharding import PartitionSpec as P

D = 7168
TOP = 8
CAP = 12
PART = 6
PAD = 8
WIDE = 256
GROUPS = 8
BLOCK = 4
COST = 400_000_000_000


score_scale = 192 ** (-0.5)
norm_eps = 1e-06
neg_fill = -1e30
bf16, f32 = jnp.bfloat16, jnp.float32


def exchange(chunks, axis):
    return lax.all_to_all(chunks, axis, split_axis=0, concat_axis=0, tiled=True)


def exchange_chips(chunks):
    count = lax.axis_size("ctx")
    groups = [list(range(core, count, 2)) for core in range(2)]
    return lax.all_to_all(
        chunks, "ctx", split_axis=0, concat_axis=0, tiled=True, axis_index_groups=groups
    )


def swap(value):
    count = lax.axis_size("ctx")
    return lax.ppermute(value, "ctx", [(i, i ^ 1) for i in range(count)])


def dot(left, right):
    return jnp.dot(left, right, preferred_element_type=f32)


def dot_last(left, right):
    return lax.dot_general(left, right, (((1,), (1,)), ((), ())), preferred_element_type=f32)


def iota(shape, dim):
    return lax.broadcasted_iota(jnp.int32, shape, dim)


def local_kernel(kernel, out_shape, *operands, spaces=None, grant=6, **kwargs):
    spaces = spaces or [pltpu.VMEM] * len(operands)
    return pl.pallas_call(
        kernel,
        out_shape=out_shape,
        in_specs=[pl.BlockSpec(memory_space=space) for space in spaces],
        out_specs=jax.tree.map(lambda _: pl.BlockSpec(memory_space=pltpu.VMEM), out_shape),
        compiler_params=pltpu.CompilerParams(vmem_limit_bytes=grant * 1024 * 1024),
        **kwargs,
    )(*operands)


def routing_kernel(core_ref, expert_ref, gate_ref, placed_ref, table_ref):
    core = core_ref[0]
    group, run = expert_ref.shape
    tokens = group * run
    spread = (iota((tokens, group), 0) // run == iota((tokens, group), 1)).astype(f32)
    inside = iota((tokens, run), 0) % run == iota((tokens, run), 1)

    def column(values):
        values = jnp.dot(spread, values, preferred_element_type=f32, precision=lax.Precision.HIGHEST)
        return jnp.sum(jnp.where(inside, values, 0.0), axis=1, keepdims=True)

    expert, gate = column(expert_ref[...]), column(gate_ref[...])
    lane = iota((tokens, 128), 1).astype(f32)
    picked = expert == lane
    earlier = (iota((tokens, tokens), 1) < iota((tokens, tokens), 0)).astype(bf16)
    rank = dot(earlier, picked.astype(bf16))
    rank = jnp.sum(jnp.where(picked, rank, 0.0), axis=1, keepdims=True)

    def slot_in(part):
        place = rank - (part * PART).astype(f32)
        valid = (expert >= 0) & (place >= 0) & (place < PART)
        return jnp.where(valid, expert * PAD + place, -1.0)

    slot = slot_in(core)
    padded = placed_ref.shape[0]
    slot_rows = jnp.transpose(jnp.broadcast_to(slot, (tokens, padded)))
    placed_ref[...] = (slot_rows == iota((padded, tokens), 0).astype(f32)).astype(bf16)
    table_ref[...] = jnp.where(lane == 0, slot, jnp.where(lane == 1, slot_in(1 - core), gate))


def dispatch_kernel(placed_ref, own_ref, pair_ref, out_ref):
    placed = placed_ref[...]
    width = own_ref.shape[1]
    for start, rows in ((0, own_ref), (WIDE, pair_ref)):
        out_ref[:, start : start + WIDE] = jnp.zeros((placed.shape[0], WIDE), bf16)
        out_ref[:, start : start + width] = dot(placed, rows[...]).astype(bf16)


def slot_choice(rows, columns, half, flip):
    wide, narrow = (1, 0) if not flip else (0, 1)
    padded, packed = iota((rows, columns), wide), iota((rows, columns), narrow)
    packed_place = packed // PART * PAD + packed % PART
    return ((padded == packed_place) & (packed < half)).astype(bf16)


def packed_kernel(half, received_ref, gain_ref, gain_pair_ref, own_ref, pair_ref, square_ref):
    width = gain_ref.shape[1]
    rows = dot(slot_choice(128, received_ref.shape[0], half, False), received_ref[...])
    own_ref[...] = (rows[:half, :width] * gain_ref[0:1, :]).astype(bf16)
    pair_ref[...] = (rows[:half, WIDE : WIDE + width] * gain_pair_ref[0:1, :]).astype(bf16)
    squares = jnp.sum(rows * rows, axis=1, keepdims=True)
    squares = jnp.transpose(jnp.broadcast_to(squares, (128, 128)))[:16]
    high = squares.astype(bf16).astype(f32)
    sub = iota((16, 128), 0)
    square_ref[...] = jnp.where(sub == 0, high, jnp.where(sub == 1, squares - high, 0.0)).astype(bf16)


def gate_up_kernel(own_ref, pair_ref, square_ref, gate_own, gate_pair, up_own, up_pair, out_ref):
    half = own_ref.shape[0]
    owners, _, lanes = out_ref.shape
    own, pair, squares = own_ref[...], pair_ref[...], square_ref[...]
    group = 4
    for first in range(0, owners, group):
        span = slice(first * lanes, (first + group) * lanes)
        gate = (dot(own, gate_own[:, span]) + dot(pair, gate_pair[:, span])).astype(bf16)
        up = (dot(own, up_own[:, span]) + dot(pair, up_pair[:, span])).astype(bf16)
        for at in range(group):
            lane = slice(at * lanes, (at + 1) * lanes)
            out_ref[first + at, :half] = gate[:, lane]
            out_ref[first + at, half : 2 * half] = up[:, lane]
            out_ref[first + at, 2 * half :] = squares


def hidden_unit_kernel(half, partial_ref, out_ref):
    total = jnp.sum(partial_ref[...].astype(f32), axis=0)
    squares = total[2 * half : 2 * half + 1] + total[2 * half + 1 : 2 * half + 2]
    lanes = squares.shape[1]
    scale = lax.rsqrt(squares / D + norm_eps)
    scale = jnp.transpose(jnp.broadcast_to(scale, (lanes, lanes)))[:half]
    gate = total[:half] * scale
    up = total[half : 2 * half] * scale
    units = (gate / (1.0 + jnp.exp(-gate)) * up).astype(bf16)
    for owner in range(out_ref.shape[0]):
        out_ref[owner] = units


def combine_kernel(returned_ref, table_ref, rows_ref, own_ref, pair_ref, out_ref):
    tokens, width = rows_ref.shape
    padded = returned_ref.shape[0]
    slot, gate = table_ref[:, 0:1], table_ref[:, 2:3]
    choice = (slot == iota((tokens, padded), 1).astype(f32)).astype(bf16)
    moe = dot(choice, returned_ref[...]) * gate
    next_own = (rows_ref[...].astype(f32) + moe[:, :width]).astype(bf16)
    next_pair = moe[:, WIDE : WIDE + width].astype(bf16)
    target, source = iota((tokens, tokens), 0), iota((tokens, tokens), 1)
    run = GROUPS * BLOCK
    rest = target % (tokens // BLOCK)
    wanted = rest // GROUPS * run + rest % GROUPS * BLOCK + target // (tokens // BLOCK)
    order = (source == wanted).astype(bf16)
    own = dot(order, next_own).astype(bf16)
    pair = dot(order, next_pair).astype(bf16)
    out_ref[...] = (dot(own, own_ref[...]) + dot(pair, pair_ref[...])).astype(bf16)


def next_kernel(returned_ref, rest_ref, table_ref, rows_ref, out_ref):
    tokens, width = rows_ref.shape
    padded = returned_ref.shape[0]
    lane = iota((tokens, padded), 1).astype(f32)
    moe = dot((table_ref[:, 0:1] == lane).astype(bf16), returned_ref[:, :width])
    moe += dot((table_ref[:, 1:2] == lane).astype(bf16), rest_ref[:, :width])
    out_ref[...] = (rows_ref[...].astype(f32) + moe * table_ref[:, 2:3]).astype(bf16)


def body(
    hidden,
    routes,
    gates,
    moe_gain,
    gate_weight,
    up_weight,
    down_weight,
    latent_weight,
    latent_gain,
    queries,
    subtree_end,
):
    row_group, shard_count, width = hidden.shape
    tokens = row_group * shard_count
    exp_count = lax.axis_size("exp")
    ctx_count = lax.axis_size("ctx")
    chips = ctx_count // 2
    half = exp_count * PART
    padded = exp_count * PAD
    hidden_width = gate_weight.shape[2]
    lanes = hidden_width // chips
    latent_width = latent_weight.shape[1]

    rows = hidden.reshape(tokens, width)
    rows_pair = swap(rows)
    core = lax.rem(lax.axis_index("ctx"), 2)
    shape = jax.ShapeDtypeStruct
    near = routes < exp_count
    expert = jnp.max(jnp.where(near, routes, -1), axis=2).astype(f32)
    gate = jnp.sum(jnp.where(near, gates, 0.0), axis=2)
    placed, table = local_kernel(
        routing_kernel,
        (shape((padded, tokens), bf16), shape((tokens, 128), f32)),
        core.reshape(1),
        expert,
        gate,
        spaces=[pltpu.SMEM] + [pltpu.VMEM] * 2,
    )
    wide = shape((padded, 2 * WIDE), bf16)
    dispatched = local_kernel(dispatch_kernel, wide, placed, rows, rows_pair)
    own = (moe_gain, gate_weight[0], up_weight[0], down_weight[0].T, latent_weight)
    dispatched, own = lax.optimization_barrier((dispatched, own))
    gain_own = jnp.broadcast_to(own[0][None, :], (8, width))
    down_own = own[3]
    gain_pair, gate_pair, up_pair, down_pair, latent_pair = [swap(value) for value in (gain_own,) + own[1:]]
    gate_own, up_own = own[1], own[2]
    received = exchange(dispatched.reshape(exp_count, PAD, 2 * WIDE), "exp").reshape(padded, 2 * WIDE)

    packed = local_kernel(
        lambda *refs: packed_kernel(half, *refs),
        (shape((half, width), bf16), shape((half, width), bf16), shape((16, 128), bf16)),
        received,
        gain_own,
        gain_pair,
        cost_estimate=pl.CostEstimate(flops=COST, bytes_accessed=COST, transcendentals=0),
    )
    partial = local_kernel(
        gate_up_kernel, shape((chips, 2 * half + 16, lanes), bf16), *packed, gate_own, gate_pair, up_own, up_pair
    )
    partial = exchange_chips(partial)
    units = local_kernel(
        lambda *refs: hidden_unit_kernel(half, *refs), shape((chips, half, lanes), bf16), partial
    )
    spread = exchange_chips(units).transpose(1, 0, 2).reshape(half, hidden_width)

    fill = ((0, 0), (0, WIDE - width))
    expert_out = jnp.concatenate(
        [
            jnp.pad(lax.dot_general(spread, w, (((1,), (1,)), ((), ())), preferred_element_type=f32).astype(bf16), fill)
            for w in (down_own, down_pair)
        ],
        axis=1,
    )
    expert_out = jnp.pad(expert_out.reshape(exp_count, PART, 2 * WIDE), ((0, 0), (0, PAD - PART), (0, 0)))
    returned = exchange(expert_out, "exp").reshape(padded, 2 * WIDE)
    returned_rest = swap(returned[:, WIDE:])
    latent_part = local_kernel(
        combine_kernel,
        jax.ShapeDtypeStruct((tokens, latent_width), bf16),
        returned,
        table,
        rows,
        latent_weight,
        latent_pair,
    )
    latent_part = exchange(latent_part.reshape(ctx_count, GROUPS, latent_width), "ctx")
    latent_raw = jnp.sum(latent_part.astype(f32), axis=0)
    latent_rms = lax.rsqrt(jnp.mean(latent_raw * latent_raw, axis=1, keepdims=True) + norm_eps)
    latent = (latent_raw * latent_rms * latent_gain[None, :]).astype(bf16)
    latent, returned_rest = lax.optimization_barrier((latent, returned_rest))
    plane = exchange(jnp.broadcast_to(latent[None], (exp_count,) + latent.shape), "exp")
    plane = plane.transpose(1, 0, 2)
    own = jnp.repeat(plane, BLOCK // 2, axis=0)
    prompt = jnp.broadcast_to(plane[:1], own.shape)
    keys = exchange_chips(jnp.concatenate([prompt, own], axis=1))
    keys = keys.reshape(chips * 2 * exp_count, latent_width)
    all_keys = (keys, swap(keys))

    next_rows = local_kernel(
        next_kernel, jax.ShapeDtypeStruct(rows.shape, bf16), returned, returned_rest, table, rows
    )

    shard_index = lax.axis_index("ctx")
    group = shard_index // BLOCK
    ends = subtree_end.reshape(GROUPS, BLOCK, exp_count, row_group // 2, 2)
    positions = jnp.arange(subtree_end.shape[0], dtype=jnp.int32).reshape(ends.shape)

    def key_order(table, hide, part):
        table = lax.dynamic_index_in_dim(table, part, 4, keepdims=False)
        own_table = lax.dynamic_index_in_dim(table, group, 0, keepdims=False)
        own_table = jnp.where(group == 0, hide, own_table)
        both = jnp.stack([table[0], own_table])
        return both.transpose(1, 3, 0, 2).reshape(-1)

    local, heads = queries.shape[:2]
    query_index = shard_index * local + jnp.arange(local, dtype=jnp.int32)

    def attended(part_keys, part):
        key_end, key_index = key_order(ends, -1, part), key_order(positions, 0, part)
        visible = (key_index[None, :] <= query_index[:, None]) & (query_index[:, None] <= key_end[None, :])
        visible = visible[:, None, :]
        scores = jnp.einsum("qhl,kl->qhk", queries, part_keys, preferred_element_type=f32) * score_scale
        scores = jnp.where(visible, scores, neg_fill)
        top = jnp.max(scores, axis=2)
        exp_scores = jnp.where(visible, jnp.exp(scores - top[:, :, None]), 0.0)
        mixed = jnp.einsum("qhk,kl->qhl", exp_scores.astype(bf16), part_keys, preferred_element_type=f32)
        return top, jnp.sum(exp_scores, axis=2), mixed

    parts = [attended(part_keys, part) for part_keys, part in zip(all_keys, (core, 1 - core))]
    top = jnp.maximum(parts[0][0], parts[1][0])
    shares = [jnp.exp(part[0] - top) for part in parts]
    denom = sum(share * part[1] for share, part in zip(shares, parts))
    mixed = sum(share[:, :, None] * part[2] for share, part in zip(shares, parts))
    attn_out = (mixed / denom[:, :, None]).astype(bf16)
    return (next_rows.reshape(hidden.shape), attn_out)


def solution(mesh):
    return jax.shard_map(
        body,
        mesh=mesh,
        in_specs=(
            P("exp", None, "ctx"),
            P("exp", None, None),
            P("exp", None, None),
            P("ctx"),
            P("exp", "ctx", None),
            P("exp", "ctx", None),
            P("exp", None, "ctx"),
            P("ctx", None),
            P(),
            P("ctx", "exp", None),
            P(),
        ),
        out_specs=(P("exp", None, "ctx"), P("ctx", "exp", None)),
        check_vma=False,
    )
```

time: 165 us -> 154 us (0.933)
  blocking collectives: 109 us -> 11.6 us
  starting transfers between devices: 10.2 us -> 72.2 us
  waiting for transfers between devices: 27 us -> 46.7 us
  Pallas kernels: 0 us -> 7.48 us
  matrix products: 7.52 us -> 2.85 us
    all_to_all x5 -> x1, blocking collectives: 109 us -> 11.6 us  [exchange_chips(): lax.all_to_all(chunks, 'ctx', split_axis=0, concat_axis=0, tiled=True, ax...]
    ppermute x0 -> x8, starting transfers between devices: none -> 31.9 us  [swap(): return lax.ppermute(value, 'ctx', [(i, i ^ 1) for i in range(count)])]
    all_to_all x2 -> x4, starting transfers between devices: 10.2 us -> 29.8 us  [exchange(): return lax.all_to_all(chunks, axis, split_axis=0, concat_axis=0, tiled=True)]
    all_to_all x0 -> x2, waiting for transfers between devices: none -> 17.3 us  [exchange_chips(): lax.all_to_all(chunks, 'ctx', split_axis=0, concat_axis=0, tiled=True, ax...]
    all_to_all x0 -> x2, starting transfers between devices: none -> 10.5 us  [exchange_chips(): lax.all_to_all(chunks, 'ctx', split_axis=0, concat_axis=0, tiled=True, ax...]
    pallas_call x0 -> x7, Pallas kernels: none -> 7.48 us  [local_kernel(): pl.pallas_call(kernel, out_shape=out_shape, in_specs=[pl.BlockSpec(memory...]
    sub x1 -> x0, matrix products: 2.42 us -> none  [body(): exp_scores = jnp.where(visible[:, None, :], jnp.exp(scores - top), 0.0)]
    dot_general x9 -> x6, matrix products: 5.11 us -> 2.85 us  [the longest x2 1 us: attended(): jnp.einsum('qhl,kl->qhk', queries, part_keys, preferred_element_type=f32)]
  transfers between devices with their start and end apart: 2 -> 14, of which waited for: 2 -> 7; matrix products, arithmetic and copies ran while one was open for 1% -> 4% of each run, Pallas kernels for 0% -> 1%
where the time goes in v2:
time: 154 us; the launch traced here: 153 us
  starting transfers between devices  72.2 us (47%)
  waiting for transfers between devices  46.7 us (30%)
  blocking collectives  11.6 us (8%)
  local copies, waits for them, and re-layouts  7.77 us (5%)
  Pallas kernels  7.48 us (5%)
  other arithmetic  3.52 us (2%)
  matrix products  2.85 us (2%)
    ppermute x8, starting transfers between devices, swap(): return lax.ppermute(value, 'ctx', [(i, i ^ 1) for i in range(count)])  31.9 us
    all_to_all x4, starting transfers between devices, exchange(): return lax.all_to_all(chunks, axis, split_axis=0, concat_axis=0, tiled=True)  29.8 us
    all_to_all x4, waiting for transfers between devices, exchange(): return lax.all_to_all(chunks, axis, split_axis=0, concat_axis=0, tiled=True)  28.2 us
    all_to_all x2, waiting for transfers between devices, exchange_chips(): lax.all_to_all(chunks, 'ctx', split_axis=0, concat_axis=0, tiled=True, ax...  17.3 us
    all_to_all x1, blocking collectives, exchange_chips(): lax.all_to_all(chunks, 'ctx', split_axis=0, concat_axis=0, tiled=True, ax...  11.6 us
    all_to_all x2, starting transfers between devices, exchange_chips(): lax.all_to_all(chunks, 'ctx', split_axis=0, concat_axis=0, tiled=True, ax...  10.5 us
    pallas_call x7, Pallas kernels, local_kernel(): pl.pallas_call(kernel, out_shape=out_shape, in_specs=[pl.BlockSpec(memory...  7.48 us
    unnamed x24, local copies, waits for them, and re-layouts  4.08 us
  transfers between devices with their start and end apart: 14, of which 7 were waited for; matrix products, arithmetic and copies ran while one was open for 4% of the time, Pallas kernels for 1%

profile of v2, /device:TPU:1, one launch (start us, length us, event | category | flops | bytes accessed | tf_op | source)
XLA Modules:
  0.0 153.2 jit_solution(12066208632809271440)
XLA Ops:
  0.6 0.0 copy-start
  0.6 0.0 copy-start.1
  0.7 8.9 %collective-permute-start = (bf16[256,224]{1,0:T(8,128)(2,1)}, bf16[256,224]{1,0:T(8,128)(2,1)S(1)}, u32[]{:S(2)}, u32[]{:S(2)}) collective-permute-start(bf16[256,224]{1,0:T(8,128)(2,1)} %bitcast.78), channel_id=1, source_target_pairs={{0,16},{16,0},{32,48},{48,32},{64,80},{80,64},{96,112},{112,96},{1... | collective-permute-start | bytes 344072 | tf_op jit(solution)/shard_map/ppermute | solution.py:39
  9.6 0.8 fusion.30
  10.4 0.8 fusion.31.gate_ref
  11.2 0.7 shard_map.122
  11.9 0.8 shard_map.123
  12.8 9.7 %all-to-all-start = ((bf16[16,8,512]{2,1,0:T(8,128)(2,1)}), bf16[16,8,512]{2,1,0:T(8,128)(2,1)S(1)}, u32[]{:S(2)}, u32[]{:S(2)}) async-start(bf16[16,8,512]{2,1,0:T(8,128)(2,1)} %bitcast.6), calls=%async_computation | async-start | bytes 262144 | tf_op jit(solution)/shard_map/all_to_all | solution.py:26
  22.5 2.2 %collective-permute-start.1 = (f32[8,224]{1,0:T(8,128)S(1)}, f32[8,224]{1,0:T(8,128)S(1)}, u32[]{:S(2)}, u32[]{:S(2)}) collective-permute-start(f32[8,224]{1,0:T(8,128)S(1)} %broadcast_in_dim.82.refs_1_), channel_id=1, source_target_pairs={{0,16},{16,0},{32,48},{48,32},{64,80},{80,64},{96,112},{112,96},{1... | collective-permute-start | bytes 21512 | tf_op jit(solution)/shard_map/ppermute | solution.py:39
  24.7 2.1 %collective-permute-start.2 = (bf16[224,2048]{1,0:T(8,128)(2,1)}, bf16[224,2048]{1,0:T(8,128)(2,1)}, u32[]{:S(2)}, u32[]{:S(2)}) collective-permute-start(bf16[224,2048]{1,0:T(8,128)(2,1)} %bitcast.82), channel_id=1, source_target_pairs={{0,16},{16,0},{32,48},{48,32},{64,80},{80,64},{96,112},{112,96},{1... | collective-permute-start | bytes 2752520 | tf_op jit(solution)/shard_map/ppermute | solution.py:39
  26.8 2.2 %collective-permute-start.3 = (bf16[224,2048]{1,0:T(8,128)(2,1)}, bf16[224,2048]{1,0:T(8,128)(2,1)}, u32[]{:S(2)}, u32[]{:S(2)}) collective-permute-start(bf16[224,2048]{1,0:T(8,128)(2,1)} %bitcast.84), channel_id=1, source_target_pairs={{0,16},{16,0},{32,48},{48,32},{64,80},{80,64},{96,112},{112,96},{1... | collective-permute-start | bytes 2752520 | tf_op jit(solution)/shard_map/ppermute | solution.py:39
  29.1 5.8 %all-to-all-done = bf16[16,8,512]{2,1,0:T(8,128)(2,1)S(1)} async-done(((bf16[16,8,512]{2,1,0:T(8,128)(2,1)}), bf16[16,8,512]{2,1,0:T(8,128)(2,1)S(1)}, u32[]{:S(2)}, u32[]{:S(2)}) %all-to-all-start) | async-done | bytes 131104 | tf_op jit(solution)/shard_map/all_to_all | solution.py:26
  34.9 0.3 shard_map.124
  35.2 0.0 collective-permute-done.3.up_pair
  35.2 0.9 copy-done.3
  36.1 0.3 copy-done.4
  36.4 3.1 %shard_map.125 = bf16[16,208,128]{2,1,0:T(8,128)(2,1)} custom-call(bf16[96,224]{1,0:T(8,128)(2,1)S(1)} %get-tuple-element.18.own_ref, bf16[96,224]{1,0:T(8,128)(2,1)S(1)} %get-tuple-element.19.pair_ref, bf16[16,128]{1,0:T(8,128)(2,1)S(1)} %get-tuple-element.20.square_ref, bf16[224,2048]{1,0:T(8,128)(2,1)S(1)} %bitcast.83, ...), custom_call_target="tpu_custom_call" | custom-call | tf_op jit(solution)/shard_map/pallas_call | solution.py:56
  39.5 6.9 %all-to-all-start.1 = ((bf16[16,208,128]{2,1,0:T(8,128)(2,1)}), bf16[16,208,128]{2,1,0:T(8,128)(2,1)S(1)}, u32[]{:S(2)}, u32[]{:S(2)}) async-start(bf16[16,208,128]{2,1,0:T(8,128)(2,1)} %shard_map.125), calls=%async_computation.1 | async-start | bytes 1703936 | tf_op jit(solution)/shard_map/all_to_all | solution.py:32
  46.4 4.1 %collective-permute-start.4 = (bf16[224,2048]{1,0:T(8,128)(2,1)S(1)}, bf16[224,2048]{1,0:T(8,128)(2,1)S(1)}, u32[]{:S(2)}, u32[]{:S(2)}) collective-permute-start(bf16[224,2048]{1,0:T(8,128)(2,1)S(1)} %bitcast.91), channel_id=1, source_target_pairs={{0,16},{16,0},{32,48},{48,32},{64,80},{80,64},{96,112},{112,96},{1... | collective-permute-start | bytes 2752520 | tf_op jit(solution)/shard_map/ppermute | solution.py:39
  50.5 9.0 %all-to-all-done.1.refs_0_ = bf16[16,208,128]{2,1,0:T(8,128)(2,1)S(1)} async-done(((bf16[16,208,128]{2,1,0:T(8,128)(2,1)}), bf16[16,208,128]{2,1,0:T(8,128)(2,1)S(1)}, u32[]{:S(2)}, u32[]{:S(2)}) %all-to-all-start.1) | async-done | bytes 852000 | tf_op jit(solution)/shard_map/all_to_all | solution.py:32
  59.5 0.1 shard_map.126
  59.6 11.6 %all_to_all.35 = bf16[16,96,128]{2,1,0:T(8,128)(2,1)S(1)} all-to-all(bf16[16,96,128]{2,1,0:T(8,128)(2,1)S(1)} %shard_map.126), channel_id=1, replica_groups={{0,32,64,96,128,160,192,224,256,288,320,352,384,416,448,480},{16,48,80,..., dimensions={0} | all-to-all | bytes 786432 | tf_op jit(solution)/shard_map/all_to_all | solution.py:32
  71.2 0.4 convolution_convert_fusion.1
  71.6 0.4 convolution_convert_fusion
  72.1 0.0 copy-start.5
  72.1 0.7 pad.13
  72.8 9.1 %all-to-all-start.3 = ((bf16[16,8,512]{2,1,0:T(8,128)(2,1)}), bf16[16,8,512]{2,1,0:T(8,128)(2,1)S(1)}, u32[]{:S(2)}, u32[]{:S(2)}) async-start(bf16[16,8,512]{2,1,0:T(8,128)(2,1)} %pad.13), calls=%async_computation.3 | async-start | bytes 262144 | tf_op jit(solution)/shard_map/all_to_all | solution.py:26
  81.9 4.3 %collective-permute-start.5 = (bf16[224,512]{1,0:T(8,128)(2,1)S(1)}, bf16[224,512]{1,0:T(8,128)(2,1)S(1)}, u32[]{:S(2)}, u32[]{:S(2)}) collective-permute-start(bf16[224,512]{1,0:T(8,128)(2,1)S(1)} %copy-done.5), channel_id=1, source_target_pairs={{0,16},{16,0},{32,48},{48,32},{64,80},{80,64},{96,112},{112,96},{1... | collective-permute-start | bytes 688136 | tf_op jit(solution)/shard_map/ppermute | solution.py:39
  86.2 1.1 collective-permute-done.5.pair_ref
  87.3 6.6 %all-to-all-done.3 = bf16[16,8,512]{2,1,0:T(8,128)(2,1)S(1)} async-done(((bf16[16,8,512]{2,1,0:T(8,128)(2,1)}), bf16[16,8,512]{2,1,0:T(8,128)(2,1)S(1)}, u32[]{:S(2)}, u32[]{:S(2)}) %all-to-all-start.3) | async-done | bytes 131104 | tf_op jit(solution)/shard_map/all_to_all | solution.py:26
  93.9 1.4 shard_map.127
  95.3 7.5 %all-to-all-start.4 = ((bf16[32,8,512]{2,1,0:T(8,128)(2,1)}), bf16[32,8,512]{2,1,0:T(8,128)(2,1)S(1)}, u32[]{:S(2)}, u32[]{:S(2)}) async-start(bf16[32,8,512]{2,1,0:T(8,128)(2,1)} %bitcast.10), calls=%async_computation.4 | async-start | bytes 524288 | tf_op jit(solution)/shard_map/all_to_all | solution.py:26
  102.9 0.7 copy-done.7
  103.6 1.3 reshape.345
  104.9 0.3 constant_dynamic-slice_fusion.1
  105.2 2.1 %collective-permute-start.6 = (bf16[128,256]{1,0:T(8,128)(2,1)S(1)}, bf16[128,256]{1,0:T(8,128)(2,1)S(1)}, u32[]{:S(2)}, u32[]{:S(2)}) collective-permute-start(bf16[128,256]{1,0:T(8,128)(2,1)S(1)} %slice.40), channel_id=1, source_target_pairs={{0,16},{16,0},{32,48},{48,32},{64,80},{80,64},{96,112},{112,96},{1... | collective-permute-start | bytes 196616 | tf_op jit(solution)/shard_map/ppermute | solution.py:39
  107.4 4.3 %all-to-all-done.4 = bf16[32,8,512]{2,1,0:T(8,128)(2,1)S(1)} async-done(((bf16[32,8,512]{2,1,0:T(8,128)(2,1)}), bf16[32,8,512]{2,1,0:T(8,128)(2,1)S(1)}, u32[]{:S(2)}, u32[]{:S(2)}) %all-to-all-start.4) | async-done | bytes 262176 | tf_op jit(solution)/shard_map/all_to_all | solution.py:26
  111.8 0.1 multiply_reduce_fusion
  111.9 0.5 copy-done.8
  112.4 0.1 multiply_convert_fusion
  112.5 0.7 broadcast_in_dim.86
  113.2 3.5 %all-to-all-start.5 = ((bf16[16,8,512]{2,1,0:T(8,128)(2,1)}), bf16[16,8,512]{2,1,0:T(8,128)(2,1)S(1)}, u32[]{:S(2)}, u32[]{:S(2)}) async-start(bf16[16,8,512]{2,1,0:T(8,128)(2,1)} %broadcast_in_dim.86), calls=%async_computation.5 | async-start | bytes 262144 | tf_op jit(solution)/shard_map/all_to_all | solution.py:26
  116.7 0.2 copy.85
  116.9 0.2 copy.84
  117.0 0.2 copy.86
  117.3 11.4 %all-to-all-done.5 = bf16[16,8,512]{2,1,0:T(8,128)(2,1)S(1)} async-done(((bf16[16,8,512]{2,1,0:T(8,128)(2,1)}), bf16[16,8,512]{2,1,0:T(8,128)(2,1)S(1)}, u32[]{:S(2)}, u32[]{:S(2)}) %all-to-all-start.5) | async-done | bytes 131104 | tf_op jit(solution)/shard_map/all_to_all | solution.py:26
  128.8 0.8 pad_maximum_fusion
  129.6 3.6 %all-to-all-start.6 = ((bf16[16,32,512]{2,1,0:T(8,128)(2,1)}), bf16[16,32,512]{2,1,0:T(8,128)(2,1)S(1)}, u32[]{:S(2)}, u32[]{:S(2)}) async-start(bf16[16,32,512]{2,1,0:T(8,128)(2,1)} %pad_maximum_fusion), calls=%async_computation.6 | async-start | bytes 1048576 | tf_op jit(solution)/shard_map/all_to_all | solution.py:32
  133.3 0.2 copy.74
  133.5 0.1 le.74
  133.6 0.1 le.77
  133.7 0.1 le.80
  133.8 0.1 le.70
  133.9 8.3 %all-to-all-done.6 = bf16[16,32,512]{2,1,0:T(8,128)(2,1)S(1)} async-done(((bf16[16,32,512]{2,1,0:T(8,128)(2,1)}), bf16[16,32,512]{2,1,0:T(8,128)(2,1)S(1)}, u32[]{:S(2)}, u32[]{:S(2)}) %all-to-all-start.6) | async-done | bytes 524320 | tf_op jit(solution)/shard_map/all_to_all | solution.py:32
  142.3 5.9 %collective-permute-start.7 = (bf16[512,512]{1,0:T(8,128)(2,1)S(1)}, bf16[512,512]{1,0:T(8,128)(2,1)S(1)}, u32[]{:S(2)}, u32[]{:S(2)}) collective-permute-start(bf16[512,512]{1,0:T(8,128)(2,1)S(1)} %bitcast.87), channel_id=1, source_target_pairs={{0,16},{16,0},{32,48},{48,32},{64,80},{80,64},{96,112},{112,96},{1... | collective-permute-start | bytes 1572872 | tf_op jit(solution)/shard_map/ppermute | solution.py:39
  148.2 0.3 compare_and_fusion
  148.6 1.0 shard_map.128
  149.5 0.5 fusion.38
  150.0 0.2 fusion.7
  150.2 0.5 fusion.39
  150.8 0.2 fusion.9
  151.0 0.5 convolution_multiply_fusion.1
  151.5 0.5 fusion.6
  152.0 1.2 copy.80
  (43 shorter events, 0.4 us)
Async XLA Ops:
  0.6 148.9 %copy-start = (bf16[128,4,512]{2,1,0:T(4,128)(2,1)S(1)}, bf16[128,4,512]{2,1,0:T(4,128)(2,1)}, u32[]{:S(2)}) copy-start(bf16[128,4,512]{2,1,0:T(4,128)(2,1)} %param.20) | copy-start | bytes 1572868
  0.6 11.3 %copy-start.1 = (bf16[8,32,224]{2,1,0:T(8,128)(2,1)S(1)}, bf16[8,32,224]{2,1,0:T(8,128)(2,1)}, u32[]{:S(2)}) copy-start(bf16[8,32,224]{2,1,0:T(8,128)(2,1)} %param.11) | copy-start | bytes 344068
  0.7 11.3 %collective-permute-start = (bf16[256,224]{1,0:T(8,128)(2,1)}, bf16[256,224]{1,0:T(8,128)(2,1)S(1)}, u32[]{:S(2)}, u32[]{:S(2)}) collective-permute-start(bf16[256,224]{1,0:T(8,128)(2,1)} %bitcast.78), channel_id=1, source_target_pairs={{0,16},{16,0},{32,48},{48,32},{64,80},{80,64},{96,112},{112,96},{1... | collective-permute-start | bytes 344072 | tf_op jit(solution)/shard_map/ppermute | solution.py:39
  12.8 9.7 %copy-start.9 = (f32[224]{0:T(256)S(1)}, f32[224]{0:T(256)}, u32[]{:S(2)}) copy-start(f32[224]{0:T(256)} %param.14) | copy-start | bytes 2692
  12.8 22.1 %all-to-all-start = ((bf16[16,8,512]{2,1,0:T(8,128)(2,1)}), bf16[16,8,512]{2,1,0:T(8,128)(2,1)S(1)}, u32[]{:S(2)}, u32[]{:S(2)}) async-start(bf16[16,8,512]{2,1,0:T(8,128)(2,1)} %bitcast.6), calls=%async_computation | async-start | bytes 262144 | tf_op jit(solution)/shard_map/all_to_all | solution.py:26
  22.5 6.6 %collective-permute-start.1 = (f32[8,224]{1,0:T(8,128)S(1)}, f32[8,224]{1,0:T(8,128)S(1)}, u32[]{:S(2)}, u32[]{:S(2)}) collective-permute-start(f32[8,224]{1,0:T(8,128)S(1)} %broadcast_in_dim.82.refs_1_), channel_id=1, source_target_pairs={{0,16},{16,0},{32,48},{48,32},{64,80},{80,64},{96,112},{112,96},{1... | collective-permute-start | bytes 21512 | tf_op jit(solution)/shard_map/ppermute | solution.py:39
  24.7 10.5 %collective-permute-start.2 = (bf16[224,2048]{1,0:T(8,128)(2,1)}, bf16[224,2048]{1,0:T(8,128)(2,1)}, u32[]{:S(2)}, u32[]{:S(2)}) collective-permute-start(bf16[224,2048]{1,0:T(8,128)(2,1)} %bitcast.82), channel_id=1, source_target_pairs={{0,16},{16,0},{32,48},{48,32},{64,80},{80,64},{96,112},{112,96},{1... | collective-permute-start | bytes 2752520 | tf_op jit(solution)/shard_map/ppermute | solution.py:39
  26.8 8.4 %collective-permute-start.3 = (bf16[224,2048]{1,0:T(8,128)(2,1)}, bf16[224,2048]{1,0:T(8,128)(2,1)}, u32[]{:S(2)}, u32[]{:S(2)}) collective-permute-start(bf16[224,2048]{1,0:T(8,128)(2,1)} %bitcast.84), channel_id=1, source_target_pairs={{0,16},{16,0},{32,48},{48,32},{64,80},{80,64},{96,112},{112,96},{1... | collective-permute-start | bytes 2752520 | tf_op jit(solution)/shard_map/ppermute | solution.py:39
  34.9 1.2 copy-start.3
  34.9 1.5 copy-start.4
  39.5 6.9 %copy-start.6 = (bf16[1,2048,224]{1,2,0:T(8,128)(2,1)S(1)}, bf16[1,2048,224]{1,2,0:T(8,128)(2,1)}, u32[]{:S(2)}) copy-start(bf16[1,2048,224]{1,2,0:T(8,128)(2,1)} %param.17) | copy-start | bytes 2752516
  39.5 19.9 %all-to-all-start.1 = ((bf16[16,208,128]{2,1,0:T(8,128)(2,1)}), bf16[16,208,128]{2,1,0:T(8,128)(2,1)S(1)}, u32[]{:S(2)}, u32[]{:S(2)}) async-start(bf16[16,208,128]{2,1,0:T(8,128)(2,1)} %shard_map.125), calls=%async_computation.1 | async-start | bytes 1703936 | tf_op jit(solution)/shard_map/all_to_all | solution.py:32
  46.4 25.2 %collective-permute-start.4 = (bf16[224,2048]{1,0:T(8,128)(2,1)S(1)}, bf16[224,2048]{1,0:T(8,128)(2,1)S(1)}, u32[]{:S(2)}, u32[]{:S(2)}) collective-permute-start(bf16[224,2048]{1,0:T(8,128)(2,1)S(1)} %bitcast.91), channel_id=1, source_target_pairs={{0,16},{16,0},{32,48},{48,32},{64,80},{80,64},{96,112},{112,96},{1... | collective-permute-start | bytes 2752520 | tf_op jit(solution)/shard_map/ppermute | solution.py:39
  72.1 9.8 %copy-start.5 = (bf16[224,512]{1,0:T(8,128)(2,1)S(1)}, bf16[224,512]{1,0:T(8,128)(2,1)}, u32[]{:S(2)}) copy-start(bf16[224,512]{1,0:T(8,128)(2,1)} %own_ref.1) | copy-start | bytes 688132
  72.8 21.1 %copy-start.2 = (bf16[8,32,224]{2,1,0:T(8,128)(2,1)S(1)}, bf16[8,32,224]{2,1,0:T(8,128)(2,1)}, u32[]{:S(2)}) copy-start(bf16[8,32,224]{2,1,0:T(8,128)(2,1)} %param.11) | copy-start | bytes 344068
  72.8 21.1 %all-to-all-start.3 = ((bf16[16,8,512]{2,1,0:T(8,128)(2,1)}), bf16[16,8,512]{2,1,0:T(8,128)(2,1)S(1)}, u32[]{:S(2)}, u32[]{:S(2)}) async-start(bf16[16,8,512]{2,1,0:T(8,128)(2,1)} %pad.13), calls=%async_computation.3 | async-start | bytes 262144 | tf_op jit(solution)/shard_map/all_to_all | solution.py:26
  81.9 5.4 %collective-permute-start.5 = (bf16[224,512]{1,0:T(8,128)(2,1)S(1)}, bf16[224,512]{1,0:T(8,128)(2,1)S(1)}, u32[]{:S(2)}, u32[]{:S(2)}) collective-permute-start(bf16[224,512]{1,0:T(8,128)(2,1)S(1)} %copy-done.5), channel_id=1, source_target_pairs={{0,16},{16,0},{32,48},{48,32},{64,80},{80,64},{96,112},{112,96},{1... | collective-permute-start | bytes 688136 | tf_op jit(solution)/shard_map/ppermute | solution.py:39
  95.3 16.4 %all-to-all-start.4 = ((bf16[32,8,512]{2,1,0:T(8,128)(2,1)}), bf16[32,8,512]{2,1,0:T(8,128)(2,1)S(1)}, u32[]{:S(2)}, u32[]{:S(2)}) async-start(bf16[32,8,512]{2,1,0:T(8,128)(2,1)} %bitcast.10), calls=%async_computation.4 | async-start | bytes 524288 | tf_op jit(solution)/shard_map/all_to_all | solution.py:26
  102.8 0.7 copy-start.7
  105.2 7.3 %collective-permute-start.6 = (bf16[128,256]{1,0:T(8,128)(2,1)S(1)}, bf16[128,256]{1,0:T(8,128)(2,1)S(1)}, u32[]{:S(2)}, u32[]{:S(2)}) collective-permute-start(bf16[128,256]{1,0:T(8,128)(2,1)S(1)} %slice.40), channel_id=1, source_target_pairs={{0,16},{16,0},{32,48},{48,32},{64,80},{80,64},{96,112},{112,96},{1... | collective-permute-start | bytes 196616 | tf_op jit(solution)/shard_map/ppermute | solution.py:39
  111.7 0.7 copy-start.8
  113.2 15.5 %all-to-all-start.5 = ((bf16[16,8,512]{2,1,0:T(8,128)(2,1)}), bf16[16,8,512]{2,1,0:T(8,128)(2,1)S(1)}, u32[]{:S(2)}, u32[]{:S(2)}) async-start(bf16[16,8,512]{2,1,0:T(8,128)(2,1)} %broadcast_in_dim.86), calls=%async_computation.5 | async-start | bytes 262144 | tf_op jit(solution)/shard_map/all_to_all | solution.py:26
  129.6 12.6 %all-to-all-start.6 = ((bf16[16,32,512]{2,1,0:T(8,128)(2,1)}), bf16[16,32,512]{2,1,0:T(8,128)(2,1)S(1)}, u32[]{:S(2)}, u32[]{:S(2)}) async-start(bf16[16,32,512]{2,1,0:T(8,128)(2,1)} %pad_maximum_fusion), calls=%async_computation.6 | async-start | bytes 1048576 | tf_op jit(solution)/shard_map/all_to_all | solution.py:32
  142.3 8.0 %collective-permute-start.7 = (bf16[512,512]{1,0:T(8,128)(2,1)S(1)}, bf16[512,512]{1,0:T(8,128)(2,1)S(1)}, u32[]{:S(2)}, u32[]{:S(2)}) collective-permute-start(bf16[512,512]{1,0:T(8,128)(2,1)S(1)} %bitcast.87), channel_id=1, source_target_pairs={{0,16},{16,0},{32,48},{48,32},{64,80},{80,64},{96,112},{112,96},{1... | collective-permute-start | bytes 1572872 | tf_op jit(solution)/shard_map/ppermute | solution.py:39

commit v3 on v2

--- a/solution.py
+++ b/solution.py
@@ -13,7 +13,7 @@
 WIDE = 256
 GROUPS = 8
 BLOCK = 4
-COST = 400_000_000_000
+COST = 5_000_000_000
 
 
 score_scale = 192 ** (-0.5)
@@ -63,18 +63,24 @@
     )(*operands)
 
 
-def routing_kernel(core_ref, expert_ref, gate_ref, placed_ref, table_ref):
-    core = core_ref[0]
-    group, run = expert_ref.shape
+def column(values):
+    group, run = values.shape
     tokens = group * run
     spread = (iota((tokens, group), 0) // run == iota((tokens, group), 1)).astype(f32)
     inside = iota((tokens, run), 0) % run == iota((tokens, run), 1)
-
-    def column(values):
-        values = jnp.dot(spread, values, preferred_element_type=f32, precision=lax.Precision.HIGHEST)
-        return jnp.sum(jnp.where(inside, values, 0.0), axis=1, keepdims=True)
-
-    expert, gate = column(expert_ref[...]), column(gate_ref[...])
+    values = jnp.dot(spread, values, preferred_element_type=f32, precision=lax.Precision.HIGHEST)
+    return jnp.sum(jnp.where(inside, values, 0.0), axis=1, keepdims=True)
+
+
+def gate_kernel(gate_ref, gain_ref, out_ref, gains_ref):
+    out_ref[...] = jnp.broadcast_to(column(gate_ref[...]), out_ref.shape)
+    gains_ref[...] = jnp.broadcast_to(gain_ref[...], gains_ref.shape)
+
+
+def routing_kernel(core_ref, expert_ref, placed_ref, table_ref):
+    core = core_ref[0]
+    expert = column(expert_ref[...])
+    tokens = expert.shape[0]
     lane = iota((tokens, 128), 1).astype(f32)
     picked = expert == lane
     earlier = (iota((tokens, tokens), 1) < iota((tokens, tokens), 0)).astype(bf16)
@@ -90,7 +96,7 @@
     padded = placed_ref.shape[0]
     slot_rows = jnp.transpose(jnp.broadcast_to(slot, (tokens, padded)))
     placed_ref[...] = (slot_rows == iota((padded, tokens), 0).astype(f32)).astype(bf16)
-    table_ref[...] = jnp.where(lane == 0, slot, jnp.where(lane == 1, slot_in(1 - core), gate))
+    table_ref[...] = jnp.where(lane == 0, slot, slot_in(1 - core))
 
 
 def dispatch_kernel(placed_ref, own_ref, pair_ref, out_ref):
@@ -149,10 +155,10 @@
         out_ref[owner] = units
 
 
-def combine_kernel(returned_ref, table_ref, rows_ref, own_ref, pair_ref, out_ref):
+def combine_kernel(returned_ref, table_ref, gate_ref, rows_ref, own_ref, pair_ref, out_ref):
     tokens, width = rows_ref.shape
     padded = returned_ref.shape[0]
-    slot, gate = table_ref[:, 0:1], table_ref[:, 2:3]
+    slot, gate = table_ref[:, 0:1], gate_ref[:, 0:1]
     choice = (slot == iota((tokens, padded), 1).astype(f32)).astype(bf16)
     moe = dot(choice, returned_ref[...]) * gate
     next_own = (rows_ref[...].astype(f32) + moe[:, :width]).astype(bf16)
@@ -167,13 +173,58 @@
     out_ref[...] = (dot(own, own_ref[...]) + dot(pair, pair_ref[...])).astype(bf16)
 
 
-def next_kernel(returned_ref, rest_ref, table_ref, rows_ref, out_ref):
+def latent_kernel(part_ref, gain_ref, out_ref):
+    raw = jnp.sum(part_ref[...].astype(f32), axis=0)
+    scale = lax.rsqrt(jnp.mean(raw * raw, axis=1, keepdims=True) + norm_eps)
+    latent = (raw * scale * gain_ref[...]).astype(bf16)
+    for plane in range(out_ref.shape[0]):
+        out_ref[plane] = latent
+
+
+def key_kernel(plane_ref, out_ref):
+    chips, rows, _ = out_ref.shape
+    planes = rows // 2
+    total = plane_ref.shape[0]
+    target, source = iota((total, total), 0), iota((total, total), 1)
+    order = (source == target % planes * GROUPS + target // planes).astype(bf16)
+    ordered = dot(order, plane_ref[...]).astype(bf16)
+    for chip in range(chips):
+        run = chip // (BLOCK // 2)
+        out_ref[chip, :planes] = ordered[:planes]
+        out_ref[chip, planes:] = ordered[run * planes : (run + 1) * planes]
+
+
+def next_kernel(returned_ref, rest_ref, table_ref, gate_ref, rows_ref, out_ref):
     tokens, width = rows_ref.shape
     padded = returned_ref.shape[0]
     lane = iota((tokens, padded), 1).astype(f32)
     moe = dot((table_ref[:, 0:1] == lane).astype(bf16), returned_ref[:, :width])
     moe += dot((table_ref[:, 1:2] == lane).astype(bf16), rest_ref[:, :width])
-    out_ref[...] = (rows_ref[...].astype(f32) + moe * table_ref[:, 2:3]).astype(bf16)
+    out_ref[...] = (rows_ref[...].astype(f32) + moe * gate_ref[:, 0:1]).astype(bf16)
+
+
+def attend(queries_ref, keys_ref, seen_ref):
+    keys = keys_ref[...]
+    seen = jnp.concatenate([seen_ref[...]] * (queries_ref.shape[0] // seen_ref.shape[0]), axis=0) > 0
+    scores = jnp.where(seen, dot_last(queries_ref[...], keys) * score_scale, neg_fill)
+    top = jnp.max(scores, axis=1, keepdims=True)
+    weights = jnp.where(seen, jnp.exp(scores - top), 0.0)
+    return top, jnp.sum(weights, axis=1, keepdims=True), dot(weights.astype(bf16), keys)
+
+
+def first_kernel(queries_ref, keys_ref, seen_ref, stats_ref, mixed_ref):
+    top, denom, mixed = attend(queries_ref, keys_ref, seen_ref)
+    stats_ref[...] = jnp.where(iota(stats_ref.shape, 1) == 0, top, denom)
+    mixed_ref[...] = mixed
+
+
+def second_kernel(queries_ref, keys_ref, seen_ref, stats_ref, mixed_ref, out_ref):
+    top, denom, mixed = attend(queries_ref, keys_ref, seen_ref)
+    first_top, first_denom = stats_ref[:, 0:1], stats_ref[:, 1:2]
+    most = jnp.maximum(top, first_top)
+    share, first_share = jnp.exp(top - most), jnp.exp(first_top - most)
+    total = denom * share + first_denom * first_share
+    out_ref[...] = (mixed * (share / total) + mixed_ref[...] * (first_share / total)).astype(bf16)
 
 
 def body(
@@ -203,26 +254,29 @@
     rows = hidden.reshape(tokens, width)
     rows_pair = swap(rows)
     core = lax.rem(lax.axis_index("ctx"), 2)
+
     shape = jax.ShapeDtypeStruct
     near = routes < exp_count
     expert = jnp.max(jnp.where(near, routes, -1), axis=2).astype(f32)
-    gate = jnp.sum(jnp.where(near, gates, 0.0), axis=2)
     placed, table = local_kernel(
         routing_kernel,
         (shape((padded, tokens), bf16), shape((tokens, 128), f32)),
         core.reshape(1),
         expert,
-        gate,
-        spaces=[pltpu.SMEM] + [pltpu.VMEM] * 2,
+        spaces=[pltpu.SMEM, pltpu.VMEM],
     )
     wide = shape((padded, 2 * WIDE), bf16)
     dispatched = local_kernel(dispatch_kernel, wide, placed, rows, rows_pair)
-    own = (moe_gain, gate_weight[0], up_weight[0], down_weight[0].T, latent_weight)
-    dispatched, own = lax.optimization_barrier((dispatched, own))
-    gain_own = jnp.broadcast_to(own[0][None, :], (8, width))
-    down_own = own[3]
-    gain_pair, gate_pair, up_pair, down_pair, latent_pair = [swap(value) for value in (gain_own,) + own[1:]]
-    gate_own, up_own = own[1], own[2]
+    own = (gate_weight[0], up_weight[0], down_weight[0].T, latent_weight, moe_gain)
+    late = (gates, latent_gain)
+    dispatched, own, late = lax.optimization_barrier((dispatched, own, late))
+    gate = jnp.sum(jnp.where(near, late[0], 0.0), axis=2)
+    gate, latent_gains = local_kernel(
+        gate_kernel, (shape((tokens, 128), f32), shape((8, latent_width), f32)), gate, late[1][None, :]
+    )
+    gate_own, up_own, down_own, _, gain_own = own
+    gain_own = jnp.broadcast_to(gain_own[None, :], (8, width))
+    gate_pair, up_pair, down_pair, latent_pair, gain_pair = [swap(value) for value in own[:4] + (gain_own,)]
     received = exchange(dispatched.reshape(exp_count, PAD, 2 * WIDE), "exp").reshape(padded, 2 * WIDE)
 
     packed = local_kernel(
@@ -258,26 +312,26 @@
         jax.ShapeDtypeStruct((tokens, latent_width), bf16),
         returned,
         table,
+        gate,
         rows,
         latent_weight,
         latent_pair,
     )
     latent_part = exchange(latent_part.reshape(ctx_count, GROUPS, latent_width), "ctx")
-    latent_raw = jnp.sum(latent_part.astype(f32), axis=0)
-    latent_rms = lax.rsqrt(jnp.mean(latent_raw * latent_raw, axis=1, keepdims=True) + norm_eps)
-    latent = (latent_raw * latent_rms * latent_gain[None, :]).astype(bf16)
+    latent = local_kernel(
+        latent_kernel, shape((exp_count, GROUPS, latent_width), bf16), latent_part, latent_gains
+    )
     latent, returned_rest = lax.optimization_barrier((latent, returned_rest))
-    plane = exchange(jnp.broadcast_to(latent[None], (exp_count,) + latent.shape), "exp")
-    plane = plane.transpose(1, 0, 2)
-    own = jnp.repeat(plane, BLOCK // 2, axis=0)
-    prompt = jnp.broadcast_to(plane[:1], own.shape)
-    keys = exchange_chips(jnp.concatenate([prompt, own], axis=1))
-    keys = keys.reshape(chips * 2 * exp_count, latent_width)
-    all_keys = (keys, swap(keys))
-
+    plane = exchange(latent, "exp").reshape(exp_count * GROUPS, latent_width)
     next_rows = local_kernel(
-        next_kernel, jax.ShapeDtypeStruct(rows.shape, bf16), returned, returned_rest, table, rows
-    )
+        next_kernel, shape(rows.shape, bf16), returned, returned_rest, table, gate, rows
+    )
+    local, heads = queries.shape[:2]
+    queries = queries.transpose(1, 0, 2).reshape(heads * local, latent_width)
+    chunks = local_kernel(key_kernel, shape((chips, 2 * exp_count, latent_width), bf16), plane)
+    chunks, next_rows, queries = lax.optimization_barrier((chunks, next_rows, queries))
+    keys = exchange_chips(chunks).reshape(chips * 2 * exp_count, latent_width)
+    keys_pair = swap(keys)
 
     shard_index = lax.axis_index("ctx")
     group = shard_index // BLOCK
@@ -291,26 +345,31 @@
         both = jnp.stack([table[0], own_table])
         return both.transpose(1, 3, 0, 2).reshape(-1)
 
-    local, heads = queries.shape[:2]
     query_index = shard_index * local + jnp.arange(local, dtype=jnp.int32)
 
-    def attended(part_keys, part):
+    def visible(part):
         key_end, key_index = key_order(ends, -1, part), key_order(positions, 0, part)
-        visible = (key_index[None, :] <= query_index[:, None]) & (query_index[:, None] <= key_end[None, :])
-        visible = visible[:, None, :]
-        scores = jnp.einsum("qhl,kl->qhk", queries, part_keys, preferred_element_type=f32) * score_scale
-        scores = jnp.where(visible, scores, neg_fill)
-        top = jnp.max(scores, axis=2)
-        exp_scores = jnp.where(visible, jnp.exp(scores - top[:, :, None]), 0.0)
-        mixed = jnp.einsum("qhk,kl->qhl", exp_scores.astype(bf16), part_keys, preferred_element_type=f32)
-        return top, jnp.sum(exp_scores, axis=2), mixed
-
-    parts = [attended(part_keys, part) for part_keys, part in zip(all_keys, (core, 1 - core))]
-    top = jnp.maximum(parts[0][0], parts[1][0])
-    shares = [jnp.exp(part[0] - top) for part in parts]
-    denom = sum(share * part[1] for share, part in zip(shares, parts))
-    mixed = sum(share[:, :, None] * part[2] for share, part in zip(shares, parts))
-    attn_out = (mixed / denom[:, :, None]).astype(bf16)
+        seen = (key_index[None, :] <= query_index[:, None]) & (query_index[:, None] <= key_end[None, :])
+        return seen.astype(f32)
+
+    first = local_kernel(
+        first_kernel,
+        (shape((heads * local, 128), f32), shape((heads * local, latent_width), f32)),
+        queries,
+        keys,
+        visible(core),
+        grant=16,
+    )
+    attn_out = local_kernel(
+        second_kernel,
+        shape((heads * local, latent_width), bf16),
+        queries,
+        keys_pair,
+        visible(1 - core),
+        *first,
+        grant=16,
+    )
+    attn_out = attn_out.reshape(heads, local, latent_width).transpose(1, 0, 2)
     return (next_rows.reshape(hidden.shape), attn_out)
 
 

time: 154 us -> 152 us (0.987)
  Pallas kernels: 7.48 us -> 10.8 us
  other arithmetic: 3.52 us -> 1.05 us
  matrix products: 2.85 us -> 0.85 us
    pallas_call x7 -> x12, Pallas kernels: 7.48 us -> 10.8 us  [local_kernel(): pl.pallas_call(kernel, out_shape=out_shape, in_specs=[pl.BlockSpec(memory...]
    dot_general x4 -> x0, matrix products: 2 us -> none  [the longest x2 1 us: attended(): jnp.einsum('qhl,kl->qhk', queries, part_keys, preferred_element_type=f32)]
    all_to_all x4, waiting for transfers between devices: 28.2 us -> 26.5 us  [exchange(): return lax.all_to_all(chunks, axis, split_axis=0, concat_axis=0, tiled=True)]
    unnamed x24 -> x27, local copies, waits for them, and re-layouts: 4.08 us -> 3.79 us
  transfers between devices with their start and end apart: 14 -> 14, of which waited for: 7 -> 8; matrix products, arithmetic and copies ran while one was open for 4% -> 3% of each run, Pallas kernels for 1% -> 3%
where the time goes in v3:
time: 152 us; the launch traced here: 151 us
  starting transfers between devices  71.5 us (47%)
  waiting for transfers between devices  45.7 us (30%)
  blocking collectives  11.5 us (8%)
  Pallas kernels  10.8 us (7%)
  local copies, waits for them, and re-layouts  8.01 us (5%)
    ppermute x8, starting transfers between devices, swap(): return lax.ppermute(value, 'ctx', [(i, i ^ 1) for i in range(count)])  31 us
    all_to_all x4, starting transfers between devices, exchange(): return lax.all_to_all(chunks, axis, split_axis=0, concat_axis=0, tiled=True)  30.1 us
    all_to_all x4, waiting for transfers between devices, exchange(): return lax.all_to_all(chunks, axis, split_axis=0, concat_axis=0, tiled=True)  26.5 us
    all_to_all x2, waiting for transfers between devices, exchange_chips(): lax.all_to_all(chunks, 'ctx', split_axis=0, concat_axis=0, tiled=True, ax...  17.6 us
    all_to_all x1, blocking collectives, exchange_chips(): lax.all_to_all(chunks, 'ctx', split_axis=0, concat_axis=0, tiled=True, ax...  11.5 us
    pallas_call x12, Pallas kernels, local_kernel(): pl.pallas_call(kernel, out_shape=out_shape, in_specs=[pl.BlockSpec(memory...  10.8 us
    all_to_all x2, starting transfers between devices, exchange_chips(): lax.all_to_all(chunks, 'ctx', split_axis=0, concat_axis=0, tiled=True, ax...  10.5 us
    unnamed x27, local copies, waits for them, and re-layouts  3.79 us
  transfers between devices with their start and end apart: 14, of which 8 were waited for; matrix products, arithmetic and copies ran while one was open for 3% of the time, Pallas kernels for 3%

profile of v3, /device:TPU:1, one launch (start us, length us, event | category | flops | bytes accessed | tf_op | source)
XLA Modules:
  0.0 150.6 jit_solution(6614665682338100834)
XLA Ops:
  0.6 8.8 %collective-permute-start = (bf16[256,224]{1,0:T(8,128)(2,1)}, bf16[256,224]{1,0:T(8,128)(2,1)S(1)}, u32[]{:S(2)}, u32[]{:S(2)}) collective-permute-start(bf16[256,224]{1,0:T(8,128)(2,1)} %bitcast.66), channel_id=1, source_target_pairs={{0,16},{16,0},{32,48},{48,32},{64,80},{80,64},{96,112},{112,96},{1... | collective-permute-start | bytes 344072 | tf_op jit(solution)/shard_map/ppermute | solution.py:39
  9.4 0.8 fusion.7
  10.2 0.7 shard_map.122
  10.9 0.0 copy-start
  10.9 0.9 copy-done
  11.8 0.8 shard_map.123
  12.7 9.7 %all-to-all-start = ((bf16[16,8,512]{2,1,0:T(8,128)(2,1)}), bf16[16,8,512]{2,1,0:T(8,128)(2,1)S(1)}, u32[]{:S(2)}, u32[]{:S(2)}) async-start(bf16[16,8,512]{2,1,0:T(8,128)(2,1)} %bitcast.6), calls=%async_computation | async-start | bytes 262144 | tf_op jit(solution)/shard_map/all_to_all | solution.py:26
  22.4 2.2 %collective-permute-start.2 = (bf16[224,2048]{1,0:T(8,128)(2,1)}, bf16[224,2048]{1,0:T(8,128)(2,1)S(1)}, u32[]{:S(2)}, u32[]{:S(2)}) collective-permute-start(bf16[224,2048]{1,0:T(8,128)(2,1)} %bitcast.70), channel_id=1, source_target_pairs={{0,16},{16,0},{32,48},{48,32},{64,80},{80,64},{96,112},{112,96},{1... | collective-permute-start | bytes 2752520 | tf_op jit(solution)/shard_map/ppermute | solution.py:39
  24.6 2.1 %collective-permute-start.3 = (bf16[224,2048]{1,0:T(8,128)(2,1)}, bf16[224,2048]{1,0:T(8,128)(2,1)S(1)}, u32[]{:S(2)}, u32[]{:S(2)}) collective-permute-start(bf16[224,2048]{1,0:T(8,128)(2,1)} %bitcast.72), channel_id=1, source_target_pairs={{0,16},{16,0},{32,48},{48,32},{64,80},{80,64},{96,112},{112,96},{1... | collective-permute-start | bytes 2752520 | tf_op jit(solution)/shard_map/ppermute | solution.py:39
  26.7 2.2 %collective-permute-start.1 = (f32[8,224]{1,0:T(8,128)S(1)}, f32[8,224]{1,0:T(8,128)S(1)}, u32[]{:S(2)}, u32[]{:S(2)}) collective-permute-start(f32[8,224]{1,0:T(8,128)S(1)} %broadcast_in_dim.31.refs_1_), channel_id=1, source_target_pairs={{0,16},{16,0},{32,48},{48,32},{64,80},{80,64},{96,112},{112,96},{1... | collective-permute-start | bytes 21512 | tf_op jit(solution)/shard_map/ppermute | solution.py:39
  29.0 0.8 collective-permute-done.1.refs_2_
  29.8 4.9 %all-to-all-done = bf16[16,8,512]{2,1,0:T(8,128)(2,1)S(1)} async-done(((bf16[16,8,512]{2,1,0:T(8,128)(2,1)}), bf16[16,8,512]{2,1,0:T(8,128)(2,1)S(1)}, u32[]{:S(2)}, u32[]{:S(2)}) %all-to-all-start) | async-done | bytes 131104 | tf_op jit(solution)/shard_map/all_to_all | solution.py:26
  34.7 0.3 shard_map.124
  35.0 0.0 collective-permute-done.2.gate_pair
  35.0 0.0 collective-permute-done.3.up_pair
  35.0 0.9 copy-done.2
  35.9 0.3 copy-done.3
  36.2 1.7 %shard_map.125 = bf16[16,208,128]{2,1,0:T(8,128)(2,1)} custom-call(bf16[96,224]{1,0:T(8,128)(2,1)S(1)} %get-tuple-element.27.own_ref, bf16[96,224]{1,0:T(8,128)(2,1)S(1)} %get-tuple-element.28.pair_ref, bf16[16,128]{1,0:T(8,128)(2,1)S(1)} %get-tuple-element.29.square_ref, bf16[224,2048]{1,0:T(8,128)(2,1)S(1)} %bitcast.71, ...), custom_call_target="tpu_custom_call" | custom-call | tf_op jit(solution)/shard_map/pallas_call | solution.py:56
  37.8 6.9 %all-to-all-start.1 = ((bf16[16,208,128]{2,1,0:T(8,128)(2,1)}), bf16[16,208,128]{2,1,0:T(8,128)(2,1)S(1)}, u32[]{:S(2)}, u32[]{:S(2)}) async-start(bf16[16,208,128]{2,1,0:T(8,128)(2,1)} %shard_map.125), calls=%async_computation.1 | async-start | bytes 1703936 | tf_op jit(solution)/shard_map/all_to_all | solution.py:32
  44.8 4.1 %collective-permute-start.4 = (bf16[224,2048]{1,0:T(8,128)(2,1)S(1)}, bf16[224,2048]{1,0:T(8,128)(2,1)S(1)}, u32[]{:S(2)}, u32[]{:S(2)}) collective-permute-start(bf16[224,2048]{1,0:T(8,128)(2,1)S(1)} %bitcast.77), channel_id=1, source_target_pairs={{0,16},{16,0},{32,48},{48,32},{64,80},{80,64},{96,112},{112,96},{1... | collective-permute-start | bytes 2752520 | tf_op jit(solution)/shard_map/ppermute | solution.py:39
  48.9 8.8 %all-to-all-done.1.refs_0_ = bf16[16,208,128]{2,1,0:T(8,128)(2,1)S(1)} async-done(((bf16[16,208,128]{2,1,0:T(8,128)(2,1)}), bf16[16,208,128]{2,1,0:T(8,128)(2,1)S(1)}, u32[]{:S(2)}, u32[]{:S(2)}) %all-to-all-start.1) | async-done | bytes 852000 | tf_op jit(solution)/shard_map/all_to_all | solution.py:32
  57.8 0.1 shard_map.126
  57.9 11.5 %all_to_all.35 = bf16[16,96,128]{2,1,0:T(8,128)(2,1)S(1)} all-to-all(bf16[16,96,128]{2,1,0:T(8,128)(2,1)S(1)} %shard_map.126), channel_id=1, replica_groups={{0,32,64,96,128,160,192,224,256,288,320,352,384,416,448,480},{16,48,80,..., dimensions={0} | all-to-all | bytes 786432 | tf_op jit(solution)/shard_map/all_to_all | solution.py:32
  69.4 0.4 convolution_convert_fusion.1
  69.9 0.4 convolution_convert_fusion
  70.4 0.0 copy-start.4
  70.4 0.7 pad.13
  71.1 9.2 %all-to-all-start.3 = ((bf16[16,8,512]{2,1,0:T(8,128)(2,1)}), bf16[16,8,512]{2,1,0:T(8,128)(2,1)S(1)}, u32[]{:S(2)}, u32[]{:S(2)}) async-start(bf16[16,8,512]{2,1,0:T(8,128)(2,1)} %pad.13), calls=%async_computation.3 | async-start | bytes 262144 | tf_op jit(solution)/shard_map/all_to_all | solution.py:26
  80.3 4.2 %collective-permute-start.5 = (bf16[224,512]{1,0:T(8,128)(2,1)S(1)}, bf16[224,512]{1,0:T(8,128)(2,1)S(1)}, u32[]{:S(2)}, u32[]{:S(2)}) collective-permute-start(bf16[224,512]{1,0:T(8,128)(2,1)S(1)} %copy-done.4), channel_id=1, source_target_pairs={{0,16},{16,0},{32,48},{48,32},{64,80},{80,64},{96,112},{112,96},{1... | collective-permute-start | bytes 688136 | tf_op jit(solution)/shard_map/ppermute | solution.py:39
  84.6 0.3 shard_map.127
  84.9 0.7 collective-permute-done.5.pair_ref
  85.6 6.7 %all-to-all-done.3 = bf16[16,8,512]{2,1,0:T(8,128)(2,1)S(1)} async-done(((bf16[16,8,512]{2,1,0:T(8,128)(2,1)}), bf16[16,8,512]{2,1,0:T(8,128)(2,1)S(1)}, u32[]{:S(2)}, u32[]{:S(2)}) %all-to-all-start.3) | async-done | bytes 131104 | tf_op jit(solution)/shard_map/all_to_all | solution.py:26
  92.3 1.4 shard_map.128
  93.7 7.7 %all-to-all-start.4 = ((bf16[32,8,512]{2,1,0:T(8,128)(2,1)}), bf16[32,8,512]{2,1,0:T(8,128)(2,1)S(1)}, u32[]{:S(2)}, u32[]{:S(2)}) async-start(bf16[32,8,512]{2,1,0:T(8,128)(2,1)} %bitcast.11), calls=%async_computation.4 | async-start | bytes 524288 | tf_op jit(solution)/shard_map/all_to_all | solution.py:26
  101.4 2.3 %collective-permute-start.6 = (bf16[128,256]{1,0:T(8,128)(2,1)S(1)}, bf16[128,256]{1,0:T(8,128)(2,1)S(1)}, u32[]{:S(2)}, u32[]{:S(2)}) collective-permute-start(bf16[128,256]{1,0:T(8,128)(2,1)S(1)} %slice.36), channel_id=1, source_target_pairs={{0,16},{16,0},{32,48},{48,32},{64,80},{80,64},{96,112},{112,96},{1... | collective-permute-start | bytes 196616 | tf_op jit(solution)/shard_map/ppermute | solution.py:39
  103.6 6.7 %all-to-all-done.4.part_ref = bf16[32,8,512]{2,1,0:T(8,128)(2,1)S(1)} async-done(((bf16[32,8,512]{2,1,0:T(8,128)(2,1)}), bf16[32,8,512]{2,1,0:T(8,128)(2,1)S(1)}, u32[]{:S(2)}, u32[]{:S(2)}) %all-to-all-start.4) | async-done | bytes 262176 | tf_op jit(solution)/shard_map/all_to_all | solution.py:26
  110.4 0.8 shard_map.129
  111.2 0.0 collective-permute-done.6.rest_ref
  111.2 3.5 %all-to-all-start.5 = ((bf16[16,8,512]{2,1,0:T(8,128)(2,1)}), bf16[16,8,512]{2,1,0:T(8,128)(2,1)S(1)}, u32[]{:S(2)}, u32[]{:S(2)}) async-start(bf16[16,8,512]{2,1,0:T(8,128)(2,1)} %shard_map.129), calls=%async_computation.5 | async-start | bytes 262144 | tf_op jit(solution)/shard_map/all_to_all | solution.py:26
  114.7 0.0 copy-start.10
  114.7 0.7 copy-done.10
  115.4 1.3 reshape.216
  116.7 0.0 copy-start.7
  116.8 0.3 constant_dynamic-slice_fusion.1
  117.1 0.2 copy.45
  117.3 0.5 copy-done.7
  117.8 0.1 copy.32
  117.9 1.0 shard_map.131
  118.9 8.2 %all-to-all-done.5 = bf16[16,8,512]{2,1,0:T(8,128)(2,1)S(1)} async-done(((bf16[16,8,512]{2,1,0:T(8,128)(2,1)}), bf16[16,8,512]{2,1,0:T(8,128)(2,1)S(1)}, u32[]{:S(2)}, u32[]{:S(2)}) %all-to-all-start.5) | async-done | bytes 131104 | tf_op jit(solution)/shard_map/all_to_all | solution.py:26
  127.1 1.0 shard_map.130
  128.0 3.6 %all-to-all-start.6 = ((bf16[16,32,512]{2,1,0:T(8,128)(2,1)}), bf16[16,32,512]{2,1,0:T(8,128)(2,1)S(1)}, u32[]{:S(2)}, u32[]{:S(2)}) async-start(bf16[16,32,512]{2,1,0:T(8,128)(2,1)} %shard_map.130), calls=%async_computation.6 | async-start | bytes 1048576 | tf_op jit(solution)/shard_map/all_to_all | solution.py:32
  131.7 0.1 le.26
  131.8 0.1 le.61
  131.9 0.2 copy.38
  132.1 0.2 copy.44
  132.2 8.8 %all-to-all-done.6 = bf16[16,32,512]{2,1,0:T(8,128)(2,1)S(1)} async-done(((bf16[16,32,512]{2,1,0:T(8,128)(2,1)}), bf16[16,32,512]{2,1,0:T(8,128)(2,1)S(1)}, u32[]{:S(2)}, u32[]{:S(2)}) %all-to-all-start.6) | async-done | bytes 524320 | tf_op jit(solution)/shard_map/all_to_all | solution.py:32
  141.0 5.0 %collective-permute-start.7 = (bf16[512,512]{1,0:T(8,128)(2,1)S(1)}, bf16[512,512]{1,0:T(8,128)(2,1)S(1)}, u32[]{:S(2)}, u32[]{:S(2)}) collective-permute-start(bf16[512,512]{1,0:T(8,128)(2,1)S(1)} %bitcast.60), channel_id=1, source_target_pairs={{0,16},{16,0},{32,48},{48,32},{64,80},{80,64},{96,112},{112,96},{1... | collective-permute-start | bytes 1572872 | tf_op jit(solution)/shard_map/ppermute | solution.py:39
  146.1 0.1 le.64
  146.2 0.2 copy.43
  146.3 0.1 le.58
  146.4 0.1 and_convert_fusion
  146.6 1.0 shard_map.132
  147.6 1.8 %shard_map.133 = bf16[512,512]{1,0:T(8,128)(2,1)S(1)} custom-call(bf16[512,512]{1,0:T(8,128)(2,1)S(1)} %bitcast.59, bf16[512,512]{1,0:T(8,128)(2,1)S(1)} %collective-permute-done.7.keys_ref, f32[128,512]{1,0:T(8,128)S(1)} %get-tuple-element.55.seen_ref, f32[512,128]{1,0:T(8,128)S(1)} %get-tuple-element.44.stats_ref, f32[512,512]{1,0:T(8,128)S(1)} %get-tuple-element.45.mixed_ref), custom_call_target="tpu_custom_call" | custom-call | tf_op jit(solution)/shard_map/pallas_call | solution.py:56
  149.4 1.2 copy.56
  (36 shorter events, 0.3 us)
Async XLA Ops:
  0.6 10.3 %collective-permute-start = (bf16[256,224]{1,0:T(8,128)(2,1)}, bf16[256,224]{1,0:T(8,128)(2,1)S(1)}, u32[]{:S(2)}, u32[]{:S(2)}) collective-permute-start(bf16[256,224]{1,0:T(8,128)(2,1)} %bitcast.66), channel_id=1, source_target_pairs={{0,16},{16,0},{32,48},{48,32},{64,80},{80,64},{96,112},{112,96},{1... | collective-permute-start | bytes 344072 | tf_op jit(solution)/shard_map/ppermute | solution.py:39
  10.9 0.9 copy-start
  12.7 14.0 %copy-start.11 = (f32[224]{0:T(256)S(1)}, f32[224]{0:T(256)}, u32[]{:S(2)}) copy-start(f32[224]{0:T(256)} %param.14) | copy-start | bytes 2692
  12.7 22.0 %all-to-all-start = ((bf16[16,8,512]{2,1,0:T(8,128)(2,1)}), bf16[16,8,512]{2,1,0:T(8,128)(2,1)S(1)}, u32[]{:S(2)}, u32[]{:S(2)}) async-start(bf16[16,8,512]{2,1,0:T(8,128)(2,1)} %bitcast.6), calls=%async_computation | async-start | bytes 262144 | tf_op jit(solution)/shard_map/all_to_all | solution.py:26
  22.4 12.7 %collective-permute-start.2 = (bf16[224,2048]{1,0:T(8,128)(2,1)}, bf16[224,2048]{1,0:T(8,128)(2,1)S(1)}, u32[]{:S(2)}, u32[]{:S(2)}) collective-permute-start(bf16[224,2048]{1,0:T(8,128)(2,1)} %bitcast.70), channel_id=1, source_target_pairs={{0,16},{16,0},{32,48},{48,32},{64,80},{80,64},{96,112},{112,96},{1... | collective-permute-start | bytes 2752520 | tf_op jit(solution)/shard_map/ppermute | solution.py:39
  24.6 10.4 %collective-permute-start.3 = (bf16[224,2048]{1,0:T(8,128)(2,1)}, bf16[224,2048]{1,0:T(8,128)(2,1)S(1)}, u32[]{:S(2)}, u32[]{:S(2)}) collective-permute-start(bf16[224,2048]{1,0:T(8,128)(2,1)} %bitcast.72), channel_id=1, source_target_pairs={{0,16},{16,0},{32,48},{48,32},{64,80},{80,64},{96,112},{112,96},{1... | collective-permute-start | bytes 2752520 | tf_op jit(solution)/shard_map/ppermute | solution.py:39
  26.7 3.1 %collective-permute-start.1 = (f32[8,224]{1,0:T(8,128)S(1)}, f32[8,224]{1,0:T(8,128)S(1)}, u32[]{:S(2)}, u32[]{:S(2)}) collective-permute-start(f32[8,224]{1,0:T(8,128)S(1)} %broadcast_in_dim.31.refs_1_), channel_id=1, source_target_pairs={{0,16},{16,0},{32,48},{48,32},{64,80},{80,64},{96,112},{112,96},{1... | collective-permute-start | bytes 21512 | tf_op jit(solution)/shard_map/ppermute | solution.py:39
  34.7 1.2 copy-start.2
  34.7 1.5 copy-start.3
  37.8 6.9 %copy-start.6 = (bf16[1,2048,224]{1,2,0:T(8,128)(2,1)S(1)}, bf16[1,2048,224]{1,2,0:T(8,128)(2,1)}, u32[]{:S(2)}) copy-start(bf16[1,2048,224]{1,2,0:T(8,128)(2,1)} %param.17) | copy-start | bytes 2752516
  37.8 19.9 %all-to-all-start.1 = ((bf16[16,208,128]{2,1,0:T(8,128)(2,1)}), bf16[16,208,128]{2,1,0:T(8,128)(2,1)S(1)}, u32[]{:S(2)}, u32[]{:S(2)}) async-start(bf16[16,208,128]{2,1,0:T(8,128)(2,1)} %shard_map.125), calls=%async_computation.1 | async-start | bytes 1703936 | tf_op jit(solution)/shard_map/all_to_all | solution.py:32
  44.8 25.1 %collective-permute-start.4 = (bf16[224,2048]{1,0:T(8,128)(2,1)S(1)}, bf16[224,2048]{1,0:T(8,128)(2,1)S(1)}, u32[]{:S(2)}, u32[]{:S(2)}) collective-permute-start(bf16[224,2048]{1,0:T(8,128)(2,1)S(1)} %bitcast.77), channel_id=1, source_target_pairs={{0,16},{16,0},{32,48},{48,32},{64,80},{80,64},{96,112},{112,96},{1... | collective-permute-start | bytes 2752520 | tf_op jit(solution)/shard_map/ppermute | solution.py:39
  70.4 9.9 %copy-start.4 = (bf16[224,512]{1,0:T(8,128)(2,1)S(1)}, bf16[224,512]{1,0:T(8,128)(2,1)}, u32[]{:S(2)}) copy-start(bf16[224,512]{1,0:T(8,128)(2,1)} %own_ref.1) | copy-start | bytes 688132
  71.1 13.5 %copy-start.8 = (s32[8,32,8]{1,2,0:T(8,128)S(1)}, s32[8,32,8]{1,2,0:T(8,128)}, u32[]{:S(2)}) copy-start(s32[8,32,8]{1,2,0:T(8,128)} %param.12) | copy-start | bytes 24580
  71.1 13.5 %copy-start.9 = (f32[8,32,8]{1,2,0:T(8,128)S(1)}, f32[8,32,8]{1,2,0:T(8,128)}, u32[]{:S(2)}) copy-start(f32[8,32,8]{1,2,0:T(8,128)} %param.13) | copy-start | bytes 24580
  71.1 13.5 %copy-start.5 = (f32[512]{0:T(512)S(1)}, f32[512]{0:T(512)}, u32[]{:S(2)}) copy-start(f32[512]{0:T(512)} %param.19) | copy-start | bytes 6148
  71.1 21.2 %copy-start.1 = (bf16[8,32,224]{2,1,0:T(8,128)(2,1)S(1)}, bf16[8,32,224]{2,1,0:T(8,128)(2,1)}, u32[]{:S(2)}) copy-start(bf16[8,32,224]{2,1,0:T(8,128)(2,1)} %param.11) | copy-start | bytes 344068
  71.1 21.2 %all-to-all-start.3 = ((bf16[16,8,512]{2,1,0:T(8,128)(2,1)}), bf16[16,8,512]{2,1,0:T(8,128)(2,1)S(1)}, u32[]{:S(2)}, u32[]{:S(2)}) async-start(bf16[16,8,512]{2,1,0:T(8,128)(2,1)} %pad.13), calls=%async_computation.3 | async-start | bytes 262144 | tf_op jit(solution)/shard_map/all_to_all | solution.py:26
  80.3 5.3 %collective-permute-start.5 = (bf16[224,512]{1,0:T(8,128)(2,1)S(1)}, bf16[224,512]{1,0:T(8,128)(2,1)S(1)}, u32[]{:S(2)}, u32[]{:S(2)}) collective-permute-start(bf16[224,512]{1,0:T(8,128)(2,1)S(1)} %copy-done.4), channel_id=1, source_target_pairs={{0,16},{16,0},{32,48},{48,32},{64,80},{80,64},{96,112},{112,96},{1... | collective-permute-start | bytes 688136 | tf_op jit(solution)/shard_map/ppermute | solution.py:39
  93.7 16.7 %all-to-all-start.4 = ((bf16[32,8,512]{2,1,0:T(8,128)(2,1)}), bf16[32,8,512]{2,1,0:T(8,128)(2,1)S(1)}, u32[]{:S(2)}, u32[]{:S(2)}) async-start(bf16[32,8,512]{2,1,0:T(8,128)(2,1)} %bitcast.11), calls=%async_computation.4 | async-start | bytes 524288 | tf_op jit(solution)/shard_map/all_to_all | solution.py:26
  101.4 9.8 %collective-permute-start.6 = (bf16[128,256]{1,0:T(8,128)(2,1)S(1)}, bf16[128,256]{1,0:T(8,128)(2,1)S(1)}, u32[]{:S(2)}, u32[]{:S(2)}) collective-permute-start(bf16[128,256]{1,0:T(8,128)(2,1)S(1)} %slice.36), channel_id=1, source_target_pairs={{0,16},{16,0},{32,48},{48,32},{64,80},{80,64},{96,112},{112,96},{1... | collective-permute-start | bytes 196616 | tf_op jit(solution)/shard_map/ppermute | solution.py:39
  111.2 15.9 %all-to-all-start.5 = ((bf16[16,8,512]{2,1,0:T(8,128)(2,1)}), bf16[16,8,512]{2,1,0:T(8,128)(2,1)S(1)}, u32[]{:S(2)}, u32[]{:S(2)}) async-start(bf16[16,8,512]{2,1,0:T(8,128)(2,1)} %shard_map.129), calls=%async_computation.5 | async-start | bytes 262144 | tf_op jit(solution)/shard_map/all_to_all | solution.py:26
  114.7 0.7 copy-start.10
  116.7 1.0 copy-start.7
  128.0 13.0 %all-to-all-start.6 = ((bf16[16,32,512]{2,1,0:T(8,128)(2,1)}), bf16[16,32,512]{2,1,0:T(8,128)(2,1)S(1)}, u32[]{:S(2)}, u32[]{:S(2)}) async-start(bf16[16,32,512]{2,1,0:T(8,128)(2,1)} %shard_map.130), calls=%async_computation.6 | async-start | bytes 1048576 | tf_op jit(solution)/shard_map/all_to_all | solution.py:32
  141.0 6.6 %collective-permute-start.7 = (bf16[512,512]{1,0:T(8,128)(2,1)S(1)}, bf16[512,512]{1,0:T(8,128)(2,1)S(1)}, u32[]{:S(2)}, u32[]{:S(2)}) collective-permute-start(bf16[512,512]{1,0:T(8,128)(2,1)S(1)} %bitcast.60), channel_id=1, source_target_pairs={{0,16},{16,0},{32,48},{48,32},{64,80},{80,64},{96,112},{112,96},{1... | collective-permute-start | bytes 1572872 | tf_op jit(solution)/shard_map/ppermute | solution.py:39

commit v4 on v3

--- a/solution.py
+++ b/solution.py
@@ -72,9 +72,29 @@
     return jnp.sum(jnp.where(inside, values, 0.0), axis=1, keepdims=True)
 
 
-def gate_kernel(gate_ref, gain_ref, out_ref, gains_ref):
+def side_kernel(place_ref, gate_ref, gain_ref, ends_ref, out_ref, gains_ref, seen_ref, seen_pair_ref):
     out_ref[...] = jnp.broadcast_to(column(gate_ref[...]), out_ref.shape)
     gains_ref[...] = jnp.broadcast_to(gain_ref[...], gains_ref.shape)
+    shard, core = place_ref[0], place_ref[1]
+    local, count = seen_ref.shape
+    shards = ends_ref.shape[0]
+    ends = ends_ref[...].astype(f32)
+    query = (shard * local + iota((local, count), 0)).astype(f32)
+    planes = local // 8
+    chip, rest = iota((count, 1), 0) // (2 * planes), iota((count, 1), 0) % (2 * planes)
+    run = jnp.where(rest >= planes, shard // BLOCK, 0)
+    hidden = (rest >= planes) & (shard // BLOCK == 0)
+    key_shard = run * BLOCK + chip // 4
+    chosen = (iota((count, shards), 1) == key_shard).astype(f32)
+    chosen = jnp.dot(chosen, ends, preferred_element_type=f32, precision=lax.Precision.HIGHEST)
+    for part, ref in ((core, seen_ref), (1 - core, seen_pair_ref)):
+        row = rest % planes * 8 + chip % 4 * 2 + part
+        end = jnp.sum(jnp.where(iota((count, local), 1) == row, chosen, 0.0), axis=1, keepdims=True)
+        end = jnp.where(hidden, -1.0, end)
+        index = (key_shard * local + row).astype(f32)
+        end = jnp.transpose(jnp.broadcast_to(end, (count, local)))
+        index = jnp.transpose(jnp.broadcast_to(index, (count, local)))
+        ref[...] = ((index <= query) & (query <= end)).astype(f32)
 
 
 def routing_kernel(core_ref, expert_ref, placed_ref, table_ref):
@@ -268,11 +288,19 @@
     wide = shape((padded, 2 * WIDE), bf16)
     dispatched = local_kernel(dispatch_kernel, wide, placed, rows, rows_pair)
     own = (gate_weight[0], up_weight[0], down_weight[0].T, latent_weight, moe_gain)
-    late = (gates, latent_gain)
+    late = (gates, latent_gain, subtree_end)
     dispatched, own, late = lax.optimization_barrier((dispatched, own, late))
     gate = jnp.sum(jnp.where(near, late[0], 0.0), axis=2)
-    gate, latent_gains = local_kernel(
-        gate_kernel, (shape((tokens, 128), f32), shape((8, latent_width), f32)), gate, late[1][None, :]
+    local, heads = queries.shape[:2]
+    sight = shape((local, chips * 2 * exp_count), f32)
+    gate, latent_gains, seen, seen_pair = local_kernel(
+        side_kernel,
+        (shape((tokens, 128), f32), shape((8, latent_width), f32), sight, sight),
+        jnp.stack([lax.axis_index("ctx"), core]),
+        gate,
+        late[1][None, :],
+        late[2].reshape(ctx_count, local),
+        spaces=[pltpu.SMEM] + [pltpu.VMEM] * 3,
     )
     gate_own, up_own, down_own, _, gain_own = own
     gain_own = jnp.broadcast_to(gain_own[None, :], (8, width))
@@ -326,38 +354,18 @@
     next_rows = local_kernel(
         next_kernel, shape(rows.shape, bf16), returned, returned_rest, table, gate, rows
     )
-    local, heads = queries.shape[:2]
     queries = queries.transpose(1, 0, 2).reshape(heads * local, latent_width)
     chunks = local_kernel(key_kernel, shape((chips, 2 * exp_count, latent_width), bf16), plane)
     chunks, next_rows, queries = lax.optimization_barrier((chunks, next_rows, queries))
     keys = exchange_chips(chunks).reshape(chips * 2 * exp_count, latent_width)
     keys_pair = swap(keys)
 
-    shard_index = lax.axis_index("ctx")
-    group = shard_index // BLOCK
-    ends = subtree_end.reshape(GROUPS, BLOCK, exp_count, row_group // 2, 2)
-    positions = jnp.arange(subtree_end.shape[0], dtype=jnp.int32).reshape(ends.shape)
-
-    def key_order(table, hide, part):
-        table = lax.dynamic_index_in_dim(table, part, 4, keepdims=False)
-        own_table = lax.dynamic_index_in_dim(table, group, 0, keepdims=False)
-        own_table = jnp.where(group == 0, hide, own_table)
-        both = jnp.stack([table[0], own_table])
-        return both.transpose(1, 3, 0, 2).reshape(-1)
-
-    query_index = shard_index * local + jnp.arange(local, dtype=jnp.int32)
-
-    def visible(part):
-        key_end, key_index = key_order(ends, -1, part), key_order(positions, 0, part)
-        seen = (key_index[None, :] <= query_index[:, None]) & (query_index[:, None] <= key_end[None, :])
-        return seen.astype(f32)
-
     first = local_kernel(
         first_kernel,
         (shape((heads * local, 128), f32), shape((heads * local, latent_width), f32)),
         queries,
         keys,
-        visible(core),
+        seen,
         grant=16,
     )
     attn_out = local_kernel(
@@ -365,7 +373,7 @@
         shape((heads * local, latent_width), bf16),
         queries,
         keys_pair,
-        visible(1 - core),
+        seen_pair,
         *first,
         grant=16,
     )

time: 152 us -> 150 us (0.987)
  blocking collectives: 11.5 us -> 23.8 us
  waiting for transfers between devices: 45.7 us -> 38.6 us
  local copies, waits for them, and re-layouts: 8.01 us -> 4.79 us
  starting transfers between devices: 71.5 us -> 68.3 us
    all_to_all x1 -> x2, blocking collectives: 11.5 us -> 23.8 us  [exchange_chips(): lax.all_to_all(chunks, 'ctx', split_axis=0, concat_axis=0, tiled=True, ax...]
    all_to_all x2 -> x1, waiting for transfers between devices: 17.6 us -> 8.84 us  [exchange_chips(): lax.all_to_all(chunks, 'ctx', split_axis=0, concat_axis=0, tiled=True, ax...]
    all_to_all x2 -> x1, starting transfers between devices: 10.5 us -> 6.9 us  [exchange_chips(): lax.all_to_all(chunks, 'ctx', split_axis=0, concat_axis=0, tiled=True, ax...]
    all_to_all x4, waiting for transfers between devices: 26.5 us -> 28.4 us  [exchange(): return lax.all_to_all(chunks, axis, split_axis=0, concat_axis=0, tiled=True)]
    unnamed x27 -> x24, local copies, waits for them, and re-layouts: 3.79 us -> 2.77 us
  transfers between devices with their start and end apart: 14 -> 13, of which waited for: 8 -> 7; matrix products, arithmetic and copies ran while one was open for 3% -> 1% of each run, Pallas kernels for 3% -> 3%
where the time goes in v4:
time: 150 us; the launch traced here: 149 us
  starting transfers between devices  68.3 us (46%)
  waiting for transfers between devices  38.6 us (26%)
  blocking collectives  23.8 us (16%)
  Pallas kernels  11 us (7%)
  local copies, waits for them, and re-layouts  4.79 us (3%)
    ppermute x8, starting transfers between devices, swap(): return lax.ppermute(value, 'ctx', [(i, i ^ 1) for i in range(count)])  31.3 us
    all_to_all x4, starting transfers between devices, exchange(): return lax.all_to_all(chunks, axis, split_axis=0, concat_axis=0, tiled=True)  30.1 us
    all_to_all x4, waiting for transfers between devices, exchange(): return lax.all_to_all(chunks, axis, split_axis=0, concat_axis=0, tiled=True)  28.4 us
    all_to_all x2, blocking collectives, exchange_chips(): lax.all_to_all(chunks, 'ctx', split_axis=0, concat_axis=0, tiled=True, ax...  23.8 us
    pallas_call x12, Pallas kernels, local_kernel(): pl.pallas_call(kernel, out_shape=out_shape, in_specs=[pl.BlockSpec(memory...  11 us
    all_to_all x1, waiting for transfers between devices, exchange_chips(): lax.all_to_all(chunks, 'ctx', split_axis=0, concat_axis=0, tiled=True, ax...  8.84 us
    all_to_all x1, starting transfers between devices, exchange_chips(): lax.all_to_all(chunks, 'ctx', split_axis=0, concat_axis=0, tiled=True, ax...  6.9 us
  transfers between devices with their start and end apart: 13, of which 7 were waited for; matrix products, arithmetic and copies ran while one was open for 1% of the time, Pallas kernels for 3%

profile of v4, /device:TPU:1, one launch (start us, length us, event | category | flops | bytes accessed | tf_op | source)
XLA Modules:
  0.0 149.3 jit_solution(18048043400761263460)
XLA Ops:
  0.6 8.8 %collective-permute-start = (bf16[256,224]{1,0:T(8,128)(2,1)}, bf16[256,224]{1,0:T(8,128)(2,1)S(1)}, u32[]{:S(2)}, u32[]{:S(2)}) collective-permute-start(bf16[256,224]{1,0:T(8,128)(2,1)} %bitcast.46), channel_id=1, source_target_pairs={{0,16},{16,0},{32,48},{48,32},{64,80},{80,64},{96,112},{112,96},{1... | collective-permute-start | bytes 344072 | tf_op jit(solution)/shard_map/ppermute | solution.py:39
  9.4 0.8 fusion.7
  10.2 0.7 shard_map.122
  10.9 0.0 collective-permute-done.pair_ref
  10.9 0.0 copy-start
  10.9 0.9 copy-done
  11.8 0.8 shard_map.123
  12.7 0.0 copy-start.11
  12.7 9.7 %all-to-all-start = ((bf16[16,8,512]{2,1,0:T(8,128)(2,1)}), bf16[16,8,512]{2,1,0:T(8,128)(2,1)S(1)}, u32[]{:S(2)}, u32[]{:S(2)}) async-start(bf16[16,8,512]{2,1,0:T(8,128)(2,1)} %bitcast.6), calls=%async_computation | async-start | bytes 262144 | tf_op jit(solution)/shard_map/all_to_all | solution.py:26
  22.4 2.2 %collective-permute-start.2 = (bf16[224,2048]{1,0:T(8,128)(2,1)}, bf16[224,2048]{1,0:T(8,128)(2,1)S(1)}, u32[]{:S(2)}, u32[]{:S(2)}) collective-permute-start(bf16[224,2048]{1,0:T(8,128)(2,1)} %bitcast.50), channel_id=1, source_target_pairs={{0,16},{16,0},{32,48},{48,32},{64,80},{80,64},{96,112},{112,96},{1... | collective-permute-start | bytes 2752520 | tf_op jit(solution)/shard_map/ppermute | solution.py:39
  24.6 2.1 %collective-permute-start.3 = (bf16[224,2048]{1,0:T(8,128)(2,1)}, bf16[224,2048]{1,0:T(8,128)(2,1)S(1)}, u32[]{:S(2)}, u32[]{:S(2)}) collective-permute-start(bf16[224,2048]{1,0:T(8,128)(2,1)} %bitcast.52), channel_id=1, source_target_pairs={{0,16},{16,0},{32,48},{48,32},{64,80},{80,64},{96,112},{112,96},{1... | collective-permute-start | bytes 2752520 | tf_op jit(solution)/shard_map/ppermute | solution.py:39
  26.7 0.0 copy-done.11
  26.7 2.2 %collective-permute-start.1 = (f32[8,224]{1,0:T(8,128)S(1)}, f32[8,224]{1,0:T(8,128)S(1)}, u32[]{:S(2)}, u32[]{:S(2)}) collective-permute-start(f32[8,224]{1,0:T(8,128)S(1)} %broadcast_in_dim.18.refs_1_), channel_id=1, source_target_pairs={{0,16},{16,0},{32,48},{48,32},{64,80},{80,64},{96,112},{112,96},{1... | collective-permute-start | bytes 21512 | tf_op jit(solution)/shard_map/ppermute | solution.py:39
  29.0 0.8 collective-permute-done.1.refs_2_
  29.8 4.9 %all-to-all-done = bf16[16,8,512]{2,1,0:T(8,128)(2,1)S(1)} async-done(((bf16[16,8,512]{2,1,0:T(8,128)(2,1)}), bf16[16,8,512]{2,1,0:T(8,128)(2,1)S(1)}, u32[]{:S(2)}, u32[]{:S(2)}) %all-to-all-start) | async-done | bytes 131104 | tf_op jit(solution)/shard_map/all_to_all | solution.py:26
  34.7 0.3 shard_map.124
  35.0 0.0 collective-permute-done.2.gate_pair
  35.0 0.0 collective-permute-done.3.up_pair
  35.0 0.9 copy-done.2
  35.9 0.3 copy-done.3
  36.2 1.7 %shard_map.125 = bf16[16,208,128]{2,1,0:T(8,128)(2,1)} custom-call(bf16[96,224]{1,0:T(8,128)(2,1)S(1)} %get-tuple-element.30.own_ref, bf16[96,224]{1,0:T(8,128)(2,1)S(1)} %get-tuple-element.31.pair_ref, bf16[16,128]{1,0:T(8,128)(2,1)S(1)} %get-tuple-element.32.square_ref, bf16[224,2048]{1,0:T(8,128)(2,1)S(1)} %bitcast.51, ...), custom_call_target="tpu_custom_call" | custom-call | tf_op jit(solution)/shard_map/pallas_call | solution.py:56
  37.9 6.9 %all-to-all-start.1 = ((bf16[16,208,128]{2,1,0:T(8,128)(2,1)}), bf16[16,208,128]{2,1,0:T(8,128)(2,1)S(1)}, u32[]{:S(2)}, u32[]{:S(2)}) async-start(bf16[16,208,128]{2,1,0:T(8,128)(2,1)} %shard_map.125), calls=%async_computation.1 | async-start | bytes 1703936 | tf_op jit(solution)/shard_map/all_to_all | solution.py:32
  44.8 0.0 copy-done.7
  44.8 4.1 %collective-permute-start.4 = (bf16[224,2048]{1,0:T(8,128)(2,1)S(1)}, bf16[224,2048]{1,0:T(8,128)(2,1)S(1)}, u32[]{:S(2)}, u32[]{:S(2)}) collective-permute-start(bf16[224,2048]{1,0:T(8,128)(2,1)S(1)} %bitcast.58), channel_id=1, source_target_pairs={{0,16},{16,0},{32,48},{48,32},{64,80},{80,64},{96,112},{112,96},{1... | collective-permute-start | bytes 2752520 | tf_op jit(solution)/shard_map/ppermute | solution.py:39
  48.9 8.8 %all-to-all-done.1.refs_0_ = bf16[16,208,128]{2,1,0:T(8,128)(2,1)S(1)} async-done(((bf16[16,208,128]{2,1,0:T(8,128)(2,1)}), bf16[16,208,128]{2,1,0:T(8,128)(2,1)S(1)}, u32[]{:S(2)}, u32[]{:S(2)}) %all-to-all-start.1) | async-done | bytes 852000 | tf_op jit(solution)/shard_map/all_to_all | solution.py:32
  57.8 0.1 shard_map.126
  57.9 11.5 %all_to_all.35 = bf16[16,96,128]{2,1,0:T(8,128)(2,1)S(1)} all-to-all(bf16[16,96,128]{2,1,0:T(8,128)(2,1)S(1)} %shard_map.126), channel_id=1, replica_groups={{0,32,64,96,128,160,192,224,256,288,320,352,384,416,448,480},{16,48,80,..., dimensions={0} | all-to-all | bytes 786432 | tf_op jit(solution)/shard_map/all_to_all | solution.py:32
  69.5 0.4 convolution_convert_fusion.1
  69.9 0.0 collective-permute-done.4
  69.9 0.4 convolution_convert_fusion
  70.4 0.0 copy-start.4
  70.4 0.7 pad.13
  71.1 9.2 %all-to-all-start.3 = ((bf16[16,8,512]{2,1,0:T(8,128)(2,1)}), bf16[16,8,512]{2,1,0:T(8,128)(2,1)S(1)}, u32[]{:S(2)}, u32[]{:S(2)}) async-start(bf16[16,8,512]{2,1,0:T(8,128)(2,1)} %pad.13), calls=%async_computation.3 | async-start | bytes 262144 | tf_op jit(solution)/shard_map/all_to_all | solution.py:26
  80.3 0.0 copy-done.4
  80.3 4.2 %collective-permute-start.5 = (bf16[224,512]{1,0:T(8,128)(2,1)S(1)}, bf16[224,512]{1,0:T(8,128)(2,1)S(1)}, u32[]{:S(2)}, u32[]{:S(2)}) collective-permute-start(bf16[224,512]{1,0:T(8,128)(2,1)S(1)} %copy-done.4), channel_id=1, source_target_pairs={{0,16},{16,0},{32,48},{48,32},{64,80},{80,64},{96,112},{112,96},{1... | collective-permute-start | bytes 688136 | tf_op jit(solution)/shard_map/ppermute | solution.py:39
  84.6 0.1 pad_add_fusion.place_ref
  84.6 0.0 copy-done.9
  84.6 0.0 copy-done.10
  84.7 0.0 copy-start.6
  84.7 0.7 copy-done.5
  85.4 0.0 copy-done.6
  85.4 1.4 shard_map.127
  86.8 0.0 collective-permute-done.5.pair_ref
  86.8 5.5 %all-to-all-done.3 = bf16[16,8,512]{2,1,0:T(8,128)(2,1)S(1)} async-done(((bf16[16,8,512]{2,1,0:T(8,128)(2,1)}), bf16[16,8,512]{2,1,0:T(8,128)(2,1)S(1)}, u32[]{:S(2)}, u32[]{:S(2)}) %all-to-all-start.3) | async-done | bytes 131104 | tf_op jit(solution)/shard_map/all_to_all | solution.py:26
  92.3 0.0 copy-done.1
  92.3 1.4 shard_map.128
  93.7 7.7 %all-to-all-start.4 = ((bf16[32,8,512]{2,1,0:T(8,128)(2,1)}), bf16[32,8,512]{2,1,0:T(8,128)(2,1)S(1)}, u32[]{:S(2)}, u32[]{:S(2)}) async-start(bf16[32,8,512]{2,1,0:T(8,128)(2,1)} %bitcast.13), calls=%async_computation.4 | async-start | bytes 524288 | tf_op jit(solution)/shard_map/all_to_all | solution.py:26
  101.4 0.0 copy-start.8
  101.4 2.4 %collective-permute-start.6 = (bf16[128,256]{1,0:T(8,128)(2,1)S(1)}, bf16[128,256]{1,0:T(8,128)(2,1)S(1)}, u32[]{:S(2)}, u32[]{:S(2)}) collective-permute-start(bf16[128,256]{1,0:T(8,128)(2,1)S(1)} %slice.4), channel_id=1, source_target_pairs={{0,16},{16,0},{32,48},{48,32},{64,80},{80,64},{96,112},{112,96},{1... | collective-permute-start | bytes 196616 | tf_op jit(solution)/shard_map/ppermute | solution.py:39
  103.8 6.6 %all-to-all-done.4.part_ref = bf16[32,8,512]{2,1,0:T(8,128)(2,1)S(1)} async-done(((bf16[32,8,512]{2,1,0:T(8,128)(2,1)}), bf16[32,8,512]{2,1,0:T(8,128)(2,1)S(1)}, u32[]{:S(2)}, u32[]{:S(2)}) %all-to-all-start.4) | async-done | bytes 262176 | tf_op jit(solution)/shard_map/all_to_all | solution.py:26
  110.4 0.8 shard_map.129
  111.2 0.0 collective-permute-done.6.rest_ref
  111.2 3.5 %all-to-all-start.5 = ((bf16[16,8,512]{2,1,0:T(8,128)(2,1)}), bf16[16,8,512]{2,1,0:T(8,128)(2,1)S(1)}, u32[]{:S(2)}, u32[]{:S(2)}) async-start(bf16[16,8,512]{2,1,0:T(8,128)(2,1)} %shard_map.129), calls=%async_computation.5 | async-start | bytes 262144 | tf_op jit(solution)/shard_map/all_to_all | solution.py:26
  114.7 0.0 copy-done.8
  114.7 0.1 copy.16
  114.8 1.0 shard_map.131
  115.8 11.3 %all-to-all-done.5 = bf16[16,8,512]{2,1,0:T(8,128)(2,1)S(1)} async-done(((bf16[16,8,512]{2,1,0:T(8,128)(2,1)}), bf16[16,8,512]{2,1,0:T(8,128)(2,1)S(1)}, u32[]{:S(2)}, u32[]{:S(2)}) %all-to-all-start.5) | async-done | bytes 131104 | tf_op jit(solution)/shard_map/all_to_all | solution.py:26
  127.1 0.2 shard_map.130
  127.3 12.3 %all_to_all.36 = bf16[16,32,512]{2,1,0:T(8,128)(2,1)S(1)} all-to-all(bf16[16,32,512]{2,1,0:T(8,128)(2,1)S(1)} %shard_map.130), channel_id=1, replica_groups={{0,32,64,96,128,160,192,224,256,288,320,352,384,416,448,480},{16,48,80,..., dimensions={0} | all-to-all | bytes 1048576 | tf_op jit(solution)/shard_map/all_to_all | solution.py:32
  139.6 5.2 %collective-permute-start.7 = (bf16[512,512]{1,0:T(8,128)(2,1)S(1)}, bf16[512,512]{1,0:T(8,128)(2,1)S(1)}, u32[]{:S(2)}, u32[]{:S(2)}) collective-permute-start(bf16[512,512]{1,0:T(8,128)(2,1)S(1)} %bitcast.40), channel_id=1, source_target_pairs={{0,16},{16,0},{32,48},{48,32},{64,80},{80,64},{96,112},{112,96},{1... | collective-permute-start | bytes 1572872 | tf_op jit(solution)/shard_map/ppermute | solution.py:39
  144.8 1.0 shard_map.132
  145.8 0.5 collective-permute-done.7.keys_ref
  146.3 1.8 %shard_map.133 = bf16[512,512]{1,0:T(8,128)(2,1)S(1)} custom-call(bf16[512,512]{1,0:T(8,128)(2,1)S(1)} %bitcast.39, bf16[512,512]{1,0:T(8,128)(2,1)S(1)} %collective-permute-done.7.keys_ref, f32[128,512]{1,0:T(8,128)S(1)} %get-tuple-element.48.seen_ref, f32[512,128]{1,0:T(8,128)S(1)} %get-tuple-element.50.stats_ref, f32[512,512]{1,0:T(8,128)S(1)} %get-tuple-element.51.mixed_ref), custom_call_target="tpu_custom_call" | custom-call | tf_op jit(solution)/shard_map/pallas_call | solution.py:56
  148.1 1.2 copy.28
  (13 shorter events, 0.1 us)
Async XLA Ops:
  0.6 10.3 %collective-permute-start = (bf16[256,224]{1,0:T(8,128)(2,1)}, bf16[256,224]{1,0:T(8,128)(2,1)S(1)}, u32[]{:S(2)}, u32[]{:S(2)}) collective-permute-start(bf16[256,224]{1,0:T(8,128)(2,1)} %bitcast.46), channel_id=1, source_target_pairs={{0,16},{16,0},{32,48},{48,32},{64,80},{80,64},{96,112},{112,96},{1... | collective-permute-start | bytes 344072 | tf_op jit(solution)/shard_map/ppermute | solution.py:39
  10.9 0.9 copy-start
  12.7 14.0 %copy-start.11 = (f32[224]{0:T(256)S(1)}, f32[224]{0:T(256)}, u32[]{:S(2)}) copy-start(f32[224]{0:T(256)} %param.14) | copy-start | bytes 2692
  12.7 22.0 %all-to-all-start = ((bf16[16,8,512]{2,1,0:T(8,128)(2,1)}), bf16[16,8,512]{2,1,0:T(8,128)(2,1)S(1)}, u32[]{:S(2)}, u32[]{:S(2)}) async-start(bf16[16,8,512]{2,1,0:T(8,128)(2,1)} %bitcast.6), calls=%async_computation | async-start | bytes 262144 | tf_op jit(solution)/shard_map/all_to_all | solution.py:26
  22.4 12.7 %collective-permute-start.2 = (bf16[224,2048]{1,0:T(8,128)(2,1)}, bf16[224,2048]{1,0:T(8,128)(2,1)S(1)}, u32[]{:S(2)}, u32[]{:S(2)}) collective-permute-start(bf16[224,2048]{1,0:T(8,128)(2,1)} %bitcast.50), channel_id=1, source_target_pairs={{0,16},{16,0},{32,48},{48,32},{64,80},{80,64},{96,112},{112,96},{1... | collective-permute-start | bytes 2752520 | tf_op jit(solution)/shard_map/ppermute | solution.py:39
  24.6 10.4 %collective-permute-start.3 = (bf16[224,2048]{1,0:T(8,128)(2,1)}, bf16[224,2048]{1,0:T(8,128)(2,1)S(1)}, u32[]{:S(2)}, u32[]{:S(2)}) collective-permute-start(bf16[224,2048]{1,0:T(8,128)(2,1)} %bitcast.52), channel_id=1, source_target_pairs={{0,16},{16,0},{32,48},{48,32},{64,80},{80,64},{96,112},{112,96},{1... | collective-permute-start | bytes 2752520 | tf_op jit(solution)/shard_map/ppermute | solution.py:39
  26.7 3.1 %collective-permute-start.1 = (f32[8,224]{1,0:T(8,128)S(1)}, f32[8,224]{1,0:T(8,128)S(1)}, u32[]{:S(2)}, u32[]{:S(2)}) collective-permute-start(f32[8,224]{1,0:T(8,128)S(1)} %broadcast_in_dim.18.refs_1_), channel_id=1, source_target_pairs={{0,16},{16,0},{32,48},{48,32},{64,80},{80,64},{96,112},{112,96},{1... | collective-permute-start | bytes 21512 | tf_op jit(solution)/shard_map/ppermute | solution.py:39
  34.7 1.2 copy-start.2
  34.7 1.5 copy-start.3
  37.9 6.9 %copy-start.7 = (bf16[1,2048,224]{1,2,0:T(8,128)(2,1)S(1)}, bf16[1,2048,224]{1,2,0:T(8,128)(2,1)}, u32[]{:S(2)}) copy-start(bf16[1,2048,224]{1,2,0:T(8,128)(2,1)} %param.17) | copy-start | bytes 2752516
  37.9 19.9 %all-to-all-start.1 = ((bf16[16,208,128]{2,1,0:T(8,128)(2,1)}), bf16[16,208,128]{2,1,0:T(8,128)(2,1)S(1)}, u32[]{:S(2)}, u32[]{:S(2)}) async-start(bf16[16,208,128]{2,1,0:T(8,128)(2,1)} %shard_map.125), calls=%async_computation.1 | async-start | bytes 1703936 | tf_op jit(solution)/shard_map/all_to_all | solution.py:32
  44.8 25.1 %collective-permute-start.4 = (bf16[224,2048]{1,0:T(8,128)(2,1)S(1)}, bf16[224,2048]{1,0:T(8,128)(2,1)S(1)}, u32[]{:S(2)}, u32[]{:S(2)}) collective-permute-start(bf16[224,2048]{1,0:T(8,128)(2,1)S(1)} %bitcast.58), channel_id=1, source_target_pairs={{0,16},{16,0},{32,48},{48,32},{64,80},{80,64},{96,112},{112,96},{1... | collective-permute-start | bytes 2752520 | tf_op jit(solution)/shard_map/ppermute | solution.py:39
  70.4 9.9 %copy-start.4 = (bf16[224,512]{1,0:T(8,128)(2,1)S(1)}, bf16[224,512]{1,0:T(8,128)(2,1)}, u32[]{:S(2)}) copy-start(bf16[224,512]{1,0:T(8,128)(2,1)} %own_ref.1) | copy-start | bytes 688132
  71.1 13.5 %copy-start.9 = (s32[8,32,8]{1,2,0:T(8,128)S(1)}, s32[8,32,8]{1,2,0:T(8,128)}, u32[]{:S(2)}) copy-start(s32[8,32,8]{1,2,0:T(8,128)} %param.12) | copy-start | bytes 24580
  71.1 13.5 %copy-start.10 = (f32[8,32,8]{1,2,0:T(8,128)S(1)}, f32[8,32,8]{1,2,0:T(8,128)}, u32[]{:S(2)}) copy-start(f32[8,32,8]{1,2,0:T(8,128)} %param.13) | copy-start | bytes 24580
  71.1 21.2 %copy-start.1 = (bf16[8,32,224]{2,1,0:T(8,128)(2,1)S(1)}, bf16[8,32,224]{2,1,0:T(8,128)(2,1)}, u32[]{:S(2)}) copy-start(bf16[8,32,224]{2,1,0:T(8,128)(2,1)} %param.11) | copy-start | bytes 344068
  71.1 21.2 %all-to-all-start.3 = ((bf16[16,8,512]{2,1,0:T(8,128)(2,1)}), bf16[16,8,512]{2,1,0:T(8,128)(2,1)S(1)}, u32[]{:S(2)}, u32[]{:S(2)}) async-start(bf16[16,8,512]{2,1,0:T(8,128)(2,1)} %pad.13), calls=%async_computation.3 | async-start | bytes 262144 | tf_op jit(solution)/shard_map/all_to_all | solution.py:26
  80.3 6.4 %collective-permute-start.5 = (bf16[224,512]{1,0:T(8,128)(2,1)S(1)}, bf16[224,512]{1,0:T(8,128)(2,1)S(1)}, u32[]{:S(2)}, u32[]{:S(2)}) collective-permute-start(bf16[224,512]{1,0:T(8,128)(2,1)S(1)} %copy-done.4), channel_id=1, source_target_pairs={{0,16},{16,0},{32,48},{48,32},{64,80},{80,64},{96,112},{112,96},{1... | collective-permute-start | bytes 688136 | tf_op jit(solution)/shard_map/ppermute | solution.py:39
  84.6 0.7 copy-start.5
  84.7 0.7 copy-start.6
  93.7 16.7 %all-to-all-start.4 = ((bf16[32,8,512]{2,1,0:T(8,128)(2,1)}), bf16[32,8,512]{2,1,0:T(8,128)(2,1)S(1)}, u32[]{:S(2)}, u32[]{:S(2)}) async-start(bf16[32,8,512]{2,1,0:T(8,128)(2,1)} %bitcast.13), calls=%async_computation.4 | async-start | bytes 524288 | tf_op jit(solution)/shard_map/all_to_all | solution.py:26
  101.4 13.3 %copy-start.8 = (bf16[128,4,512]{2,1,0:T(4,128)(2,1)S(1)}, bf16[128,4,512]{2,1,0:T(4,128)(2,1)}, u32[]{:S(2)}) copy-start(bf16[128,4,512]{2,1,0:T(4,128)(2,1)} %param.20) | copy-start | bytes 1572868
  101.4 9.8 %collective-permute-start.6 = (bf16[128,256]{1,0:T(8,128)(2,1)S(1)}, bf16[128,256]{1,0:T(8,128)(2,1)S(1)}, u32[]{:S(2)}, u32[]{:S(2)}) collective-permute-start(bf16[128,256]{1,0:T(8,128)(2,1)S(1)} %slice.4), channel_id=1, source_target_pairs={{0,16},{16,0},{32,48},{48,32},{64,80},{80,64},{96,112},{112,96},{1... | collective-permute-start | bytes 196616 | tf_op jit(solution)/shard_map/ppermute | solution.py:39
  111.2 15.9 %all-to-all-start.5 = ((bf16[16,8,512]{2,1,0:T(8,128)(2,1)}), bf16[16,8,512]{2,1,0:T(8,128)(2,1)S(1)}, u32[]{:S(2)}, u32[]{:S(2)}) async-start(bf16[16,8,512]{2,1,0:T(8,128)(2,1)} %shard_map.129), calls=%async_computation.5 | async-start | bytes 262144 | tf_op jit(solution)/shard_map/all_to_all | solution.py:26
  139.6 6.7 %collective-permute-start.7 = (bf16[512,512]{1,0:T(8,128)(2,1)S(1)}, bf16[512,512]{1,0:T(8,128)(2,1)S(1)}, u32[]{:S(2)}, u32[]{:S(2)}) collective-permute-start(bf16[512,512]{1,0:T(8,128)(2,1)S(1)} %bitcast.40), channel_id=1, source_target_pairs={{0,16},{16,0},{32,48},{48,32},{64,80},{80,64},{96,112},{112,96},{1... | collective-permute-start | bytes 1572872 | tf_op jit(solution)/shard_map/ppermute | solution.py:39

commit v5 on v4

--- a/solution.py
+++ b/solution.py
@@ -31,6 +31,14 @@
     groups = [list(range(core, count, 2)) for core in range(2)]
     return lax.all_to_all(
         chunks, "ctx", split_axis=0, concat_axis=0, tiled=True, axis_index_groups=groups
+    )
+
+
+def exchange_pairs(chunks):
+    count, planes = lax.axis_size("ctx"), lax.axis_size("exp")
+    groups = [list(range(chip * 2 * planes, (chip + 1) * 2 * planes)) for chip in range(count // 2)]
+    return lax.all_to_all(
+        chunks, ("ctx", "exp"), split_axis=0, concat_axis=0, tiled=True, axis_index_groups=groups
     )
 
 
@@ -98,7 +106,7 @@
 
 
 def routing_kernel(core_ref, expert_ref, placed_ref, table_ref):
-    core = core_ref[0]
+    core = core_ref[0].astype(f32)
     expert = column(expert_ref[...])
     tokens = expert.shape[0]
     lane = iota((tokens, 128), 1).astype(f32)
@@ -107,24 +115,22 @@
     rank = dot(earlier, picked.astype(bf16))
     rank = jnp.sum(jnp.where(picked, rank, 0.0), axis=1, keepdims=True)
 
-    def slot_in(part):
-        place = rank - (part * PART).astype(f32)
-        valid = (expert >= 0) & (place >= 0) & (place < PART)
-        return jnp.where(valid, expert * PAD + place, -1.0)
-
-    slot = slot_in(core)
-    padded = placed_ref.shape[0]
-    slot_rows = jnp.transpose(jnp.broadcast_to(slot, (tokens, padded)))
-    placed_ref[...] = (slot_rows == iota((padded, tokens), 0).astype(f32)).astype(bf16)
-    table_ref[...] = jnp.where(lane == 0, slot, slot_in(1 - core))
-
-
-def dispatch_kernel(placed_ref, own_ref, pair_ref, out_ref):
+    count = placed_ref.shape[0]
+    part = jnp.where(rank >= PART, 1.0, 0.0)
+    valid = (expert >= 0) & (rank < CAP)
+    slot = expert * PAD + rank - part * PART
+    slot_rows = jnp.where(valid, part * (count // 2) + slot, -1.0)
+    slot_rows = jnp.transpose(jnp.broadcast_to(slot_rows, (tokens, count)))
+    placed_ref[...] = (slot_rows == iota((count, tokens), 0).astype(f32)).astype(bf16)
+    wanted = jnp.where(lane == 0, core, 1.0 - core)
+    table_ref[...] = jnp.where(valid & (part == wanted), slot, -1.0)
+
+
+def dispatch_kernel(placed_ref, rows_ref, out_ref):
     placed = placed_ref[...]
-    width = own_ref.shape[1]
-    for start, rows in ((0, own_ref), (WIDE, pair_ref)):
-        out_ref[:, start : start + WIDE] = jnp.zeros((placed.shape[0], WIDE), bf16)
-        out_ref[:, start : start + width] = dot(placed, rows[...]).astype(bf16)
+    width = rows_ref.shape[1]
+    out_ref[:, width:] = jnp.zeros((placed.shape[0], WIDE - width), bf16)
+    out_ref[:, :width] = dot(placed, rows_ref[...]).astype(bf16)
 
 
 def slot_choice(rows, columns, half, flip):
@@ -134,12 +140,15 @@
     return ((padded == packed_place) & (packed < half)).astype(bf16)
 
 
-def packed_kernel(half, received_ref, gain_ref, gain_pair_ref, own_ref, pair_ref, square_ref):
+def packed_kernel(half, core_ref, received_ref, gain_ref, gain_pair_ref, own_ref, pair_ref, square_ref):
+    core = core_ref[0]
     width = gain_ref.shape[1]
-    rows = dot(slot_choice(128, received_ref.shape[0], half, False), received_ref[...])
-    own_ref[...] = (rows[:half, :width] * gain_ref[0:1, :]).astype(bf16)
-    pair_ref[...] = (rows[:half, WIDE : WIDE + width] * gain_pair_ref[0:1, :]).astype(bf16)
-    squares = jnp.sum(rows * rows, axis=1, keepdims=True)
+    choice = slot_choice(128, received_ref.shape[1], half, False)
+    squares = 0.0
+    for part, gains, ref in ((core, gain_ref, own_ref), (1 - core, gain_pair_ref, pair_ref)):
+        rows = dot(choice, received_ref[part])
+        ref[...] = (rows[:half, :width] * gains[0:1, :]).astype(bf16)
+        squares += jnp.sum(rows * rows, axis=1, keepdims=True)
     squares = jnp.transpose(jnp.broadcast_to(squares, (128, 128)))[:16]
     high = squares.astype(bf16).astype(f32)
     sub = iota((16, 128), 0)
@@ -272,21 +281,20 @@
     latent_width = latent_weight.shape[1]
 
     rows = hidden.reshape(tokens, width)
-    rows_pair = swap(rows)
     core = lax.rem(lax.axis_index("ctx"), 2)
 
     shape = jax.ShapeDtypeStruct
     near = routes < exp_count
     expert = jnp.max(jnp.where(near, routes, -1), axis=2).astype(f32)
+    both = 2 * padded
     placed, table = local_kernel(
         routing_kernel,
-        (shape((padded, tokens), bf16), shape((tokens, 128), f32)),
+        (shape((both, tokens), bf16), shape((tokens, 128), f32)),
         core.reshape(1),
         expert,
         spaces=[pltpu.SMEM, pltpu.VMEM],
     )
-    wide = shape((padded, 2 * WIDE), bf16)
-    dispatched = local_kernel(dispatch_kernel, wide, placed, rows, rows_pair)
+    dispatched = local_kernel(dispatch_kernel, shape((both, WIDE), bf16), placed, rows)
     own = (gate_weight[0], up_weight[0], down_weight[0].T, latent_weight, moe_gain)
     late = (gates, latent_gain, subtree_end)
     dispatched, own, late = lax.optimization_barrier((dispatched, own, late))
@@ -305,14 +313,16 @@
     gate_own, up_own, down_own, _, gain_own = own
     gain_own = jnp.broadcast_to(gain_own[None, :], (8, width))
     gate_pair, up_pair, down_pair, latent_pair, gain_pair = [swap(value) for value in own[:4] + (gain_own,)]
-    received = exchange(dispatched.reshape(exp_count, PAD, 2 * WIDE), "exp").reshape(padded, 2 * WIDE)
+    received = exchange_pairs(dispatched.reshape(2 * exp_count, PAD, WIDE)).reshape(2, padded, WIDE)
 
     packed = local_kernel(
         lambda *refs: packed_kernel(half, *refs),
         (shape((half, width), bf16), shape((half, width), bf16), shape((16, 128), bf16)),
+        core.reshape(1),
         received,
         gain_own,
         gain_pair,
+        spaces=[pltpu.SMEM] + [pltpu.VMEM] * 3,
         cost_estimate=pl.CostEstimate(flops=COST, bytes_accessed=COST, transcendentals=0),
     )
     partial = local_kernel(

time: 150 us -> 149 us (level)
  starting transfers between devices: 68.3 us -> 59.4 us
  waiting for transfers between devices: 38.6 us -> 45.5 us
    all_to_all x0 -> x1, starting transfers between devices: none -> 16.9 us  [exchange_pairs(): lax.all_to_all(chunks, ('ctx', 'exp'), split_axis=0, concat_axis=0, tiled...]
    all_to_all x4 -> x3, starting transfers between devices: 30.1 us -> 14.7 us  [exchange(): return lax.all_to_all(chunks, axis, split_axis=0, concat_axis=0, tiled=True)]
    ppermute x8 -> x7, starting transfers between devices: 31.3 us -> 21 us  [swap(): return lax.ppermute(value, 'ctx', [(i, i ^ 1) for i in range(count)])]
    all_to_all x0 -> x1, waiting for transfers between devices: none -> 8.93 us  [exchange_pairs(): lax.all_to_all(chunks, ('ctx', 'exp'), split_axis=0, concat_axis=0, tiled...]
    all_to_all x4 -> x3, waiting for transfers between devices: 28.4 us -> 23.5 us  [exchange(): return lax.all_to_all(chunks, axis, split_axis=0, concat_axis=0, tiled=True)]
    all_to_all x1, waiting for transfers between devices: 8.84 us -> 11.7 us  [exchange_chips(): lax.all_to_all(chunks, 'ctx', split_axis=0, concat_axis=0, tiled=True, ax...]
  transfers between devices with their start and end apart: 13 -> 12, of which waited for: 7 -> 7; matrix products, arithmetic and copies ran while one was open for 1% -> 0% of each run, Pallas kernels for 3% -> 3%
where the time goes in v5:
time: 149 us; the launch traced here: 148 us
  starting transfers between devices  59.4 us (40%)
  waiting for transfers between devices  45.5 us (31%)
  blocking collectives  24.8 us (17%)
  Pallas kernels  11 us (7%)
  local copies, waits for them, and re-layouts  4.79 us (3%)
    all_to_all x2, blocking collectives, exchange_chips(): lax.all_to_all(chunks, 'ctx', split_axis=0, concat_axis=0, tiled=True, ax...  24.8 us
    all_to_all x3, waiting for transfers between devices, exchange(): return lax.all_to_all(chunks, axis, split_axis=0, concat_axis=0, tiled=True)  23.5 us
    ppermute x7, starting transfers between devices, swap(): return lax.ppermute(value, 'ctx', [(i, i ^ 1) for i in range(count)])  21 us
    all_to_all x1, starting transfers between devices, exchange_pairs(): lax.all_to_all(chunks, ('ctx', 'exp'), split_axis=0, concat_axis=0, tiled...  16.9 us
    all_to_all x3, starting transfers between devices, exchange(): return lax.all_to_all(chunks, axis, split_axis=0, concat_axis=0, tiled=True)  14.7 us
    all_to_all x1, waiting for transfers between devices, exchange_chips(): lax.all_to_all(chunks, 'ctx', split_axis=0, concat_axis=0, tiled=True, ax...  11.7 us
    pallas_call x12, Pallas kernels, local_kernel(): pl.pallas_call(kernel, out_shape=out_shape, in_specs=[pl.BlockSpec(memory...  11 us
    all_to_all x1, waiting for transfers between devices, exchange_pairs(): lax.all_to_all(chunks, ('ctx', 'exp'), split_axis=0, concat_axis=0, tiled...  8.93 us
  transfers between devices with their start and end apart: 12, of which 7 were waited for; matrix products, arithmetic and copies ran while one was open for 0% of the time, Pallas kernels for 3%

profile of v5, /device:TPU:1, one launch (start us, length us, event | category | flops | bytes accessed | tf_op | source)
XLA Modules:
  0.0 148.3 jit_solution(701620676197019255)
XLA Ops:
  0.6 0.8 fusion.7
  1.4 0.7 shard_map.122
  2.1 0.0 copy-start
  2.1 0.9 copy-done
  3.0 0.8 shard_map.123
  3.9 0.0 copy-start.11
  3.9 16.9 %all-to-all-start = ((bf16[32,8,256]{2,1,0:T(8,128)(2,1)}), bf16[32,8,256]{2,1,0:T(8,128)(2,1)S(1)}, u32[]{:S(2)}, u32[]{:S(2)}) async-start(bf16[32,8,256]{2,1,0:T(8,128)(2,1)} %bitcast.6), calls=%async_computation | async-start | bytes 262144 | tf_op jit(solution)/shard_map/all_to_all | solution.py:40
  20.8 2.1 %collective-permute-start.1 = (bf16[224,2048]{1,0:T(8,128)(2,1)}, bf16[224,2048]{1,0:T(8,128)(2,1)S(1)}, u32[]{:S(2)}, u32[]{:S(2)}) collective-permute-start(bf16[224,2048]{1,0:T(8,128)(2,1)} %bitcast.49), channel_id=1, source_target_pairs={{0,16},{16,0},{32,48},{48,32},{64,80},{80,64},{96,112},{112,96},{1... | collective-permute-start | bytes 2752520 | tf_op jit(solution)/shard_map/ppermute | solution.py:47
  22.9 2.2 %collective-permute-start.2 = (bf16[224,2048]{1,0:T(8,128)(2,1)}, bf16[224,2048]{1,0:T(8,128)(2,1)S(1)}, u32[]{:S(2)}, u32[]{:S(2)}) collective-permute-start(bf16[224,2048]{1,0:T(8,128)(2,1)} %bitcast.51), channel_id=1, source_target_pairs={{0,16},{16,0},{32,48},{48,32},{64,80},{80,64},{96,112},{112,96},{1... | collective-permute-start | bytes 2752520 | tf_op jit(solution)/shard_map/ppermute | solution.py:47
  25.1 0.0 copy-done.11
  25.1 2.1 %collective-permute-start = (f32[8,224]{1,0:T(8,128)S(1)}, f32[8,224]{1,0:T(8,128)S(1)}, u32[]{:S(2)}, u32[]{:S(2)}) collective-permute-start(f32[8,224]{1,0:T(8,128)S(1)} %broadcast_in_dim.18.refs_2_), channel_id=1, source_target_pairs={{0,16},{16,0},{32,48},{48,32},{64,80},{80,64},{96,112},{112,96},{1... | collective-permute-start | bytes 21512 | tf_op jit(solution)/shard_map/ppermute | solution.py:47
  27.3 0.9 collective-permute-done.refs_3_
  28.2 8.9 %all-to-all-done = bf16[32,8,256]{2,1,0:T(8,128)(2,1)S(1)} async-done(((bf16[32,8,256]{2,1,0:T(8,128)(2,1)}), bf16[32,8,256]{2,1,0:T(8,128)(2,1)S(1)}, u32[]{:S(2)}, u32[]{:S(2)}) %all-to-all-start) | async-done | bytes 131104 | tf_op jit(solution)/shard_map/all_to_all | solution.py:40
  37.1 0.0 copy-start.2
  37.1 0.0 copy-start.3
  37.1 0.3 shard_map.124
  37.4 0.0 collective-permute-done.1.gate_pair
  37.4 0.0 collective-permute-done.2.up_pair
  37.4 0.9 copy-done.2
  38.3 0.3 copy-done.3
  38.6 1.7 %shard_map.125 = bf16[16,208,128]{2,1,0:T(8,128)(2,1)} custom-call(bf16[96,224]{1,0:T(8,128)(2,1)S(1)} %get-tuple-element.30.own_ref, bf16[96,224]{1,0:T(8,128)(2,1)S(1)} %get-tuple-element.31.pair_ref, bf16[16,128]{1,0:T(8,128)(2,1)S(1)} %get-tuple-element.32.square_ref, bf16[224,2048]{1,0:T(8,128)(2,1)S(1)} %bitcast.50, ...), custom_call_target="tpu_custom_call" | custom-call | tf_op jit(solution)/shard_map/pallas_call | solution.py:64
  40.2 6.9 %all-to-all-start.1 = ((bf16[16,208,128]{2,1,0:T(8,128)(2,1)}), bf16[16,208,128]{2,1,0:T(8,128)(2,1)S(1)}, u32[]{:S(2)}, u32[]{:S(2)}) async-start(bf16[16,208,128]{2,1,0:T(8,128)(2,1)} %shard_map.125), calls=%async_computation.1 | async-start | bytes 1703936 | tf_op jit(solution)/shard_map/all_to_all | solution.py:32
  47.1 0.0 copy-done.7
  47.1 2.6 %collective-permute-start.3 = (bf16[224,2048]{1,0:T(8,128)(2,1)S(1)}, bf16[224,2048]{1,0:T(8,128)(2,1)S(1)}, u32[]{:S(2)}, u32[]{:S(2)}) collective-permute-start(bf16[224,2048]{1,0:T(8,128)(2,1)S(1)} %bitcast.57), channel_id=1, source_target_pairs={{0,16},{16,0},{32,48},{48,32},{64,80},{80,64},{96,112},{112,96},{1... | collective-permute-start | bytes 2752520 | tf_op jit(solution)/shard_map/ppermute | solution.py:47
  49.7 11.7 %all-to-all-done.1.refs_0_ = bf16[16,208,128]{2,1,0:T(8,128)(2,1)S(1)} async-done(((bf16[16,208,128]{2,1,0:T(8,128)(2,1)}), bf16[16,208,128]{2,1,0:T(8,128)(2,1)S(1)}, u32[]{:S(2)}, u32[]{:S(2)}) %all-to-all-start.1) | async-done | bytes 852000 | tf_op jit(solution)/shard_map/all_to_all | solution.py:32
  61.4 0.1 shard_map.126
  61.5 12.6 %all_to_all.35 = bf16[16,96,128]{2,1,0:T(8,128)(2,1)S(1)} all-to-all(bf16[16,96,128]{2,1,0:T(8,128)(2,1)S(1)} %shard_map.126), channel_id=1, replica_groups={{0,32,64,96,128,160,192,224,256,288,320,352,384,416,448,480},{16,48,80,..., dimensions={0} | all-to-all | bytes 786432 | tf_op jit(solution)/shard_map/all_to_all | solution.py:32
  74.1 0.4 convolution_convert_fusion.1
  74.5 0.0 collective-permute-done.3
  74.5 0.4 convolution_convert_fusion
  75.0 0.0 copy-start.4
  75.0 0.7 pad.13
  75.7 3.6 %all-to-all-start.3 = ((bf16[16,8,512]{2,1,0:T(8,128)(2,1)}), bf16[16,8,512]{2,1,0:T(8,128)(2,1)S(1)}, u32[]{:S(2)}, u32[]{:S(2)}) async-start(bf16[16,8,512]{2,1,0:T(8,128)(2,1)} %pad.13), calls=%async_computation.3 | async-start | bytes 262144 | tf_op jit(solution)/shard_map/all_to_all | solution.py:26
  79.4 0.0 copy-done.4
  79.4 4.0 %collective-permute-start.4 = (bf16[224,512]{1,0:T(8,128)(2,1)S(1)}, bf16[224,512]{1,0:T(8,128)(2,1)S(1)}, u32[]{:S(2)}, u32[]{:S(2)}) collective-permute-start(bf16[224,512]{1,0:T(8,128)(2,1)S(1)} %copy-done.4), channel_id=1, source_target_pairs={{0,16},{16,0},{32,48},{48,32},{64,80},{80,64},{96,112},{112,96},{1... | collective-permute-start | bytes 688136 | tf_op jit(solution)/shard_map/ppermute | solution.py:47
  83.4 0.1 pad_add_fusion.place_ref
  83.4 0.0 copy-done.9
  83.4 0.0 copy-done.10
  83.5 0.0 copy-start.6
  83.5 0.7 copy-done.5
  84.2 0.0 copy-done.6
  84.2 1.4 shard_map.127
  85.6 0.0 collective-permute-done.4.pair_ref
  85.6 5.7 %all-to-all-done.3 = bf16[16,8,512]{2,1,0:T(8,128)(2,1)S(1)} async-done(((bf16[16,8,512]{2,1,0:T(8,128)(2,1)}), bf16[16,8,512]{2,1,0:T(8,128)(2,1)S(1)}, u32[]{:S(2)}, u32[]{:S(2)}) %all-to-all-start.3) | async-done | bytes 131104 | tf_op jit(solution)/shard_map/all_to_all | solution.py:26
  91.3 0.0 copy-done.1
  91.3 1.4 shard_map.128
  92.7 7.5 %all-to-all-start.4 = ((bf16[32,8,512]{2,1,0:T(8,128)(2,1)}), bf16[32,8,512]{2,1,0:T(8,128)(2,1)S(1)}, u32[]{:S(2)}, u32[]{:S(2)}) async-start(bf16[32,8,512]{2,1,0:T(8,128)(2,1)} %bitcast.13), calls=%async_computation.4 | async-start | bytes 524288 | tf_op jit(solution)/shard_map/all_to_all | solution.py:26
  100.2 0.0 copy-start.8
  100.2 2.4 %collective-permute-start.5 = (bf16[128,256]{1,0:T(8,128)(2,1)S(1)}, bf16[128,256]{1,0:T(8,128)(2,1)S(1)}, u32[]{:S(2)}, u32[]{:S(2)}) collective-permute-start(bf16[128,256]{1,0:T(8,128)(2,1)S(1)} %slice.4), channel_id=1, source_target_pairs={{0,16},{16,0},{32,48},{48,32},{64,80},{80,64},{96,112},{112,96},{1... | collective-permute-start | bytes 196616 | tf_op jit(solution)/shard_map/ppermute | solution.py:47
  102.6 6.6 %all-to-all-done.4.part_ref = bf16[32,8,512]{2,1,0:T(8,128)(2,1)S(1)} async-done(((bf16[32,8,512]{2,1,0:T(8,128)(2,1)}), bf16[32,8,512]{2,1,0:T(8,128)(2,1)S(1)}, u32[]{:S(2)}, u32[]{:S(2)}) %all-to-all-start.4) | async-done | bytes 262176 | tf_op jit(solution)/shard_map/all_to_all | solution.py:26
  109.2 0.8 shard_map.129
  110.0 0.0 collective-permute-done.5.rest_ref
  110.0 3.5 %all-to-all-start.5 = ((bf16[16,8,512]{2,1,0:T(8,128)(2,1)}), bf16[16,8,512]{2,1,0:T(8,128)(2,1)S(1)}, u32[]{:S(2)}, u32[]{:S(2)}) async-start(bf16[16,8,512]{2,1,0:T(8,128)(2,1)} %shard_map.129), calls=%async_computation.5 | async-start | bytes 262144 | tf_op jit(solution)/shard_map/all_to_all | solution.py:26
  113.5 0.0 copy-done.8
  113.5 0.1 copy.16
  113.6 1.0 shard_map.131
  114.6 11.2 %all-to-all-done.5 = bf16[16,8,512]{2,1,0:T(8,128)(2,1)S(1)} async-done(((bf16[16,8,512]{2,1,0:T(8,128)(2,1)}), bf16[16,8,512]{2,1,0:T(8,128)(2,1)S(1)}, u32[]{:S(2)}, u32[]{:S(2)}) %all-to-all-start.5) | async-done | bytes 131104 | tf_op jit(solution)/shard_map/all_to_all | solution.py:26
  125.8 0.2 shard_map.130
  125.9 12.3 %all_to_all.36 = bf16[16,32,512]{2,1,0:T(8,128)(2,1)S(1)} all-to-all(bf16[16,32,512]{2,1,0:T(8,128)(2,1)S(1)} %shard_map.130), channel_id=1, replica_groups={{0,32,64,96,128,160,192,224,256,288,320,352,384,416,448,480},{16,48,80,..., dimensions={0} | all-to-all | bytes 1048576 | tf_op jit(solution)/shard_map/all_to_all | solution.py:32
  138.2 5.6 %collective-permute-start.6 = (bf16[512,512]{1,0:T(8,128)(2,1)S(1)}, bf16[512,512]{1,0:T(8,128)(2,1)S(1)}, u32[]{:S(2)}, u32[]{:S(2)}) collective-permute-start(bf16[512,512]{1,0:T(8,128)(2,1)S(1)} %bitcast.40), channel_id=1, source_target_pairs={{0,16},{16,0},{32,48},{48,32},{64,80},{80,64},{96,112},{112,96},{1... | collective-permute-start | bytes 1572872 | tf_op jit(solution)/shard_map/ppermute | solution.py:47
  143.8 1.0 shard_map.132
  144.8 0.5 collective-permute-done.6.keys_ref
  145.4 1.8 %shard_map.133 = bf16[512,512]{1,0:T(8,128)(2,1)S(1)} custom-call(bf16[512,512]{1,0:T(8,128)(2,1)S(1)} %bitcast.39, bf16[512,512]{1,0:T(8,128)(2,1)S(1)} %collective-permute-done.6.keys_ref, f32[128,512]{1,0:T(8,128)S(1)} %get-tuple-element.48.seen_ref, f32[512,128]{1,0:T(8,128)S(1)} %get-tuple-element.50.stats_ref, f32[512,512]{1,0:T(8,128)S(1)} %get-tuple-element.51.mixed_ref), custom_call_target="tpu_custom_call" | custom-call | tf_op jit(solution)/shard_map/pallas_call | solution.py:64
  147.1 1.2 copy.28
  (11 shorter events, 0.1 us)
Async XLA Ops:
  2.1 0.9 copy-start
  3.9 21.2 %copy-start.11 = (f32[224]{0:T(256)S(1)}, f32[224]{0:T(256)}, u32[]{:S(2)}) copy-start(f32[224]{0:T(256)} %param.14) | copy-start | bytes 2692
  3.9 33.3 %all-to-all-start = ((bf16[32,8,256]{2,1,0:T(8,128)(2,1)}), bf16[32,8,256]{2,1,0:T(8,128)(2,1)S(1)}, u32[]{:S(2)}, u32[]{:S(2)}) async-start(bf16[32,8,256]{2,1,0:T(8,128)(2,1)} %bitcast.6), calls=%async_computation | async-start | bytes 262144 | tf_op jit(solution)/shard_map/all_to_all | solution.py:40
  20.8 16.7 %collective-permute-start.1 = (bf16[224,2048]{1,0:T(8,128)(2,1)}, bf16[224,2048]{1,0:T(8,128)(2,1)S(1)}, u32[]{:S(2)}, u32[]{:S(2)}) collective-permute-start(bf16[224,2048]{1,0:T(8,128)(2,1)} %bitcast.49), channel_id=1, source_target_pairs={{0,16},{16,0},{32,48},{48,32},{64,80},{80,64},{96,112},{112,96},{1... | collective-permute-start | bytes 2752520 | tf_op jit(solution)/shard_map/ppermute | solution.py:47
  22.9 14.5 %collective-permute-start.2 = (bf16[224,2048]{1,0:T(8,128)(2,1)}, bf16[224,2048]{1,0:T(8,128)(2,1)S(1)}, u32[]{:S(2)}, u32[]{:S(2)}) collective-permute-start(bf16[224,2048]{1,0:T(8,128)(2,1)} %bitcast.51), channel_id=1, source_target_pairs={{0,16},{16,0},{32,48},{48,32},{64,80},{80,64},{96,112},{112,96},{1... | collective-permute-start | bytes 2752520 | tf_op jit(solution)/shard_map/ppermute | solution.py:47
  25.1 3.1 %collective-permute-start = (f32[8,224]{1,0:T(8,128)S(1)}, f32[8,224]{1,0:T(8,128)S(1)}, u32[]{:S(2)}, u32[]{:S(2)}) collective-permute-start(f32[8,224]{1,0:T(8,128)S(1)} %broadcast_in_dim.18.refs_2_), channel_id=1, source_target_pairs={{0,16},{16,0},{32,48},{48,32},{64,80},{80,64},{96,112},{112,96},{1... | collective-permute-start | bytes 21512 | tf_op jit(solution)/shard_map/ppermute | solution.py:47
  37.1 1.2 copy-start.2
  37.1 1.5 copy-start.3
  40.2 6.9 %copy-start.7 = (bf16[1,2048,224]{1,2,0:T(8,128)(2,1)S(1)}, bf16[1,2048,224]{1,2,0:T(8,128)(2,1)}, u32[]{:S(2)}) copy-start(bf16[1,2048,224]{1,2,0:T(8,128)(2,1)} %param.17) | copy-start | bytes 2752516
  40.2 21.1 %all-to-all-start.1 = ((bf16[16,208,128]{2,1,0:T(8,128)(2,1)}), bf16[16,208,128]{2,1,0:T(8,128)(2,1)S(1)}, u32[]{:S(2)}, u32[]{:S(2)}) async-start(bf16[16,208,128]{2,1,0:T(8,128)(2,1)} %shard_map.125), calls=%async_computation.1 | async-start | bytes 1703936 | tf_op jit(solution)/shard_map/all_to_all | solution.py:32
  47.1 27.4 %collective-permute-start.3 = (bf16[224,2048]{1,0:T(8,128)(2,1)S(1)}, bf16[224,2048]{1,0:T(8,128)(2,1)S(1)}, u32[]{:S(2)}, u32[]{:S(2)}) collective-permute-start(bf16[224,2048]{1,0:T(8,128)(2,1)S(1)} %bitcast.57), channel_id=1, source_target_pairs={{0,16},{16,0},{32,48},{48,32},{64,80},{80,64},{96,112},{112,96},{1... | collective-permute-start | bytes 2752520 | tf_op jit(solution)/shard_map/ppermute | solution.py:47
  75.0 4.4 %copy-start.4 = (bf16[224,512]{1,0:T(8,128)(2,1)S(1)}, bf16[224,512]{1,0:T(8,128)(2,1)}, u32[]{:S(2)}) copy-start(bf16[224,512]{1,0:T(8,128)(2,1)} %own_ref.1) | copy-start | bytes 688132
  75.7 7.7 %copy-start.9 = (s32[8,32,8]{1,2,0:T(8,128)S(1)}, s32[8,32,8]{1,2,0:T(8,128)}, u32[]{:S(2)}) copy-start(s32[8,32,8]{1,2,0:T(8,128)} %param.12) | copy-start | bytes 24580
  75.7 7.7 %copy-start.10 = (f32[8,32,8]{1,2,0:T(8,128)S(1)}, f32[8,32,8]{1,2,0:T(8,128)}, u32[]{:S(2)}) copy-start(f32[8,32,8]{1,2,0:T(8,128)} %param.13) | copy-start | bytes 24580
  75.7 15.6 %copy-start.1 = (bf16[8,32,224]{2,1,0:T(8,128)(2,1)S(1)}, bf16[8,32,224]{2,1,0:T(8,128)(2,1)}, u32[]{:S(2)}) copy-start(bf16[8,32,224]{2,1,0:T(8,128)(2,1)} %param.11) | copy-start | bytes 344068
  75.7 15.5 %all-to-all-start.3 = ((bf16[16,8,512]{2,1,0:T(8,128)(2,1)}), bf16[16,8,512]{2,1,0:T(8,128)(2,1)S(1)}, u32[]{:S(2)}, u32[]{:S(2)}) async-start(bf16[16,8,512]{2,1,0:T(8,128)(2,1)} %pad.13), calls=%async_computation.3 | async-start | bytes 262144 | tf_op jit(solution)/shard_map/all_to_all | solution.py:26
  79.4 6.2 %collective-permute-start.4 = (bf16[224,512]{1,0:T(8,128)(2,1)S(1)}, bf16[224,512]{1,0:T(8,128)(2,1)S(1)}, u32[]{:S(2)}, u32[]{:S(2)}) collective-permute-start(bf16[224,512]{1,0:T(8,128)(2,1)S(1)} %copy-done.4), channel_id=1, source_target_pairs={{0,16},{16,0},{32,48},{48,32},{64,80},{80,64},{96,112},{112,96},{1... | collective-permute-start | bytes 688136 | tf_op jit(solution)/shard_map/ppermute | solution.py:47
  83.4 0.7 copy-start.5
  83.5 0.7 copy-start.6
  92.7 16.5 %all-to-all-start.4 = ((bf16[32,8,512]{2,1,0:T(8,128)(2,1)}), bf16[32,8,512]{2,1,0:T(8,128)(2,1)S(1)}, u32[]{:S(2)}, u32[]{:S(2)}) async-start(bf16[32,8,512]{2,1,0:T(8,128)(2,1)} %bitcast.13), calls=%async_computation.4 | async-start | bytes 524288 | tf_op jit(solution)/shard_map/all_to_all | solution.py:26
  100.2 13.3 %copy-start.8 = (bf16[128,4,512]{2,1,0:T(4,128)(2,1)S(1)}, bf16[128,4,512]{2,1,0:T(4,128)(2,1)}, u32[]{:S(2)}) copy-start(bf16[128,4,512]{2,1,0:T(4,128)(2,1)} %param.20) | copy-start | bytes 1572868
  100.2 9.8 %collective-permute-start.5 = (bf16[128,256]{1,0:T(8,128)(2,1)S(1)}, bf16[128,256]{1,0:T(8,128)(2,1)S(1)}, u32[]{:S(2)}, u32[]{:S(2)}) collective-permute-start(bf16[128,256]{1,0:T(8,128)(2,1)S(1)} %slice.4), channel_id=1, source_target_pairs={{0,16},{16,0},{32,48},{48,32},{64,80},{80,64},{96,112},{112,96},{1... | collective-permute-start | bytes 196616 | tf_op jit(solution)/shard_map/ppermute | solution.py:47
  110.0 15.8 %all-to-all-start.5 = ((bf16[16,8,512]{2,1,0:T(8,128)(2,1)}), bf16[16,8,512]{2,1,0:T(8,128)(2,1)S(1)}, u32[]{:S(2)}, u32[]{:S(2)}) async-start(bf16[16,8,512]{2,1,0:T(8,128)(2,1)} %shard_map.129), calls=%async_computation.5 | async-start | bytes 262144 | tf_op jit(solution)/shard_map/all_to_all | solution.py:26
  138.2 7.1 %collective-permute-start.6 = (bf16[512,512]{1,0:T(8,128)(2,1)S(1)}, bf16[512,512]{1,0:T(8,128)(2,1)S(1)}, u32[]{:S(2)}, u32[]{:S(2)}) collective-permute-start(bf16[512,512]{1,0:T(8,128)(2,1)S(1)} %bitcast.40), channel_id=1, source_target_pairs={{0,16},{16,0},{32,48},{48,32},{64,80},{80,64},{96,112},{112,96},{1... | collective-permute-start | bytes 1572872 | tf_op jit(solution)/shard_map/ppermute | solution.py:47

commit v6 on v5

--- a/solution.py
+++ b/solution.py
@@ -105,9 +105,15 @@
         ref[...] = ((index <= query) & (query <= end)).astype(f32)
 
 
-def routing_kernel(core_ref, expert_ref, placed_ref, table_ref):
+def dispatch_kernel(exp_count, core_ref, routes_hbm, rows_hbm, table_ref, out_ref, routes_ref, rows_ref, sems):
+    routes_copy = pltpu.make_async_copy(routes_hbm, routes_ref, sems.at[0])
+    copy = pltpu.make_async_copy(rows_hbm, rows_ref, sems.at[1])
+    routes_copy.start()
+    copy.start()
     core = core_ref[0].astype(f32)
-    expert = column(expert_ref[...])
+    routes_copy.wait()
+    routes = routes_ref[...]
+    expert = column(jnp.max(jnp.where(routes < exp_count, routes, -1), axis=1).astype(f32))
     tokens = expert.shape[0]
     lane = iota((tokens, 128), 1).astype(f32)
     picked = expert == lane
@@ -115,21 +121,18 @@
     rank = dot(earlier, picked.astype(bf16))
     rank = jnp.sum(jnp.where(picked, rank, 0.0), axis=1, keepdims=True)
 
-    count = placed_ref.shape[0]
+    count = out_ref.shape[0]
     part = jnp.where(rank >= PART, 1.0, 0.0)
     valid = (expert >= 0) & (rank < CAP)
     slot = expert * PAD + rank - part * PART
     slot_rows = jnp.where(valid, part * (count // 2) + slot, -1.0)
     slot_rows = jnp.transpose(jnp.broadcast_to(slot_rows, (tokens, count)))
-    placed_ref[...] = (slot_rows == iota((count, tokens), 0).astype(f32)).astype(bf16)
+    placed = (slot_rows == iota((count, tokens), 0).astype(f32)).astype(bf16)
     wanted = jnp.where(lane == 0, core, 1.0 - core)
     table_ref[...] = jnp.where(valid & (part == wanted), slot, -1.0)
-
-
-def dispatch_kernel(placed_ref, rows_ref, out_ref):
-    placed = placed_ref[...]
     width = rows_ref.shape[1]
-    out_ref[:, width:] = jnp.zeros((placed.shape[0], WIDE - width), bf16)
+    out_ref[:, width:] = jnp.zeros((count, WIDE - width), bf16)
+    copy.wait()
     out_ref[:, :width] = dot(placed, rows_ref[...]).astype(bf16)
 
 
@@ -285,16 +288,23 @@
 
     shape = jax.ShapeDtypeStruct
     near = routes < exp_count
-    expert = jnp.max(jnp.where(near, routes, -1), axis=2).astype(f32)
+    routes_by_top = routes.transpose(0, 2, 1)
     both = 2 * padded
-    placed, table = local_kernel(
-        routing_kernel,
-        (shape((both, tokens), bf16), shape((tokens, 128), f32)),
+    both = 2 * padded
+    table, dispatched = local_kernel(
+        lambda *refs: dispatch_kernel(exp_count, *refs),
+        (shape((tokens, 128), f32), shape((both, WIDE), bf16)),
         core.reshape(1),
-        expert,
-        spaces=[pltpu.SMEM, pltpu.VMEM],
-    )
-    dispatched = local_kernel(dispatch_kernel, shape((both, WIDE), bf16), placed, rows)
+        routes_by_top,
+        rows,
+        spaces=[pltpu.SMEM, pl.ANY, pl.ANY],
+        grant=60,
+        scratch_shapes=[
+            pltpu.VMEM(routes_by_top.shape, jnp.int32),
+            pltpu.VMEM(rows.shape, bf16),
+            pltpu.SemaphoreType.DMA((2,)),
+        ],
+    )
     own = (gate_weight[0], up_weight[0], down_weight[0].T, latent_weight, moe_gain)
     late = (gates, latent_gain, subtree_end)
     dispatched, own, late = lax.optimization_barrier((dispatched, own, late))

time: 149 us -> 148 us (level)
    pallas_call x12 -> x11, Pallas kernels: 11 us -> 11.9 us  [local_kernel(): pl.pallas_call(kernel, out_shape=out_shape, in_specs=[pl.BlockSpec(memory...]
where the time goes in v6:
time: 148 us; the launch traced here: 147 us
  starting transfers between devices  59.3 us (40%)
  waiting for transfers between devices  45.5 us (31%)
  blocking collectives  24.8 us (17%)
  Pallas kernels  11.9 us (8%)
  local copies, waits for them, and re-layouts  3.9 us (3%)
    all_to_all x2, blocking collectives, exchange_chips(): lax.all_to_all(chunks, 'ctx', split_axis=0, concat_axis=0, tiled=True, ax...  24.8 us
    all_to_all x3, waiting for transfers between devices, exchange(): return lax.all_to_all(chunks, axis, split_axis=0, concat_axis=0, tiled=True)  23.5 us
    ppermute x7, starting transfers between devices, swap(): return lax.ppermute(value, 'ctx', [(i, i ^ 1) for i in range(count)])  21 us
    all_to_all x1, starting transfers between devices, exchange_pairs(): lax.all_to_all(chunks, ('ctx', 'exp'), split_axis=0, concat_axis=0, tiled...  16.8 us
    all_to_all x3, starting transfers between devices, exchange(): return lax.all_to_all(chunks, axis, split_axis=0, concat_axis=0, tiled=True)  14.7 us
    pallas_call x11, Pallas kernels, local_kernel(): pl.pallas_call(kernel, out_shape=out_shape, in_specs=[pl.BlockSpec(memory...  11.9 us
    all_to_all x1, waiting for transfers between devices, exchange_chips(): lax.all_to_all(chunks, 'ctx', split_axis=0, concat_axis=0, tiled=True, ax...  11.6 us
    all_to_all x1, waiting for transfers between devices, exchange_pairs(): lax.all_to_all(chunks, ('ctx', 'exp'), split_axis=0, concat_axis=0, tiled...  8.93 us
  transfers between devices with their start and end apart: 12, of which 7 were waited for; matrix products, arithmetic and copies ran while one was open for 0% of the time, Pallas kernels for 3%

profile of v6, /device:TPU:1, one launch (start us, length us, event | category | flops | bytes accessed | tf_op | source)
XLA Modules:
  0.0 147.4 jit_solution(4130028893741958710)
XLA Ops:
  0.6 2.4 %shard_map.122 = (f32[256,128]{1,0:T(8,128)}, bf16[256,256]{1,0:T(8,128)(2,1)}) custom-call(s32[1]{0:T(128)} %bitcast.refs_0_, s32[8,8,32]{2,1,0:T(8,128)} %bitcast.62, bf16[256,224]{1,0:T(8,128)(2,1)} %bitcast.47), custom_call_target="tpu_custom_call" | custom-call | tf_op jit(solution)/shard_map/pallas_call | solution.py:64
  3.0 0.0 copy-start.11
  3.0 16.8 %all-to-all-start = ((bf16[32,8,256]{2,1,0:T(8,128)(2,1)}), bf16[32,8,256]{2,1,0:T(8,128)(2,1)S(1)}, u32[]{:S(2)}, u32[]{:S(2)}) async-start(bf16[32,8,256]{2,1,0:T(8,128)(2,1)} %bitcast.63), calls=%async_computation | async-start | bytes 262144 | tf_op jit(solution)/shard_map/all_to_all | solution.py:40
  19.8 2.1 %collective-permute-start.1 = (bf16[224,2048]{1,0:T(8,128)(2,1)}, bf16[224,2048]{1,0:T(8,128)(2,1)S(1)}, u32[]{:S(2)}, u32[]{:S(2)}) collective-permute-start(bf16[224,2048]{1,0:T(8,128)(2,1)} %bitcast.50), channel_id=1, source_target_pairs={{0,16},{16,0},{32,48},{48,32},{64,80},{80,64},{96,112},{112,96},{1... | collective-permute-start | bytes 2752520 | tf_op jit(solution)/shard_map/ppermute | solution.py:47
  22.0 2.2 %collective-permute-start.2 = (bf16[224,2048]{1,0:T(8,128)(2,1)}, bf16[224,2048]{1,0:T(8,128)(2,1)S(1)}, u32[]{:S(2)}, u32[]{:S(2)}) collective-permute-start(bf16[224,2048]{1,0:T(8,128)(2,1)} %bitcast.52), channel_id=1, source_target_pairs={{0,16},{16,0},{32,48},{48,32},{64,80},{80,64},{96,112},{112,96},{1... | collective-permute-start | bytes 2752520 | tf_op jit(solution)/shard_map/ppermute | solution.py:47
  24.2 0.0 copy-done.11
  24.2 2.1 %collective-permute-start = (f32[8,224]{1,0:T(8,128)S(1)}, f32[8,224]{1,0:T(8,128)S(1)}, u32[]{:S(2)}, u32[]{:S(2)}) collective-permute-start(f32[8,224]{1,0:T(8,128)S(1)} %broadcast_in_dim.13.refs_2_), channel_id=1, source_target_pairs={{0,16},{16,0},{32,48},{48,32},{64,80},{80,64},{96,112},{112,96},{1... | collective-permute-start | bytes 21512 | tf_op jit(solution)/shard_map/ppermute | solution.py:47
  26.3 0.9 collective-permute-done.refs_3_
  27.2 8.9 %all-to-all-done = bf16[32,8,256]{2,1,0:T(8,128)(2,1)S(1)} async-done(((bf16[32,8,256]{2,1,0:T(8,128)(2,1)}), bf16[32,8,256]{2,1,0:T(8,128)(2,1)S(1)}, u32[]{:S(2)}, u32[]{:S(2)}) %all-to-all-start) | async-done | bytes 131104 | tf_op jit(solution)/shard_map/all_to_all | solution.py:40
  36.2 0.0 copy-start.1
  36.2 0.0 copy-start.2
  36.2 0.3 shard_map.123
  36.5 0.0 collective-permute-done.1.gate_pair
  36.5 0.0 collective-permute-done.2.up_pair
  36.5 0.9 copy-done.1
  37.4 0.3 copy-done.2
  37.6 1.7 %shard_map.124 = bf16[16,208,128]{2,1,0:T(8,128)(2,1)} custom-call(bf16[96,224]{1,0:T(8,128)(2,1)S(1)} %get-tuple-element.30.own_ref, bf16[96,224]{1,0:T(8,128)(2,1)S(1)} %get-tuple-element.31.pair_ref, bf16[16,128]{1,0:T(8,128)(2,1)S(1)} %get-tuple-element.32.square_ref, bf16[224,2048]{1,0:T(8,128)(2,1)S(1)} %bitcast.51, ...), custom_call_target="tpu_custom_call" | custom-call | tf_op jit(solution)/shard_map/pallas_call | solution.py:64
  39.3 0.0 copy-start.7
  39.3 6.9 %all-to-all-start.1 = ((bf16[16,208,128]{2,1,0:T(8,128)(2,1)}), bf16[16,208,128]{2,1,0:T(8,128)(2,1)S(1)}, u32[]{:S(2)}, u32[]{:S(2)}) async-start(bf16[16,208,128]{2,1,0:T(8,128)(2,1)} %shard_map.124), calls=%async_computation.1 | async-start | bytes 1703936 | tf_op jit(solution)/shard_map/all_to_all | solution.py:32
  46.2 0.0 copy-done.7
  46.2 2.6 %collective-permute-start.3 = (bf16[224,2048]{1,0:T(8,128)(2,1)S(1)}, bf16[224,2048]{1,0:T(8,128)(2,1)S(1)}, u32[]{:S(2)}, u32[]{:S(2)}) collective-permute-start(bf16[224,2048]{1,0:T(8,128)(2,1)S(1)} %bitcast.58), channel_id=1, source_target_pairs={{0,16},{16,0},{32,48},{48,32},{64,80},{80,64},{96,112},{112,96},{1... | collective-permute-start | bytes 2752520 | tf_op jit(solution)/shard_map/ppermute | solution.py:47
  48.8 11.6 %all-to-all-done.1.refs_0_ = bf16[16,208,128]{2,1,0:T(8,128)(2,1)S(1)} async-done(((bf16[16,208,128]{2,1,0:T(8,128)(2,1)}), bf16[16,208,128]{2,1,0:T(8,128)(2,1)S(1)}, u32[]{:S(2)}, u32[]{:S(2)}) %all-to-all-start.1) | async-done | bytes 852000 | tf_op jit(solution)/shard_map/all_to_all | solution.py:32
  60.4 0.1 shard_map.125
  60.6 12.5 %all_to_all.35 = bf16[16,96,128]{2,1,0:T(8,128)(2,1)S(1)} all-to-all(bf16[16,96,128]{2,1,0:T(8,128)(2,1)S(1)} %shard_map.125), channel_id=1, replica_groups={{0,32,64,96,128,160,192,224,256,288,320,352,384,416,448,480},{16,48,80,..., dimensions={0} | all-to-all | bytes 786432 | tf_op jit(solution)/shard_map/all_to_all | solution.py:32
  73.1 0.4 convolution_convert_fusion.1
  73.5 0.0 collective-permute-done.3
  73.5 0.4 convolution_convert_fusion
  74.0 0.0 copy-start.9
  74.0 0.0 copy-start.10
  74.1 0.0 copy-start.4
  74.1 0.7 pad.13
  74.8 3.6 %all-to-all-start.3 = ((bf16[16,8,512]{2,1,0:T(8,128)(2,1)}), bf16[16,8,512]{2,1,0:T(8,128)(2,1)S(1)}, u32[]{:S(2)}, u32[]{:S(2)}) async-start(bf16[16,8,512]{2,1,0:T(8,128)(2,1)} %pad.13), calls=%async_computation.3 | async-start | bytes 262144 | tf_op jit(solution)/shard_map/all_to_all | solution.py:26
  78.4 0.0 copy-done.4
  78.4 4.0 %collective-permute-start.4 = (bf16[224,512]{1,0:T(8,128)(2,1)S(1)}, bf16[224,512]{1,0:T(8,128)(2,1)S(1)}, u32[]{:S(2)}, u32[]{:S(2)}) collective-permute-start(bf16[224,512]{1,0:T(8,128)(2,1)S(1)} %copy-done.4), channel_id=1, source_target_pairs={{0,16},{16,0},{32,48},{48,32},{64,80},{80,64},{96,112},{112,96},{1... | collective-permute-start | bytes 688136 | tf_op jit(solution)/shard_map/ppermute | solution.py:47
  82.4 0.1 pad_add_fusion.place_ref
  82.5 0.0 copy-done.9
  82.5 0.0 copy-done.10
  82.5 0.0 copy-start.6
  82.5 0.7 copy-done.5
  83.2 0.0 copy-done.6
  83.2 1.4 shard_map.126
  84.6 0.0 collective-permute-done.4.pair_ref
  84.6 5.7 %all-to-all-done.3 = bf16[16,8,512]{2,1,0:T(8,128)(2,1)S(1)} async-done(((bf16[16,8,512]{2,1,0:T(8,128)(2,1)}), bf16[16,8,512]{2,1,0:T(8,128)(2,1)S(1)}, u32[]{:S(2)}, u32[]{:S(2)}) %all-to-all-start.3) | async-done | bytes 131104 | tf_op jit(solution)/shard_map/all_to_all | solution.py:26
  90.3 0.0 copy-done
  90.3 0.0 copy-done.3
  90.3 1.4 shard_map.127
  91.7 7.5 %all-to-all-start.4 = ((bf16[32,8,512]{2,1,0:T(8,128)(2,1)}), bf16[32,8,512]{2,1,0:T(8,128)(2,1)S(1)}, u32[]{:S(2)}, u32[]{:S(2)}) async-start(bf16[32,8,512]{2,1,0:T(8,128)(2,1)} %bitcast.14), calls=%async_computation.4 | async-start | bytes 524288 | tf_op jit(solution)/shard_map/all_to_all | solution.py:26
  99.2 0.0 copy-start.8
  99.3 2.4 %collective-permute-start.5 = (bf16[128,256]{1,0:T(8,128)(2,1)S(1)}, bf16[128,256]{1,0:T(8,128)(2,1)S(1)}, u32[]{:S(2)}, u32[]{:S(2)}) collective-permute-start(bf16[128,256]{1,0:T(8,128)(2,1)S(1)} %slice.4), channel_id=1, source_target_pairs={{0,16},{16,0},{32,48},{48,32},{64,80},{80,64},{96,112},{112,96},{1... | collective-permute-start | bytes 196616 | tf_op jit(solution)/shard_map/ppermute | solution.py:47
  101.7 6.6 %all-to-all-done.4.part_ref = bf16[32,8,512]{2,1,0:T(8,128)(2,1)S(1)} async-done(((bf16[32,8,512]{2,1,0:T(8,128)(2,1)}), bf16[32,8,512]{2,1,0:T(8,128)(2,1)S(1)}, u32[]{:S(2)}, u32[]{:S(2)}) %all-to-all-start.4) | async-done | bytes 262176 | tf_op jit(solution)/shard_map/all_to_all | solution.py:26
  108.3 0.8 shard_map.128
  109.0 0.0 collective-permute-done.5.rest_ref
  109.0 3.5 %all-to-all-start.5 = ((bf16[16,8,512]{2,1,0:T(8,128)(2,1)}), bf16[16,8,512]{2,1,0:T(8,128)(2,1)S(1)}, u32[]{:S(2)}, u32[]{:S(2)}) async-start(bf16[16,8,512]{2,1,0:T(8,128)(2,1)} %shard_map.128), calls=%async_computation.5 | async-start | bytes 262144 | tf_op jit(solution)/shard_map/all_to_all | solution.py:26
  112.6 0.0 copy-done.8
  112.6 0.1 copy.16
  112.7 1.0 shard_map.130
  113.6 11.2 %all-to-all-done.5 = bf16[16,8,512]{2,1,0:T(8,128)(2,1)S(1)} async-done(((bf16[16,8,512]{2,1,0:T(8,128)(2,1)}), bf16[16,8,512]{2,1,0:T(8,128)(2,1)S(1)}, u32[]{:S(2)}, u32[]{:S(2)}) %all-to-all-start.5) | async-done | bytes 131104 | tf_op jit(solution)/shard_map/all_to_all | solution.py:26
  124.8 0.2 shard_map.129
  125.0 12.3 %all_to_all.36 = bf16[16,32,512]{2,1,0:T(8,128)(2,1)S(1)} all-to-all(bf16[16,32,512]{2,1,0:T(8,128)(2,1)S(1)} %shard_map.129), channel_id=1, replica_groups={{0,32,64,96,128,160,192,224,256,288,320,352,384,416,448,480},{16,48,80,..., dimensions={0} | all-to-all | bytes 1048576 | tf_op jit(solution)/shard_map/all_to_all | solution.py:32
  137.3 5.6 %collective-permute-start.6 = (bf16[512,512]{1,0:T(8,128)(2,1)S(1)}, bf16[512,512]{1,0:T(8,128)(2,1)S(1)}, u32[]{:S(2)}, u32[]{:S(2)}) collective-permute-start(bf16[512,512]{1,0:T(8,128)(2,1)S(1)} %bitcast.41), channel_id=1, source_target_pairs={{0,16},{16,0},{32,48},{48,32},{64,80},{80,64},{96,112},{112,96},{1... | collective-permute-start | bytes 1572872 | tf_op jit(solution)/shard_map/ppermute | solution.py:47
  142.9 1.0 shard_map.131
  143.9 0.5 collective-permute-done.6.keys_ref
  144.4 1.8 %shard_map.132 = bf16[512,512]{1,0:T(8,128)(2,1)S(1)} custom-call(bf16[512,512]{1,0:T(8,128)(2,1)S(1)} %bitcast.40, bf16[512,512]{1,0:T(8,128)(2,1)S(1)} %collective-permute-done.6.keys_ref, f32[128,512]{1,0:T(8,128)S(1)} %get-tuple-element.48.seen_ref, f32[512,128]{1,0:T(8,128)S(1)} %get-tuple-element.50.stats_ref, f32[512,512]{1,0:T(8,128)S(1)} %get-tuple-element.51.mixed_ref), custom_call_target="tpu_custom_call" | custom-call | tf_op jit(solution)/shard_map/pallas_call | solution.py:64
  146.2 1.2 copy.28
  (8 shorter events, 0.1 us)
Async XLA Ops:
  3.0 21.1 %copy-start.11 = (f32[224]{0:T(256)S(1)}, f32[224]{0:T(256)}, u32[]{:S(2)}) copy-start(f32[224]{0:T(256)} %param.14) | copy-start | bytes 2692
  3.0 33.1 %all-to-all-start = ((bf16[32,8,256]{2,1,0:T(8,128)(2,1)}), bf16[32,8,256]{2,1,0:T(8,128)(2,1)S(1)}, u32[]{:S(2)}, u32[]{:S(2)}) async-start(bf16[32,8,256]{2,1,0:T(8,128)(2,1)} %bitcast.63), calls=%async_computation | async-start | bytes 262144 | tf_op jit(solution)/shard_map/all_to_all | solution.py:40
  19.8 16.7 %collective-permute-start.1 = (bf16[224,2048]{1,0:T(8,128)(2,1)}, bf16[224,2048]{1,0:T(8,128)(2,1)S(1)}, u32[]{:S(2)}, u32[]{:S(2)}) collective-permute-start(bf16[224,2048]{1,0:T(8,128)(2,1)} %bitcast.50), channel_id=1, source_target_pairs={{0,16},{16,0},{32,48},{48,32},{64,80},{80,64},{96,112},{112,96},{1... | collective-permute-start | bytes 2752520 | tf_op jit(solution)/shard_map/ppermute | solution.py:47
  22.0 14.5 %collective-permute-start.2 = (bf16[224,2048]{1,0:T(8,128)(2,1)}, bf16[224,2048]{1,0:T(8,128)(2,1)S(1)}, u32[]{:S(2)}, u32[]{:S(2)}) collective-permute-start(bf16[224,2048]{1,0:T(8,128)(2,1)} %bitcast.52), channel_id=1, source_target_pairs={{0,16},{16,0},{32,48},{48,32},{64,80},{80,64},{96,112},{112,96},{1... | collective-permute-start | bytes 2752520 | tf_op jit(solution)/shard_map/ppermute | solution.py:47
  24.2 3.1 %collective-permute-start = (f32[8,224]{1,0:T(8,128)S(1)}, f32[8,224]{1,0:T(8,128)S(1)}, u32[]{:S(2)}, u32[]{:S(2)}) collective-permute-start(f32[8,224]{1,0:T(8,128)S(1)} %broadcast_in_dim.13.refs_2_), channel_id=1, source_target_pairs={{0,16},{16,0},{32,48},{48,32},{64,80},{80,64},{96,112},{112,96},{1... | collective-permute-start | bytes 21512 | tf_op jit(solution)/shard_map/ppermute | solution.py:47
  36.2 1.2 copy-start.1
  36.2 1.5 copy-start.2
  39.3 6.9 %copy-start.7 = (bf16[1,2048,224]{1,2,0:T(8,128)(2,1)S(1)}, bf16[1,2048,224]{1,2,0:T(8,128)(2,1)}, u32[]{:S(2)}) copy-start(bf16[1,2048,224]{1,2,0:T(8,128)(2,1)} %param.17) | copy-start | bytes 2752516
  39.3 21.1 %all-to-all-start.1 = ((bf16[16,208,128]{2,1,0:T(8,128)(2,1)}), bf16[16,208,128]{2,1,0:T(8,128)(2,1)S(1)}, u32[]{:S(2)}, u32[]{:S(2)}) async-start(bf16[16,208,128]{2,1,0:T(8,128)(2,1)} %shard_map.124), calls=%async_computation.1 | async-start | bytes 1703936 | tf_op jit(solution)/shard_map/all_to_all | solution.py:32
  46.2 27.3 %collective-permute-start.3 = (bf16[224,2048]{1,0:T(8,128)(2,1)S(1)}, bf16[224,2048]{1,0:T(8,128)(2,1)S(1)}, u32[]{:S(2)}, u32[]{:S(2)}) collective-permute-start(bf16[224,2048]{1,0:T(8,128)(2,1)S(1)} %bitcast.58), channel_id=1, source_target_pairs={{0,16},{16,0},{32,48},{48,32},{64,80},{80,64},{96,112},{112,96},{1... | collective-permute-start | bytes 2752520 | tf_op jit(solution)/shard_map/ppermute | solution.py:47
  74.0 8.5 %copy-start.9 = (s32[8,32,8]{1,2,0:T(8,128)S(1)}, s32[8,32,8]{1,2,0:T(8,128)}, u32[]{:S(2)}) copy-start(s32[8,32,8]{1,2,0:T(8,128)} %param.12) | copy-start | bytes 24580
  74.0 8.5 %copy-start.10 = (f32[8,32,8]{1,2,0:T(8,128)S(1)}, f32[8,32,8]{1,2,0:T(8,128)}, u32[]{:S(2)}) copy-start(f32[8,32,8]{1,2,0:T(8,128)} %param.13) | copy-start | bytes 24580
  74.1 4.4 %copy-start.4 = (bf16[224,512]{1,0:T(8,128)(2,1)S(1)}, bf16[224,512]{1,0:T(8,128)(2,1)}, u32[]{:S(2)}) copy-start(bf16[224,512]{1,0:T(8,128)(2,1)} %own_ref.1) | copy-start | bytes 688132
  74.8 15.6 %copy-start = (bf16[8,32,224]{2,1,0:T(8,128)(2,1)S(1)}, bf16[8,32,224]{2,1,0:T(8,128)(2,1)}, u32[]{:S(2)}) copy-start(bf16[8,32,224]{2,1,0:T(8,128)(2,1)} %param.11) | copy-start | bytes 344068
  74.8 15.6 %copy-start.3 = (f32[256,128]{1,0:T(8,128)S(1)}, f32[256,128]{1,0:T(8,128)}, u32[]{:S(2)}) copy-start(f32[256,128]{1,0:T(8,128)} %get-tuple-element.36.table_ref) | copy-start | bytes 393220
  74.8 15.6 %all-to-all-start.3 = ((bf16[16,8,512]{2,1,0:T(8,128)(2,1)}), bf16[16,8,512]{2,1,0:T(8,128)(2,1)S(1)}, u32[]{:S(2)}, u32[]{:S(2)}) async-start(bf16[16,8,512]{2,1,0:T(8,128)(2,1)} %pad.13), calls=%async_computation.3 | async-start | bytes 262144 | tf_op jit(solution)/shard_map/all_to_all | solution.py:26
  78.4 6.2 %collective-permute-start.4 = (bf16[224,512]{1,0:T(8,128)(2,1)S(1)}, bf16[224,512]{1,0:T(8,128)(2,1)S(1)}, u32[]{:S(2)}, u32[]{:S(2)}) collective-permute-start(bf16[224,512]{1,0:T(8,128)(2,1)S(1)} %copy-done.4), channel_id=1, source_target_pairs={{0,16},{16,0},{32,48},{48,32},{64,80},{80,64},{96,112},{112,96},{1... | collective-permute-start | bytes 688136 | tf_op jit(solution)/shard_map/ppermute | solution.py:47
  82.5 0.7 copy-start.5
  82.5 0.7 copy-start.6
  91.7 16.6 %all-to-all-start.4 = ((bf16[32,8,512]{2,1,0:T(8,128)(2,1)}), bf16[32,8,512]{2,1,0:T(8,128)(2,1)S(1)}, u32[]{:S(2)}, u32[]{:S(2)}) async-start(bf16[32,8,512]{2,1,0:T(8,128)(2,1)} %bitcast.14), calls=%async_computation.4 | async-start | bytes 524288 | tf_op jit(solution)/shard_map/all_to_all | solution.py:26
  99.2 13.3 %copy-start.8 = (bf16[128,4,512]{2,1,0:T(4,128)(2,1)S(1)}, bf16[128,4,512]{2,1,0:T(4,128)(2,1)}, u32[]{:S(2)}) copy-start(bf16[128,4,512]{2,1,0:T(4,128)(2,1)} %param.20) | copy-start | bytes 1572868
  99.3 9.8 %collective-permute-start.5 = (bf16[128,256]{1,0:T(8,128)(2,1)S(1)}, bf16[128,256]{1,0:T(8,128)(2,1)S(1)}, u32[]{:S(2)}, u32[]{:S(2)}) collective-permute-start(bf16[128,256]{1,0:T(8,128)(2,1)S(1)} %slice.4), channel_id=1, source_target_pairs={{0,16},{16,0},{32,48},{48,32},{64,80},{80,64},{96,112},{112,96},{1... | collective-permute-start | bytes 196616 | tf_op jit(solution)/shard_map/ppermute | solution.py:47
  109.0 15.8 %all-to-all-start.5 = ((bf16[16,8,512]{2,1,0:T(8,128)(2,1)}), bf16[16,8,512]{2,1,0:T(8,128)(2,1)S(1)}, u32[]{:S(2)}, u32[]{:S(2)}) async-start(bf16[16,8,512]{2,1,0:T(8,128)(2,1)} %shard_map.128), calls=%async_computation.5 | async-start | bytes 262144 | tf_op jit(solution)/shard_map/all_to_all | solution.py:26
  137.3 7.1 %collective-permute-start.6 = (bf16[512,512]{1,0:T(8,128)(2,1)S(1)}, bf16[512,512]{1,0:T(8,128)(2,1)S(1)}, u32[]{:S(2)}, u32[]{:S(2)}) collective-permute-start(bf16[512,512]{1,0:T(8,128)(2,1)S(1)} %bitcast.41), channel_id=1, source_target_pairs={{0,16},{16,0},{32,48},{48,32},{64,80},{80,64},{96,112},{112,96},{1... | collective-permute-start | bytes 1572872 | tf_op jit(solution)/shard_map/ppermute | solution.py:47

commit v7 on v6

--- a/solution.py
+++ b/solution.py
@@ -13,6 +13,7 @@
 WIDE = 256
 GROUPS = 8
 BLOCK = 4
+ORDER = [0, 4, 8, 12, 1, 5, 9, 13, 2, 6, 10, 14, 3, 7, 11, 15]
 COST = 5_000_000_000
 
 
@@ -26,9 +27,10 @@
     return lax.all_to_all(chunks, axis, split_axis=0, concat_axis=0, tiled=True)
 
 
-def exchange_chips(chunks):
+def exchange_chips(chunks, order=None):
     count = lax.axis_size("ctx")
-    groups = [list(range(core, count, 2)) for core in range(2)]
+    order = order or range(count // 2)
+    groups = [[2 * chip + core for chip in order] for core in range(2)]
     return lax.all_to_all(
         chunks, "ctx", split_axis=0, concat_axis=0, tiled=True, axis_index_groups=groups
     )
@@ -338,11 +340,11 @@
     partial = local_kernel(
         gate_up_kernel, shape((chips, 2 * half + 16, lanes), bf16), *packed, gate_own, gate_pair, up_own, up_pair
     )
-    partial = exchange_chips(partial)
+    partial = exchange_chips(partial, ORDER)
     units = local_kernel(
         lambda *refs: hidden_unit_kernel(half, *refs), shape((chips, half, lanes), bf16), partial
     )
-    spread = exchange_chips(units).transpose(1, 0, 2).reshape(half, hidden_width)
+    spread = exchange_chips(units, ORDER).transpose(1, 0, 2).reshape(half, hidden_width)
 
     fill = ((0, 0), (0, WIDE - width))
     expert_out = jnp.concatenate(

time: 148 us -> 148 us (level)
  starting transfers between devices: 59.3 us -> 61.4 us
  waiting for transfers between devices: 45.5 us -> 43.6 us
where the time goes in v7:
time: 148 us; the launch traced here: 147 us
  starting transfers between devices  61.4 us (41%)
  waiting for transfers between devices  43.6 us (29%)
  blocking collectives  24.3 us (16%)
  Pallas kernels  11.9 us (8%)
  local copies, waits for them, and re-layouts  3.9 us (3%)
    all_to_all x2, blocking collectives, exchange_chips(): lax.all_to_all(chunks, 'ctx', split_axis=0, concat_axis=0, tiled=True, ax...  24.3 us
    all_to_all x3, waiting for transfers between devices, exchange(): return lax.all_to_all(chunks, axis, split_axis=0, concat_axis=0, tiled=True)  22.4 us
    ppermute x7, starting transfers between devices, swap(): return lax.ppermute(value, 'ctx', [(i, i ^ 1) for i in range(count)])  22.1 us
    all_to_all x1, starting transfers between devices, exchange_pairs(): lax.all_to_all(chunks, ('ctx', 'exp'), split_axis=0, concat_axis=0, tiled...  16.8 us
    all_to_all x3, starting transfers between devices, exchange(): return lax.all_to_all(chunks, axis, split_axis=0, concat_axis=0, tiled=True)  15.7 us
    pallas_call x11, Pallas kernels, local_kernel(): pl.pallas_call(kernel, out_shape=out_shape, in_specs=[pl.BlockSpec(memory...  11.9 us
    all_to_all x1, waiting for transfers between devices, exchange_chips(): lax.all_to_all(chunks, 'ctx', split_axis=0, concat_axis=0, tiled=True, ax...  10.8 us
    all_to_all x1, waiting for transfers between devices, exchange_pairs(): lax.all_to_all(chunks, ('ctx', 'exp'), split_axis=0, concat_axis=0, tiled...  8.93 us
  transfers between devices with their start and end apart: 12, of which 7 were waited for; matrix products, arithmetic and copies ran while one was open for 0% of the time, Pallas kernels for 3%

profile of v7, /device:TPU:1, one launch (start us, length us, event | category | flops | bytes accessed | tf_op | source)
XLA Modules:
  0.0 147.1 jit_solution(6010751355606984563)
XLA Ops:
  0.6 2.4 %shard_map.122 = (f32[256,128]{1,0:T(8,128)}, bf16[256,256]{1,0:T(8,128)(2,1)}) custom-call(s32[1]{0:T(128)} %bitcast.refs_0_, s32[8,8,32]{2,1,0:T(8,128)} %bitcast.62, bf16[256,224]{1,0:T(8,128)(2,1)} %bitcast.47), custom_call_target="tpu_custom_call" | custom-call | tf_op jit(solution)/shard_map/pallas_call | solution.py:66
  3.0 0.0 copy-start.11
  3.0 16.8 %all-to-all-start = ((bf16[32,8,256]{2,1,0:T(8,128)(2,1)}), bf16[32,8,256]{2,1,0:T(8,128)(2,1)S(1)}, u32[]{:S(2)}, u32[]{:S(2)}) async-start(bf16[32,8,256]{2,1,0:T(8,128)(2,1)} %bitcast.63), calls=%async_computation | async-start | bytes 262144 | tf_op jit(solution)/shard_map/all_to_all | solution.py:42
  19.8 2.1 %collective-permute-start.1 = (bf16[224,2048]{1,0:T(8,128)(2,1)}, bf16[224,2048]{1,0:T(8,128)(2,1)S(1)}, u32[]{:S(2)}, u32[]{:S(2)}) collective-permute-start(bf16[224,2048]{1,0:T(8,128)(2,1)} %bitcast.50), channel_id=1, source_target_pairs={{0,16},{16,0},{32,48},{48,32},{64,80},{80,64},{96,112},{112,96},{1... | collective-permute-start | bytes 2752520 | tf_op jit(solution)/shard_map/ppermute | solution.py:49
  22.0 2.2 %collective-permute-start.2 = (bf16[224,2048]{1,0:T(8,128)(2,1)}, bf16[224,2048]{1,0:T(8,128)(2,1)S(1)}, u32[]{:S(2)}, u32[]{:S(2)}) collective-permute-start(bf16[224,2048]{1,0:T(8,128)(2,1)} %bitcast.52), channel_id=1, source_target_pairs={{0,16},{16,0},{32,48},{48,32},{64,80},{80,64},{96,112},{112,96},{1... | collective-permute-start | bytes 2752520 | tf_op jit(solution)/shard_map/ppermute | solution.py:49
  24.2 0.0 copy-done.11
  24.2 2.1 %collective-permute-start = (f32[8,224]{1,0:T(8,128)S(1)}, f32[8,224]{1,0:T(8,128)S(1)}, u32[]{:S(2)}, u32[]{:S(2)}) collective-permute-start(f32[8,224]{1,0:T(8,128)S(1)} %broadcast_in_dim.13.refs_2_), channel_id=1, source_target_pairs={{0,16},{16,0},{32,48},{48,32},{64,80},{80,64},{96,112},{112,96},{1... | collective-permute-start | bytes 21512 | tf_op jit(solution)/shard_map/ppermute | solution.py:49
  26.3 0.9 collective-permute-done.refs_3_
  27.2 8.9 %all-to-all-done = bf16[32,8,256]{2,1,0:T(8,128)(2,1)S(1)} async-done(((bf16[32,8,256]{2,1,0:T(8,128)(2,1)}), bf16[32,8,256]{2,1,0:T(8,128)(2,1)S(1)}, u32[]{:S(2)}, u32[]{:S(2)}) %all-to-all-start) | async-done | bytes 131104 | tf_op jit(solution)/shard_map/all_to_all | solution.py:42
  36.2 0.0 copy-start.1
  36.2 0.0 copy-start.2
  36.2 0.3 shard_map.123
  36.5 0.0 collective-permute-done.1.gate_pair
  36.5 0.0 collective-permute-done.2.up_pair
  36.5 0.9 copy-done.1
  37.4 0.3 copy-done.2
  37.6 1.7 %shard_map.124 = bf16[16,208,128]{2,1,0:T(8,128)(2,1)} custom-call(bf16[96,224]{1,0:T(8,128)(2,1)S(1)} %get-tuple-element.30.own_ref, bf16[96,224]{1,0:T(8,128)(2,1)S(1)} %get-tuple-element.31.pair_ref, bf16[16,128]{1,0:T(8,128)(2,1)S(1)} %get-tuple-element.32.square_ref, bf16[224,2048]{1,0:T(8,128)(2,1)S(1)} %bitcast.51, ...), custom_call_target="tpu_custom_call" | custom-call | tf_op jit(solution)/shard_map/pallas_call | solution.py:66
  39.3 0.0 copy-start.7
  39.3 6.9 %all-to-all-start.1 = ((bf16[16,208,128]{2,1,0:T(8,128)(2,1)}), bf16[16,208,128]{2,1,0:T(8,128)(2,1)S(1)}, u32[]{:S(2)}, u32[]{:S(2)}) async-start(bf16[16,208,128]{2,1,0:T(8,128)(2,1)} %shard_map.124), calls=%async_computation.1 | async-start | bytes 1703936 | tf_op jit(solution)/shard_map/all_to_all | solution.py:34
  46.2 0.0 copy-done.7
  46.2 2.6 %collective-permute-start.3 = (bf16[224,2048]{1,0:T(8,128)(2,1)S(1)}, bf16[224,2048]{1,0:T(8,128)(2,1)S(1)}, u32[]{:S(2)}, u32[]{:S(2)}) collective-permute-start(bf16[224,2048]{1,0:T(8,128)(2,1)S(1)} %bitcast.58), channel_id=1, source_target_pairs={{0,16},{16,0},{32,48},{48,32},{64,80},{80,64},{96,112},{112,96},{1... | collective-permute-start | bytes 2752520 | tf_op jit(solution)/shard_map/ppermute | solution.py:49
  48.8 10.8 %all-to-all-done.1.refs_0_ = bf16[16,208,128]{2,1,0:T(8,128)(2,1)S(1)} async-done(((bf16[16,208,128]{2,1,0:T(8,128)(2,1)}), bf16[16,208,128]{2,1,0:T(8,128)(2,1)S(1)}, u32[]{:S(2)}, u32[]{:S(2)}) %all-to-all-start.1) | async-done | bytes 852000 | tf_op jit(solution)/shard_map/all_to_all | solution.py:34
  59.6 0.1 shard_map.125
  59.7 12.1 %all_to_all.35 = bf16[16,96,128]{2,1,0:T(8,128)(2,1)S(1)} all-to-all(bf16[16,96,128]{2,1,0:T(8,128)(2,1)S(1)} %shard_map.125), channel_id=1, replica_groups={{0,128,256,384,32,160,288,416,64,192,320,448,96,224,352,480},{16,144,27..., dimensions={0} | all-to-all | bytes 786432 | tf_op jit(solution)/shard_map/all_to_all | solution.py:34
  71.9 0.4 convolution_convert_fusion.1
  72.3 0.0 collective-permute-done.3
  72.3 0.4 convolution_convert_fusion
  72.8 0.0 copy-start.9
  72.8 0.0 copy-start.10
  72.8 0.0 copy-start.4
  72.8 0.7 pad.13
  73.5 3.6 %all-to-all-start.3 = ((bf16[16,8,512]{2,1,0:T(8,128)(2,1)}), bf16[16,8,512]{2,1,0:T(8,128)(2,1)S(1)}, u32[]{:S(2)}, u32[]{:S(2)}) async-start(bf16[16,8,512]{2,1,0:T(8,128)(2,1)} %pad.13), calls=%async_computation.3 | async-start | bytes 262144 | tf_op jit(solution)/shard_map/all_to_all | solution.py:27
  77.2 0.0 copy-done.4
  77.2 5.0 %collective-permute-start.4 = (bf16[224,512]{1,0:T(8,128)(2,1)S(1)}, bf16[224,512]{1,0:T(8,128)(2,1)S(1)}, u32[]{:S(2)}, u32[]{:S(2)}) collective-permute-start(bf16[224,512]{1,0:T(8,128)(2,1)S(1)} %copy-done.4), channel_id=1, source_target_pairs={{0,16},{16,0},{32,48},{48,32},{64,80},{80,64},{96,112},{112,96},{1... | collective-permute-start | bytes 688136 | tf_op jit(solution)/shard_map/ppermute | solution.py:49
  82.2 0.1 pad_add_fusion.place_ref
  82.3 0.0 copy-done.9
  82.3 0.0 copy-done.10
  82.3 0.0 copy-start.6
  82.4 0.7 copy-done.5
  83.0 0.0 copy-done.6
  83.0 1.4 shard_map.126
  84.4 0.0 collective-permute-done.4.pair_ref
  84.5 4.6 %all-to-all-done.3 = bf16[16,8,512]{2,1,0:T(8,128)(2,1)S(1)} async-done(((bf16[16,8,512]{2,1,0:T(8,128)(2,1)}), bf16[16,8,512]{2,1,0:T(8,128)(2,1)S(1)}, u32[]{:S(2)}, u32[]{:S(2)}) %all-to-all-start.3) | async-done | bytes 131104 | tf_op jit(solution)/shard_map/all_to_all | solution.py:27
  89.1 0.0 copy-done
  89.1 0.0 copy-done.3
  89.1 1.4 shard_map.127
  90.5 8.6 %all-to-all-start.4 = ((bf16[32,8,512]{2,1,0:T(8,128)(2,1)}), bf16[32,8,512]{2,1,0:T(8,128)(2,1)S(1)}, u32[]{:S(2)}, u32[]{:S(2)}) async-start(bf16[32,8,512]{2,1,0:T(8,128)(2,1)} %bitcast.14), calls=%async_computation.4 | async-start | bytes 524288 | tf_op jit(solution)/shard_map/all_to_all | solution.py:27
  99.0 0.0 copy-start.8
  99.1 2.3 %collective-permute-start.5 = (bf16[128,256]{1,0:T(8,128)(2,1)S(1)}, bf16[128,256]{1,0:T(8,128)(2,1)S(1)}, u32[]{:S(2)}, u32[]{:S(2)}) collective-permute-start(bf16[128,256]{1,0:T(8,128)(2,1)S(1)} %slice.4), channel_id=1, source_target_pairs={{0,16},{16,0},{32,48},{48,32},{64,80},{80,64},{96,112},{112,96},{1... | collective-permute-start | bytes 196616 | tf_op jit(solution)/shard_map/ppermute | solution.py:49
  101.3 6.6 %all-to-all-done.4.part_ref = bf16[32,8,512]{2,1,0:T(8,128)(2,1)S(1)} async-done(((bf16[32,8,512]{2,1,0:T(8,128)(2,1)}), bf16[32,8,512]{2,1,0:T(8,128)(2,1)S(1)}, u32[]{:S(2)}, u32[]{:S(2)}) %all-to-all-start.4) | async-done | bytes 262176 | tf_op jit(solution)/shard_map/all_to_all | solution.py:27
  107.9 0.8 shard_map.128
  108.7 0.0 collective-permute-done.5.rest_ref
  108.7 3.5 %all-to-all-start.5 = ((bf16[16,8,512]{2,1,0:T(8,128)(2,1)}), bf16[16,8,512]{2,1,0:T(8,128)(2,1)S(1)}, u32[]{:S(2)}, u32[]{:S(2)}) async-start(bf16[16,8,512]{2,1,0:T(8,128)(2,1)} %shard_map.128), calls=%async_computation.5 | async-start | bytes 262144 | tf_op jit(solution)/shard_map/all_to_all | solution.py:27
  112.3 0.0 copy-done.8
  112.3 0.1 copy.16
  112.4 1.0 shard_map.130
  113.3 11.2 %all-to-all-done.5 = bf16[16,8,512]{2,1,0:T(8,128)(2,1)S(1)} async-done(((bf16[16,8,512]{2,1,0:T(8,128)(2,1)}), bf16[16,8,512]{2,1,0:T(8,128)(2,1)S(1)}, u32[]{:S(2)}, u32[]{:S(2)}) %all-to-all-start.5) | async-done | bytes 131104 | tf_op jit(solution)/shard_map/all_to_all | solution.py:27
  124.5 0.2 shard_map.129
  124.7 12.2 %all_to_all.36 = bf16[16,32,512]{2,1,0:T(8,128)(2,1)S(1)} all-to-all(bf16[16,32,512]{2,1,0:T(8,128)(2,1)S(1)} %shard_map.129), channel_id=1, replica_groups={{0,32,64,96,128,160,192,224,256,288,320,352,384,416,448,480},{16,48,80,..., dimensions={0} | all-to-all | bytes 1048576 | tf_op jit(solution)/shard_map/all_to_all | solution.py:34
  136.9 5.7 %collective-permute-start.6 = (bf16[512,512]{1,0:T(8,128)(2,1)S(1)}, bf16[512,512]{1,0:T(8,128)(2,1)S(1)}, u32[]{:S(2)}, u32[]{:S(2)}) collective-permute-start(bf16[512,512]{1,0:T(8,128)(2,1)S(1)} %bitcast.41), channel_id=1, source_target_pairs={{0,16},{16,0},{32,48},{48,32},{64,80},{80,64},{96,112},{112,96},{1... | collective-permute-start | bytes 1572872 | tf_op jit(solution)/shard_map/ppermute | solution.py:49
  142.6 1.0 shard_map.131
  143.6 0.5 collective-permute-done.6.keys_ref
  144.2 1.8 %shard_map.132 = bf16[512,512]{1,0:T(8,128)(2,1)S(1)} custom-call(bf16[512,512]{1,0:T(8,128)(2,1)S(1)} %bitcast.40, bf16[512,512]{1,0:T(8,128)(2,1)S(1)} %collective-permute-done.6.keys_ref, f32[128,512]{1,0:T(8,128)S(1)} %get-tuple-element.48.seen_ref, f32[512,128]{1,0:T(8,128)S(1)} %get-tuple-element.50.stats_ref, f32[512,512]{1,0:T(8,128)S(1)} %get-tuple-element.51.mixed_ref), custom_call_target="tpu_custom_call" | custom-call | tf_op jit(solution)/shard_map/pallas_call | solution.py:66
  145.9 1.2 copy.28
  (8 shorter events, 0.1 us)
Async XLA Ops:
  3.0 21.1 %copy-start.11 = (f32[224]{0:T(256)S(1)}, f32[224]{0:T(256)}, u32[]{:S(2)}) copy-start(f32[224]{0:T(256)} %param.14) | copy-start | bytes 2692
  3.0 33.1 %all-to-all-start = ((bf16[32,8,256]{2,1,0:T(8,128)(2,1)}), bf16[32,8,256]{2,1,0:T(8,128)(2,1)S(1)}, u32[]{:S(2)}, u32[]{:S(2)}) async-start(bf16[32,8,256]{2,1,0:T(8,128)(2,1)} %bitcast.63), calls=%async_computation | async-start | bytes 262144 | tf_op jit(solution)/shard_map/all_to_all | solution.py:42
  19.8 16.7 %collective-permute-start.1 = (bf16[224,2048]{1,0:T(8,128)(2,1)}, bf16[224,2048]{1,0:T(8,128)(2,1)S(1)}, u32[]{:S(2)}, u32[]{:S(2)}) collective-permute-start(bf16[224,2048]{1,0:T(8,128)(2,1)} %bitcast.50), channel_id=1, source_target_pairs={{0,16},{16,0},{32,48},{48,32},{64,80},{80,64},{96,112},{112,96},{1... | collective-permute-start | bytes 2752520 | tf_op jit(solution)/shard_map/ppermute | solution.py:49
  22.0 14.5 %collective-permute-start.2 = (bf16[224,2048]{1,0:T(8,128)(2,1)}, bf16[224,2048]{1,0:T(8,128)(2,1)S(1)}, u32[]{:S(2)}, u32[]{:S(2)}) collective-permute-start(bf16[224,2048]{1,0:T(8,128)(2,1)} %bitcast.52), channel_id=1, source_target_pairs={{0,16},{16,0},{32,48},{48,32},{64,80},{80,64},{96,112},{112,96},{1... | collective-permute-start | bytes 2752520 | tf_op jit(solution)/shard_map/ppermute | solution.py:49
  24.2 3.1 %collective-permute-start = (f32[8,224]{1,0:T(8,128)S(1)}, f32[8,224]{1,0:T(8,128)S(1)}, u32[]{:S(2)}, u32[]{:S(2)}) collective-permute-start(f32[8,224]{1,0:T(8,128)S(1)} %broadcast_in_dim.13.refs_2_), channel_id=1, source_target_pairs={{0,16},{16,0},{32,48},{48,32},{64,80},{80,64},{96,112},{112,96},{1... | collective-permute-start | bytes 21512 | tf_op jit(solution)/shard_map/ppermute | solution.py:49
  36.2 1.2 copy-start.1
  36.2 1.5 copy-start.2
  39.3 6.9 %copy-start.7 = (bf16[1,2048,224]{1,2,0:T(8,128)(2,1)S(1)}, bf16[1,2048,224]{1,2,0:T(8,128)(2,1)}, u32[]{:S(2)}) copy-start(bf16[1,2048,224]{1,2,0:T(8,128)(2,1)} %param.17) | copy-start | bytes 2752516
  39.3 20.3 %all-to-all-start.1 = ((bf16[16,208,128]{2,1,0:T(8,128)(2,1)}), bf16[16,208,128]{2,1,0:T(8,128)(2,1)S(1)}, u32[]{:S(2)}, u32[]{:S(2)}) async-start(bf16[16,208,128]{2,1,0:T(8,128)(2,1)} %shard_map.124), calls=%async_computation.1 | async-start | bytes 1703936 | tf_op jit(solution)/shard_map/all_to_all | solution.py:34
  46.2 26.1 %collective-permute-start.3 = (bf16[224,2048]{1,0:T(8,128)(2,1)S(1)}, bf16[224,2048]{1,0:T(8,128)(2,1)S(1)}, u32[]{:S(2)}, u32[]{:S(2)}) collective-permute-start(bf16[224,2048]{1,0:T(8,128)(2,1)S(1)} %bitcast.58), channel_id=1, source_target_pairs={{0,16},{16,0},{32,48},{48,32},{64,80},{80,64},{96,112},{112,96},{1... | collective-permute-start | bytes 2752520 | tf_op jit(solution)/shard_map/ppermute | solution.py:49
  72.8 9.6 %copy-start.9 = (s32[8,32,8]{1,2,0:T(8,128)S(1)}, s32[8,32,8]{1,2,0:T(8,128)}, u32[]{:S(2)}) copy-start(s32[8,32,8]{1,2,0:T(8,128)} %param.12) | copy-start | bytes 24580
  72.8 9.5 %copy-start.10 = (f32[8,32,8]{1,2,0:T(8,128)S(1)}, f32[8,32,8]{1,2,0:T(8,128)}, u32[]{:S(2)}) copy-start(f32[8,32,8]{1,2,0:T(8,128)} %param.13) | copy-start | bytes 24580
  72.8 4.4 %copy-start.4 = (bf16[224,512]{1,0:T(8,128)(2,1)S(1)}, bf16[224,512]{1,0:T(8,128)(2,1)}, u32[]{:S(2)}) copy-start(bf16[224,512]{1,0:T(8,128)(2,1)} %own_ref.1) | copy-start | bytes 688132
  73.5 15.6 %copy-start = (bf16[8,32,224]{2,1,0:T(8,128)(2,1)S(1)}, bf16[8,32,224]{2,1,0:T(8,128)(2,1)}, u32[]{:S(2)}) copy-start(bf16[8,32,224]{2,1,0:T(8,128)(2,1)} %param.11) | copy-start | bytes 344068
  73.5 15.6 %copy-start.3 = (f32[256,128]{1,0:T(8,128)S(1)}, f32[256,128]{1,0:T(8,128)}, u32[]{:S(2)}) copy-start(f32[256,128]{1,0:T(8,128)} %get-tuple-element.36.table_ref) | copy-start | bytes 393220
  73.5 15.6 %all-to-all-start.3 = ((bf16[16,8,512]{2,1,0:T(8,128)(2,1)}), bf16[16,8,512]{2,1,0:T(8,128)(2,1)S(1)}, u32[]{:S(2)}, u32[]{:S(2)}) async-start(bf16[16,8,512]{2,1,0:T(8,128)(2,1)} %pad.13), calls=%async_computation.3 | async-start | bytes 262144 | tf_op jit(solution)/shard_map/all_to_all | solution.py:27
  77.2 7.3 %collective-permute-start.4 = (bf16[224,512]{1,0:T(8,128)(2,1)S(1)}, bf16[224,512]{1,0:T(8,128)(2,1)S(1)}, u32[]{:S(2)}, u32[]{:S(2)}) collective-permute-start(bf16[224,512]{1,0:T(8,128)(2,1)S(1)} %copy-done.4), channel_id=1, source_target_pairs={{0,16},{16,0},{32,48},{48,32},{64,80},{80,64},{96,112},{112,96},{1... | collective-permute-start | bytes 688136 | tf_op jit(solution)/shard_map/ppermute | solution.py:49
  82.3 0.7 copy-start.5
  82.3 0.7 copy-start.6
  90.5 17.5 %all-to-all-start.4 = ((bf16[32,8,512]{2,1,0:T(8,128)(2,1)}), bf16[32,8,512]{2,1,0:T(8,128)(2,1)S(1)}, u32[]{:S(2)}, u32[]{:S(2)}) async-start(bf16[32,8,512]{2,1,0:T(8,128)(2,1)} %bitcast.14), calls=%async_computation.4 | async-start | bytes 524288 | tf_op jit(solution)/shard_map/all_to_all | solution.py:27
  99.0 13.2 %copy-start.8 = (bf16[128,4,512]{2,1,0:T(4,128)(2,1)S(1)}, bf16[128,4,512]{2,1,0:T(4,128)(2,1)}, u32[]{:S(2)}) copy-start(bf16[128,4,512]{2,1,0:T(4,128)(2,1)} %param.20) | copy-start | bytes 1572868
  99.1 9.7 %collective-permute-start.5 = (bf16[128,256]{1,0:T(8,128)(2,1)S(1)}, bf16[128,256]{1,0:T(8,128)(2,1)S(1)}, u32[]{:S(2)}, u32[]{:S(2)}) collective-permute-start(bf16[128,256]{1,0:T(8,128)(2,1)S(1)} %slice.4), channel_id=1, source_target_pairs={{0,16},{16,0},{32,48},{48,32},{64,80},{80,64},{96,112},{112,96},{1... | collective-permute-start | bytes 196616 | tf_op jit(solution)/shard_map/ppermute | solution.py:49
  108.7 15.8 %all-to-all-start.5 = ((bf16[16,8,512]{2,1,0:T(8,128)(2,1)}), bf16[16,8,512]{2,1,0:T(8,128)(2,1)S(1)}, u32[]{:S(2)}, u32[]{:S(2)}) async-start(bf16[16,8,512]{2,1,0:T(8,128)(2,1)} %shard_map.128), calls=%async_computation.5 | async-start | bytes 262144 | tf_op jit(solution)/shard_map/all_to_all | solution.py:27
  136.9 7.2 %collective-permute-start.6 = (bf16[512,512]{1,0:T(8,128)(2,1)S(1)}, bf16[512,512]{1,0:T(8,128)(2,1)S(1)}, u32[]{:S(2)}, u32[]{:S(2)}) collective-permute-start(bf16[512,512]{1,0:T(8,128)(2,1)S(1)} %bitcast.41), channel_id=1, source_target_pairs={{0,16},{16,0},{32,48},{48,32},{64,80},{80,64},{96,112},{112,96},{1... | collective-permute-start | bytes 1572872 | tf_op jit(solution)/shard_map/ppermute | solution.py:49
